TPU v7x, 32 devices: a whole 2x2x4 slice. The times are simulated.
32 devices in a mesh: grp: 2 (over x), chan: 4 (over y, core), ctx: 4 (over z).
Axes of the slice: x: 2, y: 2, z: 4, core: 2. Of those that a mesh axis runs over, the one named last changes fastest.
Arguments:
- features: bfloat16 [4096, 4096], P(('grp', 'ctx'), 'chan'), parts along dimension 0, may hold values from -6 to 6
- filter_taps: bfloat16 [2048, 4096], P(None, 'chan'), may hold values from -0.125 to 0.125
- skip_gain: float32 [4096], P('chan'), may hold values from -4 to 4
- in_weight: bfloat16 [4096, 3, 4096], P(None, None, 'chan'), may hold values from -0.09375 to 0.09375
- out_weight: bfloat16 [4096, 4096], P(None, 'chan'), may hold values from -0.125 to 0.125
Outputs:
- layer_out: bfloat16 [4096, 4096], P(('grp', 'ctx'), 'chan'), parts along dimension 0
There are 2 independent parts, one for each index of `grp`. A program takes and returns all parts, laid end to end along the dimension named above; an argument that names none is the same for every part. Nothing has to cross between parts.
All inputs are finite; a program needn't handle non-finite values.
Results may differ from a plain program's by a relative error of at most 0.013.
Values may be sent and summed in bfloat16 or wider, within the bound.
A program may use at most 320 MiB of HBM per device.

v0:
```python
import math

import jax
import jax.numpy as jnp
from jax import lax
from jax.sharding import PartitionSpec as P

P_SIZE = 128


def dft_tables(block_len):
    period = 2 * block_len
    freq_col = jnp.arange(period, dtype=jnp.int32)[:, None]
    place_row = jnp.arange(period, dtype=jnp.int32)[None, :]
    angles = (freq_col * place_row % period).astype(jnp.float32) * (2.0 * math.pi / period)
    forward = jnp.concatenate([jnp.cos(angles), -jnp.sin(angles)], axis=0).astype(jnp.bfloat16)
    out_place = jnp.arange(block_len, dtype=jnp.int32)[:, None] + block_len
    angle_out = (out_place * place_row % period).astype(jnp.float32) * (2.0 * math.pi / period)
    inverse = (jnp.concatenate([jnp.cos(angle_out), -jnp.sin(angle_out)], axis=1) / period).astype(
        jnp.bfloat16
    )
    return (forward, inverse)


def input_spectra(token_rows, forward):
    channels = token_rows.shape[1]
    grouped = token_rows.reshape(token_rows.shape[0] // P_SIZE, P_SIZE, channels)
    spectra = jnp.einsum(
        "fp,bpc->bfc", forward[:, :P_SIZE], grouped, preferred_element_type=jnp.float32
    )
    return spectra.astype(jnp.bfloat16)


def segment_spectra(padded, forward):
    channels = padded.shape[1]
    count = padded.shape[0] // P_SIZE - 1
    tap_blocks = padded.reshape(count + 1, P_SIZE, channels)
    segments = jnp.concatenate([tap_blocks[:-1], tap_blocks[1:]], axis=1)
    spectra = jnp.einsum("fn,knc->kfc", forward, segments, preferred_element_type=jnp.float32)
    return spectra.astype(jnp.bfloat16)


def shards(features, filter_taps, skip_gain, in_weight, out_weight):
    forward, inverse = dft_tables(P_SIZE)
    channels = in_weight.shape[2]
    tok_rows = features.shape[0]
    per_dev = tok_rows // P_SIZE
    period = 2 * P_SIZE
    total_blocks = per_dev * lax.axis_size("ctx")
    first_mine = lax.axis_index("ctx") * per_dev
    last_mine = first_mine + per_dev - 1
    padded_all = jnp.concatenate([jnp.zeros((P_SIZE, channels), jnp.bfloat16), filter_taps], axis=0)
    lag_spectra = segment_spectra(padded_all, forward)
    flipped = jnp.concatenate([lag_spectra[::-1], jnp.zeros_like(lag_spectra)], axis=0)
    flat_in = in_weight.reshape(in_weight.shape[0], 3 * channels)
    weight_slice = flat_in
    projected = jnp.dot(
        lax.all_gather(features, "chan", axis=1, tiled=True),
        weight_slice,
        preferred_element_type=jnp.float32,
    )
    query_rows = projected[:, :channels].astype(jnp.bfloat16)
    mixed_in = (projected[:, channels : 2 * channels] * projected[:, 2 * channels :]).astype(
        jnp.bfloat16
    )

    def add_spectra(running, source):
        source_re = source[:, :period].astype(jnp.float32)
        source_im = source[:, period:].astype(jnp.float32)
        outputs = []
        for out_block in range(per_dev):
            start_lag = total_blocks - 1 - (first_mine + out_block)
            window = lax.dynamic_slice_in_dim(flipped, start_lag, source.shape[0], 0).astype(
                jnp.float32
            )
            lag_re = window[:, :period]
            lag_im = window[:, period:]
            out_re = jnp.sum(lag_re * source_re - lag_im * source_im, axis=0)
            out_im = jnp.sum(lag_re * source_im + lag_im * source_re, axis=0)
            outputs.append(jnp.concatenate([out_re, out_im], axis=0))
        return running + jnp.stack(outputs)

    zero_spectra = jnp.zeros((per_dev, 2 * period, channels), jnp.float32)
    portion = lax.all_gather(mixed_in, "ctx", axis=0, tiled=True)
    first_in = jnp.int32(0) // P_SIZE

    def accumulate(current):
        return add_spectra(current, input_spectra(portion, forward))

    summed = lax.cond(first_in <= last_mine, accumulate, lambda current: current, zero_spectra)
    block_spectra = summed.astype(jnp.bfloat16)
    conv_out = jnp.einsum(
        "tf,bfc->btc", inverse, block_spectra, preferred_element_type=jnp.float32
    ).reshape(tok_rows, channels)
    gated_rows = (
        query_rows.astype(jnp.float32)
        * (conv_out + skip_gain[None, :] * mixed_in.astype(jnp.float32))
    ).astype(jnp.bfloat16)
    weight_slice = out_weight
    layer_out = jnp.dot(
        lax.all_gather(gated_rows, "chan", axis=1, tiled=True),
        weight_slice,
        preferred_element_type=jnp.float32,
    )
    return layer_out.astype(jnp.bfloat16)


def solution(mesh):
    return jax.shard_map(
        shards,
        mesh=mesh,
        in_specs=(
            P(("grp", "ctx"), "chan"),
            P(None, "chan"),
            P("chan"),
            P(None, None, "chan"),
            P(None, "chan"),
        ),
        out_specs=P(("grp", "ctx"), "chan"),
        check_vma=False,
    )
```

profile of v0, /device:TPU:11, one launch (start us, length us, event | category | flops | bytes accessed | tf_op | source)
XLA Modules:
  0.0 332.9 jit_solution(129528146827862470)
XLA Ops:
  6.5 0.0 all-gather.4.cloned.1.call-start
  6.5 0.7 all-gather.4.cloned.1.call-update
  7.3 0.0 all-gather.6.cloned.1.call-start
  7.3 33.6 %copy.13 = bf16[4096,3,1024]{0,2,1:T(8,128)(2,1)} copy(bf16[4096,3,1024]{2,0,1:T(8,128)(2,1)} %param.10) | data formatting | bytes 50331648 | tf_op args[3]
  40.9 4.0 %all-gather.4.cloned.1.call-done = bf16[512,4096]{1,0:T(8,128)(2,1)} async-done(((bf16[512,1024]{1,0:T(8,128)(2,1)}), bf16[512,4096]{1,0:T(8,128)(2,1)}) %all-gather.4.cloned.1.call-update) | async-done | bytes 4194320 | tf_op jit(solution)/shard_map/all_gather | solution.py:58
  45.0 17.9 %fusion.50 = f32[512,3072]{1,0:T(8,128)S(1)} fusion(bf16[512,4096]{1,0:T(8,128)(2,1)} %all-gather.4.cloned.1.call-done, bf16[4096,3072]{0,1:T(8,128)(2,1)} %bitcast.39), kind=kOutput, calls=%fused_computation.93 | convolution fusion | flops 12884901888 | bytes 35651584 | tf_op jit(solution)/shard_map/dot_general | solution.py:57
  62.9 0.0 copy-start
  62.9 2.6 copy-done
  65.4 1.3 fusion.25
  66.7 0.0 all-gather.6.cloned.1.call-update
  66.8 0.0 all-gather.8.cloned.1.call-start
  66.8 4.5 %pad_slice_fusion = bf16[2048,1024]{1,0:T(8,128)(2,1)} fusion(bf16[2048,1024]{1,0:T(8,128)(2,1)} %param.8), kind=kLoop, calls=%fused_computation.52 | loop fusion | bytes 8388608 | tf_op jit(solution)/shard_map/slice | solution.py:38
  71.3 6.5 %copy.14 = bf16[16,128,1024]{1,2,0:T(8,128)(2,1)} copy(bf16[16,128,1024]{2,1,0:T(8,128)(2,1)} %bitcast.41) | data formatting | bytes 8388608 | tf_op jit(solution)/shard_map/slice | solution.py:38
  77.8 6.4 %copy.15 = bf16[16,128,1024]{1,2,0:T(8,128)(2,1)} copy(bf16[16,128,1024]{2,1,0:T(8,128)(2,1)} %bitcast.40) | data formatting | bytes 8388608 | tf_op jit(solution)/shard_map/slice | solution.py:38
  84.2 1.1 negate_convert_fusion
  85.3 10.4 %convert_bitcast_fusion.1 = bf16[16,512,1024]{1,2,0:T(8,128)(2,1)} fusion(bf16[16,128,1024]{1,2,0:T(8,128)(2,1)} %copy.15, bf16[16,128,1024]{1,2,0:T(8,128)(2,1)} %copy.14, bf16[256,256]{1,0:T(8,128)(2,1)S(1)} %get-tuple-element.49, bf16[256,256]{1,0:T(8,128)(2,1)S(1)} %get-tuple-element.50), kind=kOutput, calls=%fused_computation.48 | convolution fusion | flops 4320657408 | bytes 25427968 | tf_op jit(solution)/shard_map/fn,knc->kfc/dot_general | solution.py:39
  95.7 13.8 %rev.3 = bf16[16,512,1024]{1,2,0:T(8,128)(2,1)} reverse(bf16[16,512,1024]{1,2,0:T(8,128)(2,1)} %convert_bitcast_fusion.1), dimensions={0} | reverse | bytes 33554432 | tf_op jit(solution)/shard_map/rev | solution.py:54
  109.5 1.2 fusion.46
  110.7 34.1 %all-gather.6.cloned.1.call-done = bf16[2048,1024]{1,0:T(8,128)(2,1)} async-done(((bf16[512,1024]{1,0:T(8,128)(2,1)}), bf16[2048,1024]{1,0:T(8,128)(2,1)}) %all-gather.6.cloned.1.call-update) | async-done | bytes 4194320 | tf_op jit(solution)/shard_map/all_gather | solution.py:84
  144.8 114.8 %conditional.1 = (bf16[4,512,1024]{1,2,0:T(8,128)(2,1)}) conditional(s32[]{:T(128)} %convert_element_type.68, () %tuple.13, (bf16[16,512,1024]{1,2,0:T(8,128)(2,1)}, s32[]{:T(128)}, bf16[2048,1024]{1,0:T(8,128)(2,1)}, bf16[512,256]{1,0:T(8,128)(2,1)S(1)}) %tuple.14), branch_computations={%region_0.1_spmd, %region_1.10_spmd} | conditional | flops 2344615936 | bytes 344064256 | solution.py:90
  144.8 50.4 %fusion.18 = (f32[16,512,1024]{1,2,0:T(8,128)}, f32[16,512,1024]{1,2,0:T(8,128)}, f32[16,512,1024]{1,2,0:T(8,128)}, f32[16,512,1024]{1,2,0:T(8,128)}) fusion(s32[]{:T(128)S(6)} %select_n.25, bf16[16,512,1024]{1,2,0:T(8,128)(2,1)} %get-tuple-element.19, s32[]{:T(128)S(6)} %select_n.24, s32[]{:T(128)S(6)} %select_n.26, s32[]{:T(128)S(6)} %select_n.23), kind=kLoop, calls=%fused_computation.38 | loop fusion | flops 33554432 | bytes 150994960 | tf_op jit(solution)/shard_map/cond/branch_1_fun/convert_element_type | solution.py:73
  195.2 10.4 %convert_bitcast_fusion = bf16[16,512,1024]{1,2,0:T(8,128)(2,1)} fusion(bf16[16,128,1024]{2,1,0:T(8,128)(2,1)} %bitcast.42, bf16[512,256]{1,0:T(8,128)(2,1)S(1)} %get-tuple-element.22), kind=kOutput, calls=%fused_computation.40 | convolution fusion | flops 2155872256 | bytes 21102592 | tf_op jit(solution)/shard_map/cond/branch_1_fun/fp,bpc->bfc/dot_general | solution.py:28
  205.7 49.9 %fusion.5 = (bf16[256,1024]{0,1:T(8,128)(2,1)S(1)}, bf16[256,1024]{0,1:T(8,128)(2,1)S(1)}, bf16[256,1024]{0,1:T(8,128)(2,1)S(1)}, bf16[256,1024]{0,1:T(8,128)(2,...) fusion(f32[16,512,1024]{1,2,0:T(8,128)} %get-tuple-element.40, ...), kind=kLoop, calls=%fused_computation.25 | loop fusion | flops 140509184 | bytes 155189248 | tf_op jit(solution)/shard_map/cond/branch_1_fun/reduce_sum | solution.py:78
  255.6 1.4 maximum_bitcast_fusion
  257.0 0.2 maximum_bitcast_fusion.2
  257.1 2.5 pad_maximum_fusion
  259.6 0.0 copy-start.1
  259.6 3.7 %fusion.40 = f32[4,1024,128]{1,2,0:T(8,128)S(1)} fusion(bf16[4,512,1024]{1,2,0:T(8,128)(2,1)} %get-tuple-element.51, f32[128,256]{1,0:T(8,128)} %get-tuple-element.48, f32[128,256]{1,0:T(8,128)S(1)} %get-tuple-element.47), kind=kOutput, calls=%fused_computation.82 | convolution fusion | flops 537067520 | bytes 6553600 | tf_op jit(solution)/shard_map/tf,bfc->btc/dot_general | solution.py:92
  263.3 0.0 copy-done.1
  263.3 4.7 %fusion.27 = bf16[512,1024]{1,0:T(8,128)(2,1)} fusion(f32[4,1024,128]{1,2,0:T(8,128)S(1)} %fusion.40, f32[512,3072]{1,0:T(8,128)} %copy-done, f32[1024]{0:T(1024)S(1)} %copy-done.1), kind=kLoop, calls=%fused_computation.58 | loop fusion | flops 4194304 | bytes 8392704 | tf_op jit(solution)/shard_map/convert_element_type | solution.py:98
  268.0 0.0 all-gather.8.cloned.1.call-update
  268.0 48.2 %all-gather.8.cloned.1.call-done = bf16[512,4096]{1,0:T(8,128)(2,1)} async-done(((bf16[512,1024]{1,0:T(8,128)(2,1)}), bf16[512,4096]{1,0:T(8,128)(2,1)}) %all-gather.8.cloned.1.call-update) | async-done | bytes 4194320 | tf_op jit(solution)/shard_map/all_gather | solution.py:101
  316.2 10.1 %convolution_convert_fusion = bf16[512,1024]{1,0:T(8,128)(2,1)} fusion(bf16[512,4096]{1,0:T(8,128)(2,1)} %all-gather.8.cloned.1.call-done, bf16[4096,1024]{1,0:T(8,128)(2,1)} %param.11), kind=kOutput, calls=%fused_computation.59 | convolution fusion | flops 4295491584 | bytes 13631488 | tf_op jit(solution)/shard_map/dot_general | solution.py:100
  (2 shorter events, 0.0 us)
Async XLA Ops:
  6.5 38.5 %all-gather.4.cloned.1.call-start = ((), (), s32[]{:S(2)}) async-start(), calls=%async_computation | async-start | bytes 5242880 | tf_op jit(solution)/shard_map/all_gather | solution.py:58
  7.3 137.6 %all-gather.6.cloned.1.call-start = ((), (), s32[]{:S(2)}) async-start(), calls=%async_computation.1 | async-start | bytes 5242880 | tf_op jit(solution)/shard_map/all_gather | solution.py:84
  62.9 2.6 copy-start
  66.8 249.5 %all-gather.8.cloned.1.call-start = ((), (), s32[]{:S(2)}) async-start(), calls=%async_computation.2 | async-start | bytes 5242880 | tf_op jit(solution)/shard_map/all_gather | solution.py:101
  259.6 3.7 %copy-start.1 = (f32[1024]{0:T(1024)S(1)}, f32[1024]{0:T(1024)}, u32[]{:S(2)}) copy-start(f32[1024]{0:T(1024)} %param.9) | copy-start | bytes 12292
Sparse Core Ops, SparseCore 0:
  8.9 36.0 all-gather.3
  66.9 77.9 all-gather.5
  268.1 48.0 all-gather.7
where the time goes:
time: 335 us; the launch traced here: 333 us
  other arithmetic  113 us (34%)
  waiting for transfers between devices  87.1 us (26%)
  local copies, waits for them, and re-layouts  67.3 us (20%)
  matrix products  52.5 us (16%)
  between operations  13.2 us (4%)
    convert_element_type x1, other arithmetic, add_spectra(): lax.dynamic_slice_in_dim(flipped, start_lag, source.shape[0], 0)  50.4 us
    reduce_sum x1, other arithmetic, add_spectra(): out_re = jnp.sum(lag_re * source_re - lag_im * source_im, axis=0)  49.9 us
    all_gather x1, waiting for transfers between devices, shards(): lax.all_gather(gated_rows, 'chan', axis=1, tiled=True)  48.2 us
    unnamed x5, local copies, waits for them, and re-layouts  36.2 us
    all_gather x1, waiting for transfers between devices, shards(): portion = lax.all_gather(mixed_in, 'ctx', axis=0, tiled=True)  34.1 us
    dot_general x1, matrix products, shards(): jnp.dot(lax.all_gather(features, 'chan', axis=1, tiled=True), weight_slic...  17.9 us
    slice x3, local copies, waits for them, and re-layouts, segment_spectra(): segments = jnp.concatenate([tap_blocks[:-1], tap_blocks[1:]], axis=1)  17.3 us
    rev x1, local copies, waits for them, and re-layouts, shards(): lag_spectra[::-1]  13.8 us
  transfers between devices with their start and end apart: 3, of which 3 were waited for; matrix products, arithmetic and copies ran while one was open for 23% of the time, Pallas kernels for 0%

commit v1 on v0

v1 whole, which is shorter than its diff:
```python
import functools
import math

import jax
import jax.numpy as jnp
import numpy as np
from jax import lax
from jax.experimental import pallas as pl
from jax.experimental.pallas import tpu as pltpu
from jax.sharding import PartitionSpec as P

BLOCK = 256


def tables(block):
    period = 2 * block
    freq = 2 * np.arange(block, dtype=np.int64)[:, None] + 1
    place = np.arange(period, dtype=np.int64)[None, :]
    angle = (freq * place % (2 * period)) * (math.pi / period)
    forward = np.concatenate([np.cos(angle), -np.sin(angle)], axis=0)
    kept = angle[:, block:].T
    inverse = np.concatenate([np.cos(kept), -np.sin(kept)], axis=1) / block
    return jnp.asarray(forward, jnp.bfloat16), jnp.asarray(inverse, jnp.bfloat16)


def conv_kernel(n, x_ref, taps_ref, skip_ref, fwd_ref, inv_ref, out_ref, xs, gs, ys):
    me = lax.axis_index("ctx")
    rows, cc = x_ref.shape[1], x_ref.shape[2]
    per = rows // BLOCK
    blocks = n * per
    for k in range(blocks):
        if k == 0:
            gs[k] = jnp.dot(fwd_ref[:, BLOCK:], taps_ref[:BLOCK], preferred_element_type=jnp.float32)
        else:
            gs[k] = jnp.dot(
                fwd_ref[...], taps_ref[(k - 1) * BLOCK : (k + 1) * BLOCK], preferred_element_type=jnp.float32
            )
    for a in range(blocks):
        slot = lax.rem(me - a // per + n, n)
        part = slice((a % per) * BLOCK, (a % per + 1) * BLOCK)
        xs[a] = jnp.dot(fwd_ref[:, :BLOCK], x_ref[slot, part, :], preferred_element_type=jnp.float32)

    lane = min(cc, 128)

    def mix(i, carry):
        re = pl.ds(pl.multiple_of(i * 8, 8), 8)
        im = pl.ds(pl.multiple_of(i * 8 + BLOCK, 8), 8)
        for l in range(0, cc, lane):
            ls = slice(l, l + lane)
            xr = [xs[a, re, ls] for a in range(blocks)]
            xi = [xs[a, im, ls] for a in range(blocks)]
            gr = [gs[a, re, ls] for a in range(blocks)]
            gi = [gs[a, im, ls] for a in range(blocks)]
            for b in range(blocks):
                yr = xr[0] * gr[b] - xi[0] * gi[b]
                yi = xi[0] * gr[b] + xr[0] * gi[b]
                for a in range(1, b + 1):
                    yr = yr + xr[a] * gr[b - a] - xi[a] * gi[b - a]
                    yi = yi + xi[a] * gr[b - a] + xr[a] * gi[b - a]
                ys[b, re, ls] = yr
                ys[b, im, ls] = yi
        return carry

    lax.fori_loop(0, BLOCK // 8, mix, 0)
    for b in range(blocks):
        owner = b // per
        part = slice((b % per) * BLOCK, (b % per + 1) * BLOCK)
        conv = jnp.dot(inv_ref[...], ys[b].astype(jnp.bfloat16), preferred_element_type=jnp.float32)
        held = x_ref[lax.rem(me - owner + n, n), part, :].astype(jnp.float32)
        out_ref[lax.rem(owner - me + n, n), part, :] = (conv + skip_ref[...] * held).astype(jnp.bfloat16)


def convolve(n, x, taps, skip):
    rows, cc = x.shape[1:]
    forward, inverse = tables(BLOCK)
    blocks = n * rows // BLOCK
    spectra = pltpu.VMEM((blocks, 2 * BLOCK, cc), jnp.float32)
    return pl.pallas_call(
        functools.partial(conv_kernel, n),
        out_shape=jax.ShapeDtypeStruct(x.shape, jnp.bfloat16),
        in_specs=[pl.BlockSpec(memory_space=pltpu.VMEM)] * 5,
        out_specs=pl.BlockSpec(memory_space=pltpu.VMEM),
        scratch_shapes=[spectra, spectra, spectra],
        compiler_params=pltpu.CompilerParams(vmem_limit_bytes=40 * 1024 * 1024),
        cost_estimate=pl.CostEstimate(flops=8_000_000_000, bytes_accessed=4_000_000, transcendentals=0),
    )(x, taps, skip, forward, inverse)


def shift(x, axis, n, by):
    return lax.ppermute(x, axis, [(i, (i + by) % n) for i in range(n)])


def flip(x, n, bit):
    return lax.ppermute(x, "chan", [(i, i ^ bit) for i in range(n)])


def gather_pieces(x, n):
    across = flip(x, n, 2)
    beside = flip(x, n, 1)
    return [(0, x), (1, beside), (2, across), (3, flip(across, n, 1))]


def gather(x, n):
    if n != 4:
        return lax.all_gather(x, "chan", axis=1, tiled=True)
    me = lax.axis_index("chan")
    width = x.shape[1]
    whole = jnp.zeros((x.shape[0], n * width), x.dtype)
    for far, piece in gather_pieces(x, n):
        whole = lax.dynamic_update_slice(whole, piece, (0, (me ^ far) * width))
    return whole


def exchange(parts, n):
    return [parts[0]] + [shift(parts[s], "ctx", n, s) for s in range(1, n)]


def shards(features, filter_taps, skip_gain, in_weight, out_weight):
    f32 = jnp.float32
    n_ctx, n_chan = lax.axis_size("ctx"), lax.axis_size("chan")
    ctx, chan = lax.axis_index("ctx"), lax.axis_index("chan")
    rows, channels = features.shape[0], in_weight.shape[2]
    cc = channels // n_ctx
    taps = lax.dynamic_slice_in_dim(filter_taps, ctx * cc, cc, 1)
    skip = lax.dynamic_slice_in_dim(skip_gain, ctx * cc, cc, 0)[None, :]

    whole = gather(features, n_chan)
    key = jnp.dot(whole, in_weight[:, 1], preferred_element_type=f32)
    value = jnp.dot(whole, in_weight[:, 2], preferred_element_type=f32)
    mixed = (key * value).astype(jnp.bfloat16)
    sends = [
        lax.dynamic_slice_in_dim(mixed, ((ctx + s) % n_ctx) * cc, cc, 1) for s in range(n_ctx)
    ]
    x = jnp.stack(exchange(sends, n_ctx))
    query = jnp.dot(whole, in_weight[:, 0], preferred_element_type=f32).astype(jnp.bfloat16)
    y = convolve(n_ctx, x, taps, skip)
    back = exchange([y[s] for s in range(n_ctx)], n_ctx)
    summed = jnp.zeros((rows, channels), jnp.bfloat16)
    for s in range(n_ctx):
        summed = lax.dynamic_update_slice(summed, back[s], (0, ((ctx - s + n_ctx) % n_ctx) * cc))
    gated = (query.astype(f32) * summed.astype(f32)).astype(jnp.bfloat16)
    if n_chan != 4:
        return jnp.dot(gather(gated, n_chan), out_weight, preferred_element_type=f32).astype(jnp.bfloat16)
    total = None
    for far, piece in gather_pieces(gated, n_chan):
        weight = lax.dynamic_slice_in_dim(out_weight, (chan ^ far) * channels, channels, 0)
        term = jnp.dot(piece, weight, preferred_element_type=f32)
        total = term if total is None else total + term
    return total.astype(jnp.bfloat16)


def solution(mesh):
    return jax.shard_map(
        shards,
        mesh=mesh,
        in_specs=(
            P(("grp", "ctx"), "chan"),
            P(None, "chan"),
            P("chan"),
            P(None, None, "chan"),
            P(None, "chan"),
        ),
        out_specs=P(("grp", "ctx"), "chan"),
        check_vma=False,
    )
```

time: 335 us -> 143 us (0.43)
  other arithmetic: 113 us -> 1.16 us
  local copies, waits for them, and re-layouts: 67.3 us -> 5.4 us
  matrix products: 52.5 us -> 31.1 us
  between operations: 13.2 us -> 0.24 us
  starting transfers between devices: 0.08 us -> 13 us
  Pallas kernels: 0 us -> 5.24 us
    ppermute x0 -> x12, waiting for transfers between devices: none -> 86.9 us  [the longest x6 44.4 us: flip(): return lax.ppermute(x, 'chan', [(i, i ^ bit) for i in range(n)])]
    all_gather x3 -> x0, waiting for transfers between devices: 86.4 us -> none  [the longest x1 48.2 us: shards(): lax.all_gather(gated_rows, 'chan', axis=1, tiled=True)]
    convert_element_type x3 -> x0, other arithmetic: 56.3 us -> none  [the longest x1 50.4 us: add_spectra(): lax.dynamic_slice_in_dim(flipped, start_lag, source.shape[0], 0)]
    reduce_sum x1 -> x0, other arithmetic: 49.9 us -> none  [add_spectra(): out_re = jnp.sum(lag_re * source_re - lag_im * source_im, axis=0)]
    unnamed x5 -> x12, local copies, waits for them, and re-layouts: 36.2 us -> 0.03 us
    dot_general x5 -> x7, matrix products: 52.5 us -> 31.1 us  [the longest x1 9.28 us: shards(): jnp.dot(whole, in_weight[:, 0], preferred_element_type=f32)]
    slice x3 -> x0, local copies, waits for them, and re-layouts: 17.3 us -> none  [segment_spectra(): segments = jnp.concatenate([tap_blocks[:-1], tap_blocks[1:]], axis=1)]
    rev x1 -> x0, local copies, waits for them, and re-layouts: 13.8 us -> none  [shards(): lag_spectra[::-1]]
  transfers between devices with their start and end apart: 3 -> 12, of which waited for: 3 -> 9; matrix products, arithmetic and copies ran while one was open for 23% -> 6% of each run, Pallas kernels for 0% -> 0%
where the time goes in v1:
time: 143 us
  waiting for transfers between devices  86.9 us (61%)
  matrix products  31.1 us (22%)
  starting transfers between devices  13 us (9%)
  local copies, waits for them, and re-layouts  5.4 us (4%)
  Pallas kernels  5.24 us (4%)
    ppermute x6, waiting for transfers between devices, flip(): return lax.ppermute(x, 'chan', [(i, i ^ bit) for i in range(n)])  44.4 us
    ppermute x6, waiting for transfers between devices, shift(): return lax.ppermute(x, axis, [(i, (i + by) % n) for i in range(n)])  42.4 us
    dot_general x1, matrix products, shards(): jnp.dot(whole, in_weight[:, 0], preferred_element_type=f32)  9.28 us
    dot_general x1, matrix products, shards(): value = jnp.dot(whole, in_weight[:, 2], preferred_element_type=f32)  8.45 us
    dot_general x1, matrix products, shards(): key = jnp.dot(whole, in_weight[:, 1], preferred_element_type=f32)  7.23 us
    ppermute x6, starting transfers between devices, flip(): return lax.ppermute(x, 'chan', [(i, i ^ bit) for i in range(n)])  7.15 us
    dot_general x4, matrix products, shards(): term = jnp.dot(piece, weight, preferred_element_type=f32)  6.17 us
    ppermute x6, starting transfers between devices, shift(): return lax.ppermute(x, axis, [(i, (i + by) % n) for i in range(n)])  5.9 us
  transfers between devices with their start and end apart: 12, of which 9 were waited for; matrix products, arithmetic and copies ran while one was open for 6% of the time, Pallas kernels for 0%

profile of v1, /device:TPU:11, one launch (start us, length us, event | category | flops | bytes accessed | tf_op | source)
XLA Modules:
  0.0 143.1 jit_solution(393325531601114098)
XLA Ops:
  0.0 1.2 collective-permute-start.1
  1.2 1.0 collective-permute-start
  2.2 22.0 %collective-permute-done.1 = bf16[512,1024]{1,0:T(8,128)(2,1)S(1)} collective-permute-done((bf16[512,1024]{1,0:T(8,128)(2,1)}, bf16[512,1024]{1,0:T(8,128)(2,1)S(1)}, u32[]{:S(2)}, u32[]{:S(2)}) %collective-permute-start.1) | collective-permute-done | bytes 1048608 | tf_op jit(solution)/shard_map/ppermute | solution.py:94
  24.2 1.5 %collective-permute-start.2 = (bf16[512,1024]{1,0:T(8,128)(2,1)S(1)}, bf16[512,1024]{1,0:T(8,128)(2,1)S(1)}, u32[]{:S(2)}, u32[]{:S(2)}) collective-permute-start(bf16[512,1024]{1,0:T(8,128)(2,1)S(1)} %collective-permute-done.1), channel_id=1, source_target_pairs={{0,4},{4,0},{8,12},{12,8},{1,5},{5,1},{9,13},{13,9},{2,6},{6,2},{1... | collective-permute-start | bytes 3145736 | tf_op jit(solution)/shard_map/ppermute | solution.py:94
  25.8 0.5 broadcast_in_dim.9
  26.3 0.1 constant_dynamic-update-slice_fusion.6
  26.4 0.0 collective-permute-done
  26.4 1.3 constant_dynamic-update-slice_fusion.5
  27.8 0.1 constant_dynamic-update-slice_fusion.4
  27.9 0.2 collective-permute-done.2
  28.1 0.1 constant_dynamic-update-slice_fusion.3
  28.2 8.5 %fusion = f32[512,1024]{1,0:T(8,128)S(1)} fusion(bf16[512,4096]{1,0:T(8,128)(2,1)S(1)} %constant_dynamic-update-slice_fusion.3, bf16[4096,3,1024]{2,0,1:T(8,128)(2,1)} %param.10), kind=kOutput, calls=%fused_computation | convolution fusion | flops 4294967296 | bytes 14680064 | tf_op jit(solution)/shard_map/dot_general | solution.py:129
  36.7 0.0 copy-done.2
  36.7 7.2 %multiply_convert_fusion.1 = bf16[512,1024]{1,0:T(8,128)(2,1)S(1)} fusion(f32[512,1024]{1,0:T(8,128)S(1)} %fusion, bf16[512,4096]{1,0:T(8,128)(2,1)S(1)} %constant_dynamic-update-slice_fusion.3, bf16[4096,3,1024]{2,0,1:T(8,128)(2,1)} %param.10), kind=kOutput, calls=%fused_computation.19 | convolution fusion | flops 4296015872 | bytes 15728640 | tf_op jit(solution)/shard_map/dot_general | solution.py:128
  43.9 0.0 copy-start
  43.9 0.0 copy-start.1
  43.9 0.1 dynamic-slice_bitcast_fusion
  44.1 1.4 collective-permute-start.3
  45.5 1.1 collective-permute-start.4
  46.5 1.4 collective-permute-start.5
  47.9 0.8 dynamic_slice.35
  48.7 1.3 constant_dynamic-slice_fusion.taps_ref
  50.0 1.7 %collective-permute-done.3 = bf16[512,256]{1,0:T(8,128)(2,1)S(1)} collective-permute-done((bf16[512,256]{1,0:T(8,128)(2,1)S(1)}, bf16[512,256]{1,0:T(8,128)(2,1)S(1)}, u32[]{:S(2)}, u32[]{:S(2)}) %collective-permute-start.3) | collective-permute-done | bytes 262176 | tf_op jit(solution)/shard_map/ppermute | solution.py:90
  51.7 16.0 %collective-permute-done.4 = bf16[512,256]{1,0:T(8,128)(2,1)} collective-permute-done((bf16[512,256]{1,0:T(8,128)(2,1)S(1)}, bf16[512,256]{1,0:T(8,128)(2,1)}, u32[]{:S(2)}, u32[]{:S(2)}) %collective-permute-start.4) | collective-permute-done | bytes 262176 | tf_op jit(solution)/shard_map/ppermute | solution.py:90
  67.6 2.6 %collective-permute-done.5 = bf16[512,256]{1,0:T(8,128)(2,1)} collective-permute-done((bf16[512,256]{1,0:T(8,128)(2,1)S(1)}, bf16[512,256]{1,0:T(8,128)(2,1)}, u32[]{:S(2)}, u32[]{:S(2)}) %collective-permute-start.5) | collective-permute-done | bytes 262176 | tf_op jit(solution)/shard_map/ppermute | solution.py:90
  70.2 1.2 pad_maximum_fusion.x_ref
  71.4 5.2 %shard_map.73 = bf16[4,512,256]{2,1,0:T(8,128)(2,1)S(1)} custom-call(bf16[4,512,256]{2,1,0:T(8,128)(2,1)S(1)} %pad_maximum_fusion.x_ref, bf16[2048,256]{1,0:T(8,128)(2,1)S(1)} %constant_dynamic-slice_fusion.taps_ref, f32[1,256]{1,0:T(1,128)S(1)} %bitcast.38, bf16[512,512]{1,0:T(8,128)(2,1)S(1)} %copy-done, bf16[256,512]{1,0:T(8,128)(2,1)S(1)} %copy-done.1), custom_call_target="tpu_custom_call" | custom-call | flops 8000000000 | bytes 4000000 | tf_op jit(solution)/shard_map/pallas_call | solution.py:78
  76.7 0.8 slice_bitcast_fusion
  77.4 0.0 collective-permute-start.6
  77.4 0.6 collective-permute-start.7
  78.0 1.5 %collective-permute-start.8 = (bf16[512,256]{1,0:T(8,128)(2,1)S(1)}, bf16[512,256]{1,0:T(8,128)(2,1)S(1)}, u32[]{:S(2)}, u32[]{:S(2)}) collective-permute-start(bf16[512,256]{1,0:T(8,128)(2,1)S(1)} %get-tuple-element.5), channel_id=1, source_target_pairs={{0,3},{1,0},{2,1},{3,2},{4,7},{5,4},{6,5},{7,6},{8,11},{9,8},{10,9... | collective-permute-start | bytes 786440 | tf_op jit(solution)/shard_map/ppermute | solution.py:90
  79.5 0.1 broadcast_in_dim.10
  79.7 5.4 %collective-permute-done.6 = bf16[512,256]{1,0:T(8,128)(2,1)S(1)} collective-permute-done((bf16[512,256]{1,0:T(8,128)(2,1)}, bf16[512,256]{1,0:T(8,128)(2,1)S(1)}, u32[]{:S(2)}, u32[]{:S(2)}) %collective-permute-start.6) | collective-permute-done | bytes 262176 | tf_op jit(solution)/shard_map/ppermute | solution.py:90
  85.0 14.9 %collective-permute-done.7 = bf16[512,256]{1,0:T(8,128)(2,1)S(1)} collective-permute-done((bf16[512,256]{1,0:T(8,128)(2,1)S(1)}, bf16[512,256]{1,0:T(8,128)(2,1)S(1)}, u32[]{:S(2)}, u32[]{:S(2)}) %collective-permute-start.7) | collective-permute-done | bytes 262176 | tf_op jit(solution)/shard_map/ppermute | solution.py:90
  100.0 1.9 %collective-permute-done.8 = bf16[512,256]{1,0:T(8,128)(2,1)S(1)} collective-permute-done((bf16[512,256]{1,0:T(8,128)(2,1)S(1)}, bf16[512,256]{1,0:T(8,128)(2,1)S(1)}, u32[]{:S(2)}, u32[]{:S(2)}) %collective-permute-start.8) | collective-permute-done | bytes 262176 | tf_op jit(solution)/shard_map/ppermute | solution.py:90
  101.9 0.0 slice-start.1
  101.9 9.3 %multiply_convert_fusion = bf16[512,1024]{1,0:T(8,128)(2,1)S(1)} fusion(bf16[512,1024]{1,0:T(8,128)(2,1)S(1)} %constant_dynamic-update-slice_fusion, bf16[512,4096]{1,0:T(8,128)(2,1)} %copy-done.2, bf16[4096,3,1024]{2,0,1:T(8,128)(2,1)} %param.10), kind=kOutput, calls=%fused_computation.18 | convolution fusion | flops 4297588736 | bytes 14680064 | tf_op jit(solution)/shard_map/dot_general | solution.py:135
  111.2 1.3 collective-permute-start.10
  112.5 0.8 collective-permute-start.9
  113.3 22.2 %collective-permute-done.10 = bf16[512,1024]{1,0:T(8,128)(2,1)S(1)} collective-permute-done((bf16[512,1024]{1,0:T(8,128)(2,1)S(1)}, bf16[512,1024]{1,0:T(8,128)(2,1)S(1)}, u32[]{:S(2)}, u32[]{:S(2)}) %collective-permute-start.10) | collective-permute-done | bytes 1048608 | tf_op jit(solution)/shard_map/ppermute | solution.py:94
  135.5 1.3 collective-permute-start.11
  136.9 0.0 slice-done
  136.9 1.3 fusion.15
  138.1 1.3 fusion.11
  139.4 0.0 collective-permute-done.9
  139.5 1.3 fusion.13
  140.8 0.0 collective-permute-done.11
  140.8 2.3 %add_convert_fusion = bf16[512,1024]{1,0:T(8,128)(2,1)} fusion(f32[512,1024]{1,0:T(8,128)S(1)} %fusion.11, f32[512,1024]{1,0:T(8,128)S(1)} %fusion.15, f32[512,1024]{1,0:T(8,128)S(1)} %fusion.13, bf16[512,1024]{1,0:T(8,128)(2,1)S(1)} %collective-permute-done.11, bf16[4096,1024]{1,0:T(8,128)(2,1)S(1)} %bitcast.41, s32[]{:T(128)S(6)} %select_n.70), kind=kOutput, calls=%fused_computation.9 | convolution fusion | flops 1075838976 | bytes 10485764 | tf_op jit(solution)/shard_map/dot_general | solution.py:147
  (12 shorter events, 0.1 us)
Async XLA Ops:
  0.0 26.3 %copy-start.3 = (bf16[512,1024]{1,0:T(8,128)(2,1)S(1)}, bf16[512,1024]{1,0:T(8,128)(2,1)}, u32[]{:S(2)}) copy-start(bf16[512,1024]{1,0:T(8,128)(2,1)} %param.7) | copy-start | bytes 3145732
  0.0 24.2 %collective-permute-start.1 = (bf16[512,1024]{1,0:T(8,128)(2,1)}, bf16[512,1024]{1,0:T(8,128)(2,1)S(1)}, u32[]{:S(2)}, u32[]{:S(2)}) collective-permute-start(bf16[512,1024]{1,0:T(8,128)(2,1)} %param.7), channel_id=1, source_target_pairs={{0,8},{4,12},{8,0},{12,4},{1,9},{5,13},{9,1},{13,5},{2,10},{6,14},... | collective-permute-start | bytes 3145736 | tf_op jit(solution)/shard_map/ppermute | solution.py:94
  1.2 25.2 %collective-permute-start = (bf16[512,1024]{1,0:T(8,128)(2,1)}, bf16[512,1024]{1,0:T(8,128)(2,1)}, u32[]{:S(2)}, u32[]{:S(2)}) collective-permute-start(bf16[512,1024]{1,0:T(8,128)(2,1)} %param.7), channel_id=1, source_target_pairs={{0,4},{4,0},{8,12},{12,8},{1,5},{5,1},{9,13},{13,9},{2,6},{6,2},{1... | collective-permute-start | bytes 3145736 | tf_op jit(solution)/shard_map/ppermute | solution.py:94
  24.2 3.8 %collective-permute-start.2 = (bf16[512,1024]{1,0:T(8,128)(2,1)S(1)}, bf16[512,1024]{1,0:T(8,128)(2,1)S(1)}, u32[]{:S(2)}, u32[]{:S(2)}) collective-permute-start(bf16[512,1024]{1,0:T(8,128)(2,1)S(1)} %collective-permute-done.1), channel_id=1, source_target_pairs={{0,4},{4,0},{8,12},{12,8},{1,5},{5,1},{9,13},{13,9},{2,6},{6,2},{1... | collective-permute-start | bytes 3145736 | tf_op jit(solution)/shard_map/ppermute | solution.py:94
  28.2 8.5 %copy-start.2 = (bf16[512,4096]{1,0:T(8,128)(2,1)}, bf16[512,4096]{1,0:T(8,128)(2,1)S(1)}, u32[]{:S(2)}) copy-start(bf16[512,4096]{1,0:T(8,128)(2,1)S(1)} %constant_dynamic-update-slice_fusion.3) | copy-start | bytes 12582916
  43.9 27.5 %copy-start = (bf16[512,512]{1,0:T(8,128)(2,1)S(1)}, bf16[512,512]{1,0:T(8,128)(2,1)}, u32[]{:S(2)}) copy-start(bf16[512,512]{1,0:T(8,128)(2,1)} %constant.73.clone.fwd_ref) | copy-start | bytes 1572868
  43.9 27.5 %copy-start.1 = (bf16[256,512]{1,0:T(8,128)(2,1)S(1)}, bf16[256,512]{1,0:T(8,128)(2,1)}, u32[]{:S(2)}) copy-start(bf16[256,512]{1,0:T(8,128)(2,1)} %constant.74.clone.inv_ref) | copy-start | bytes 786436
  44.1 7.6 %collective-permute-start.3 = (bf16[512,256]{1,0:T(8,128)(2,1)S(1)}, bf16[512,256]{1,0:T(8,128)(2,1)S(1)}, u32[]{:S(2)}, u32[]{:S(2)}) collective-permute-start(bf16[512,256]{1,0:T(8,128)(2,1)S(1)} %get-tuple-element.11), channel_id=1, source_target_pairs={{0,1},{1,2},{2,3},{3,0},{4,5},{5,6},{6,7},{7,4},{8,9},{9,10},{10,1... | collective-permute-start | bytes 786440 | tf_op jit(solution)/shard_map/ppermute | solution.py:90
  45.5 22.2 %collective-permute-start.4 = (bf16[512,256]{1,0:T(8,128)(2,1)S(1)}, bf16[512,256]{1,0:T(8,128)(2,1)}, u32[]{:S(2)}, u32[]{:S(2)}) collective-permute-start(bf16[512,256]{1,0:T(8,128)(2,1)S(1)} %get-tuple-element.10), channel_id=1, source_target_pairs={{0,2},{1,3},{2,0},{3,1},{4,6},{5,7},{6,4},{7,5},{8,10},{9,11},{10,... | collective-permute-start | bytes 786440 | tf_op jit(solution)/shard_map/ppermute | solution.py:90
  46.5 23.7 %collective-permute-start.5 = (bf16[512,256]{1,0:T(8,128)(2,1)S(1)}, bf16[512,256]{1,0:T(8,128)(2,1)}, u32[]{:S(2)}, u32[]{:S(2)}) collective-permute-start(bf16[512,256]{1,0:T(8,128)(2,1)S(1)} %get-tuple-element.9), channel_id=1, source_target_pairs={{0,3},{1,0},{2,1},{3,2},{4,7},{5,4},{6,5},{7,6},{8,11},{9,8},{10,9... | collective-permute-start | bytes 786440 | tf_op jit(solution)/shard_map/ppermute | solution.py:90
  77.4 7.6 %collective-permute-start.6 = (bf16[512,256]{1,0:T(8,128)(2,1)}, bf16[512,256]{1,0:T(8,128)(2,1)S(1)}, u32[]{:S(2)}, u32[]{:S(2)}) collective-permute-start(bf16[512,256]{1,0:T(8,128)(2,1)} %get-tuple-element.7), channel_id=1, source_target_pairs={{0,1},{1,2},{2,3},{3,0},{4,5},{5,6},{6,7},{7,4},{8,9},{9,10},{10,1... | collective-permute-start | bytes 786440 | tf_op jit(solution)/shard_map/ppermute | solution.py:90
  77.4 22.6 %collective-permute-start.7 = (bf16[512,256]{1,0:T(8,128)(2,1)S(1)}, bf16[512,256]{1,0:T(8,128)(2,1)S(1)}, u32[]{:S(2)}, u32[]{:S(2)}) collective-permute-start(bf16[512,256]{1,0:T(8,128)(2,1)S(1)} %get-tuple-element.6), channel_id=1, source_target_pairs={{0,2},{1,3},{2,0},{3,1},{4,6},{5,7},{6,4},{7,5},{8,10},{9,11},{10,... | collective-permute-start | bytes 786440 | tf_op jit(solution)/shard_map/ppermute | solution.py:90
  78.0 23.9 %collective-permute-start.8 = (bf16[512,256]{1,0:T(8,128)(2,1)S(1)}, bf16[512,256]{1,0:T(8,128)(2,1)S(1)}, u32[]{:S(2)}, u32[]{:S(2)}) collective-permute-start(bf16[512,256]{1,0:T(8,128)(2,1)S(1)} %get-tuple-element.5), channel_id=1, source_target_pairs={{0,3},{1,0},{2,1},{3,2},{4,7},{5,4},{6,5},{7,6},{8,11},{9,8},{10,9... | collective-permute-start | bytes 786440 | tf_op jit(solution)/shard_map/ppermute | solution.py:90
  79.5 57.4 %slice-start = ((s8[8388608]{0:T(1024)(128)(4,1)}), s8[4194304]{0:T(1024)(128)(4,1)S(1)}, s32[]{:S(2)}) async-start(s8[8388608]{0:T(1024)(128)(4,1)} %bitcast.40), calls=%async_computation | async-start | bytes 8388608
  101.9 34.9 %slice-start.1 = ((s8[8388608]{0:T(1024)(128)(4,1)}), s8[4194304]{0:T(1024)(128)(4,1)S(1)}, s32[]{:S(2)}) async-start(s8[8388608]{0:T(1024)(128)(4,1)} %bitcast.40), calls=%async_computation.1 | async-start | bytes 8388608
  111.2 24.3 %collective-permute-start.10 = (bf16[512,1024]{1,0:T(8,128)(2,1)S(1)}, bf16[512,1024]{1,0:T(8,128)(2,1)S(1)}, u32[]{:S(2)}, u32[]{:S(2)}) collective-permute-start(bf16[512,1024]{1,0:T(8,128)(2,1)S(1)} %multiply_convert_fusion), channel_id=1, source_target_pairs={{0,8},{4,12},{8,0},{12,4},{1,9},{5,13},{9,1},{13,5},{2,10},{6,14},... | collective-permute-start | bytes 3145736 | tf_op jit(solution)/shard_map/ppermute | solution.py:94
  112.5 26.9 %collective-permute-start.9 = (bf16[512,1024]{1,0:T(8,128)(2,1)S(1)}, bf16[512,1024]{1,0:T(8,128)(2,1)S(1)}, u32[]{:S(2)}, u32[]{:S(2)}) collective-permute-start(bf16[512,1024]{1,0:T(8,128)(2,1)S(1)} %multiply_convert_fusion), channel_id=1, source_target_pairs={{0,4},{4,0},{8,12},{12,8},{1,5},{5,1},{9,13},{13,9},{2,6},{6,2},{1... | collective-permute-start | bytes 3145736 | tf_op jit(solution)/shard_map/ppermute | solution.py:94
  135.5 5.2 %collective-permute-start.11 = (bf16[512,1024]{1,0:T(8,128)(2,1)S(1)}, bf16[512,1024]{1,0:T(8,128)(2,1)S(1)}, u32[]{:S(2)}, u32[]{:S(2)}) collective-permute-start(bf16[512,1024]{1,0:T(8,128)(2,1)S(1)} %collective-permute-done.10), channel_id=1, source_target_pairs={{0,4},{4,0},{8,12},{12,8},{1,5},{5,1},{9,13},{13,9},{2,6},{6,2},{1... | collective-permute-start | bytes 3145736 | tf_op jit(solution)/shard_map/ppermute | solution.py:94

commit v2 on v1

v2 whole, which is shorter than its diff:
```python
import functools
import math

import jax
import jax.numpy as jnp
import numpy as np
from jax import lax
from jax.experimental import pallas as pl
from jax.experimental.pallas import tpu as pltpu
from jax.sharding import PartitionSpec as P

BLOCK = 256


def tables(block):
    period = 2 * block
    freq = 2 * np.arange(block, dtype=np.int64)[:, None] + 1
    place = np.arange(period, dtype=np.int64)[None, :]
    angle = (freq * place % (2 * period)) * (math.pi / period)
    forward = np.concatenate([np.cos(angle), -np.sin(angle)], axis=0)
    kept = angle[:, block:].T
    inverse = np.concatenate([np.cos(kept), -np.sin(kept)], axis=1) / block
    return jnp.asarray(forward, jnp.bfloat16), jnp.asarray(inverse, jnp.bfloat16)


def conv_kernel(n, per, *refs):
    count = n * per
    x_refs, (taps_ref, skip_ref, fwd_ref, inv_ref) = refs[:count], refs[count : count + 4]
    out_refs, (xs, gs, ys) = refs[count + 4 : 2 * count + 4], refs[2 * count + 4 :]
    me = lax.axis_index("ctx")
    cc = taps_ref.shape[1]
    for k in range(count):
        if k == 0:
            gs[k] = jnp.dot(fwd_ref[:, BLOCK:], taps_ref[:BLOCK], preferred_element_type=jnp.float32)
        else:
            gs[k] = jnp.dot(
                fwd_ref[...], taps_ref[(k - 1) * BLOCK : (k + 1) * BLOCK], preferred_element_type=jnp.float32
            )
    for s in range(n):
        for t in range(per):
            xs[lax.rem(me - s + n, n) * per + t] = jnp.dot(
                fwd_ref[:, :BLOCK], x_refs[s * per + t][...], preferred_element_type=jnp.float32
            )

    lane = min(cc, 128)

    def mix(i, carry):
        re = pl.ds(pl.multiple_of(i * 8, 8), 8)
        im = pl.ds(pl.multiple_of(i * 8 + BLOCK, 8), 8)
        for l in range(0, cc, lane):
            ls = slice(l, l + lane)
            xr = [xs[a, re, ls] for a in range(count)]
            xi = [xs[a, im, ls] for a in range(count)]
            gr = [gs[a, re, ls] for a in range(count)]
            gi = [gs[a, im, ls] for a in range(count)]
            for b in range(count):
                yr = xr[0] * gr[b] - xi[0] * gi[b]
                yi = xi[0] * gr[b] + xr[0] * gi[b]
                for a in range(1, b + 1):
                    yr = yr + xr[a] * gr[b - a] - xi[a] * gi[b - a]
                    yi = yi + xi[a] * gr[b - a] + xr[a] * gi[b - a]
                ys[b, re, ls] = yr
                ys[b, im, ls] = yi
        return carry

    lax.fori_loop(0, BLOCK // 8, mix, 0)
    for s in range(n):
        for t in range(per):
            spectra = ys[lax.rem(me + s, n) * per + t].astype(jnp.bfloat16)
            conv = jnp.dot(inv_ref[...], spectra, preferred_element_type=jnp.float32)
            held = x_refs[(n - s) % n * per + t][...].astype(jnp.float32)
            out_refs[s * per + t][...] = (conv + skip_ref[...] * held).astype(jnp.bfloat16)


def convolve(n, per, x, taps, skip):
    cc = taps.shape[1]
    forward, inverse = tables(BLOCK)
    count = n * per
    spectra = pltpu.VMEM((count, 2 * BLOCK, cc), jnp.float32)
    vmem = pl.BlockSpec(memory_space=pltpu.VMEM)
    return pl.pallas_call(
        functools.partial(conv_kernel, n, per),
        out_shape=[jax.ShapeDtypeStruct((BLOCK, cc), jnp.bfloat16)] * count,
        in_specs=[vmem] * (count + 4),
        out_specs=[vmem] * count,
        scratch_shapes=[spectra, spectra, spectra],
        compiler_params=pltpu.CompilerParams(vmem_limit_bytes=40 * 1024 * 1024),
        cost_estimate=pl.CostEstimate(flops=6_000_000_000, bytes_accessed=4_000_000, transcendentals=0),
    )(*x, taps, skip, forward, inverse)


def shift(x, axis, n, by):
    return lax.ppermute(x, axis, [(i, (i + by) % n) for i in range(n)])


def flip(x, n, bit):
    return lax.ppermute(x, "chan", [(i, i ^ bit) for i in range(n)])


def after(x, *others):
    return lax.optimization_barrier((x, *others))[0]


def exchange(parts, n):
    return [parts[0]] + [shift(parts[s], "ctx", n, s) for s in range(1, n)]


def shards(features, filter_taps, skip_gain, in_weight, out_weight):
    f32 = jnp.float32
    n_ctx, n_chan = lax.axis_size("ctx"), lax.axis_size("chan")
    ctx, chan = lax.axis_index("ctx"), lax.axis_index("chan")
    rows, channels = features.shape[0], in_weight.shape[2]
    width = features.shape[1]
    cc = channels // n_ctx
    per = rows // BLOCK
    paired = n_chan == 4
    taps = lax.dynamic_slice_in_dim(filter_taps, ctx * cc, cc, 1)
    skip = lax.dynamic_slice_in_dim(skip_gain, ctx * cc, cc, 0)[None, :]
    parts = range(per)

    def into(piece, owner, s):
        weight = lax.dynamic_slice(in_weight, (owner * width, s, 0), (width, 1, channels))[:, 0]
        return jnp.dot(piece, weight, preferred_element_type=f32)

    def chunk(x, t):
        return x[t * BLOCK : (t + 1) * BLOCK]

    if paired:
        across, last = [], None
        for t in parts:
            sent = chunk(features, t)
            across.append(flip(sent if last is None else after(sent, last), n_chan, 2))
            last = across[-1]
        beside = flip(features, n_chan, 1)
        near = [into(features, chan, s) + into(beside, chan ^ 1, s) for s in range(3)]
        far = [[(chan ^ 2, across[t]), (chan ^ 3, flip(across[t], n_chan, 1))] for t in parts]
    else:
        whole = lax.all_gather(features, "chan", axis=1, tiled=True)
        near = [into(whole[:, :width], 0, s) for s in range(3)]
        far = [[(j, chunk(whole, t)[:, j * width : (j + 1) * width]) for j in range(1, n_chan)] for t in parts]

    def project(t, s):
        total = chunk(near[s], t)
        for owner, piece in far[t]:
            total = total + into(piece, owner, s)
        return total

    got = []
    for t in parts:
        mixed = (project(t, 1) * project(t, 2)).astype(jnp.bfloat16)
        sends = [
            lax.dynamic_slice_in_dim(mixed, ((ctx + s) % n_ctx) * cc, cc, 1) for s in range(n_ctx)
        ]
        got.append(exchange(sends, n_ctx))
    query = [project(t, 0).astype(jnp.bfloat16) for t in parts]
    x = [got[t][s] for s in range(n_ctx) for t in parts]
    x = lax.optimization_barrier((*x, *query))[: len(x)]
    y = convolve(n_ctx, per, x, taps, skip)

    outs, last = [], None
    for t in parts:
        sends = [y[s * per + t] for s in range(n_ctx)]
        if last is not None:
            sends = lax.optimization_barrier((*sends, *last))[:n_ctx]
        back = last = exchange(sends, n_ctx)
        summed = jnp.zeros((BLOCK, channels), jnp.bfloat16)
        for s in range(n_ctx):
            summed = lax.dynamic_update_slice(summed, back[s], (0, ((ctx - s + n_ctx) % n_ctx) * cc))
        gated = (query[t].astype(f32) * summed.astype(f32)).astype(jnp.bfloat16)
        if paired:
            far_side = flip(gated, n_chan, 2)
            pieces = [(chan, gated), (chan ^ 1, flip(gated, n_chan, 1))]
            pieces += [(chan ^ 2, far_side), (chan ^ 3, flip(far_side, n_chan, 1))]
        else:
            pieces = [(0, lax.all_gather(gated, "chan", axis=1, tiled=True))]
        total = None
        for owner, piece in pieces:
            depth = piece.shape[1]
            weight = lax.dynamic_slice_in_dim(out_weight, owner * depth, depth, 0)
            term = jnp.dot(piece, weight, preferred_element_type=f32)
            total = term if total is None else total + term
        outs.append(total.astype(jnp.bfloat16))
    return jnp.concatenate(outs, axis=0)


def solution(mesh):
    return jax.shard_map(
        shards,
        mesh=mesh,
        in_specs=(
            P(("grp", "ctx"), "chan"),
            P(None, "chan"),
            P("chan"),
            P(None, None, "chan"),
            P(None, "chan"),
        ),
        out_specs=P(("grp", "ctx"), "chan"),
        check_vma=False,
    )
```

time: 143 us -> 132 us (0.923)
  waiting for transfers between devices: 86.9 us -> 31.2 us
  matrix products: 31.1 us -> 65.5 us
  starting transfers between devices: 13 us -> 22.6 us
    ppermute x6 -> x11, waiting for transfers between devices: 44.4 us -> 4.34 us  [flip(): return lax.ppermute(x, 'chan', [(i, i ^ bit) for i in range(n)])]
    dot_general x3 -> x18, matrix products: 25 us -> 51 us  [into(): return jnp.dot(piece, weight, preferred_element_type=f32)]
    ppermute x6 -> x12, waiting for transfers between devices: 42.4 us -> 26.9 us  [shift(): return lax.ppermute(x, axis, [(i, (i + by) % n) for i in range(n)])]
    dot_general x4 -> x8, matrix products: 6.17 us -> 14.5 us  [shards(): term = jnp.dot(piece, weight, preferred_element_type=f32)]
    ppermute x6 -> x12, starting transfers between devices: 5.9 us -> 13.7 us  [shift(): return lax.ppermute(x, axis, [(i, (i + by) % n) for i in range(n)])]
    dynamic_update_slice x4 -> x0, local copies, waits for them, and re-layouts: 1.7 us -> none  [gather(): whole = lax.dynamic_update_slice(whole, piece, (0, (me ^ far) * width))]
    ppermute x6 -> x11, starting transfers between devices: 7.15 us -> 8.83 us  [flip(): return lax.ppermute(x, 'chan', [(i, i ^ bit) for i in range(n)])]
  transfers between devices with their start and end apart: 12 -> 23, of which waited for: 9 -> 8; matrix products, arithmetic and copies ran while one was open for 6% -> 53% of each run, Pallas kernels for 0% -> 0%
where the time goes in v2:
time: 132 us; the launch traced here: 131 us
  matrix products  65.5 us (50%)
  waiting for transfers between devices  31.2 us (24%)
  starting transfers between devices  22.6 us (17%)
  Pallas kernels  5.3 us (4%)
  local copies, waits for them, and re-layouts  4.51 us (3%)
    dot_general x18, matrix products, into(): return jnp.dot(piece, weight, preferred_element_type=f32)  51 us
    ppermute x12, waiting for transfers between devices, shift(): return lax.ppermute(x, axis, [(i, (i + by) % n) for i in range(n)])  26.9 us
    dot_general x8, matrix products, shards(): term = jnp.dot(piece, weight, preferred_element_type=f32)  14.5 us
    ppermute x12, starting transfers between devices, shift(): return lax.ppermute(x, axis, [(i, (i + by) % n) for i in range(n)])  13.7 us
    ppermute x11, starting transfers between devices, flip(): return lax.ppermute(x, 'chan', [(i, i ^ bit) for i in range(n)])  8.83 us
    pallas_call x1, Pallas kernels, convolve(): pl.pallas_call(functools.partial(conv_kernel, n, per), out_shape=[jax.Sha...  5.3 us
    ppermute x11, waiting for transfers between devices, flip(): return lax.ppermute(x, 'chan', [(i, i ^ bit) for i in range(n)])  4.34 us
  transfers between devices with their start and end apart: 23, of which 8 were waited for; matrix products, arithmetic and copies ran while one was open for 53% of the time, Pallas kernels for 0%

profile of v2, /device:TPU:11, one launch (start us, length us, event | category | flops | bytes accessed | tf_op | source)
XLA Modules:
  0.0 131.0 jit_solution(3067261016029595366)
XLA Ops:
  0.7 1.3 fusion.192
  1.9 1.3 %collective-permute-start.1 = (bf16[256,1024]{1,0:T(8,128)(2,1)S(1)}, bf16[256,1024]{1,0:T(8,128)(2,1)S(1)}, u32[]{:S(2)}, u32[]{:S(2)}) collective-permute-start(bf16[256,1024]{1,0:T(8,128)(2,1)S(1)} %get-tuple-element.48), channel_id=1, source_target_pairs={{0,8},{4,12},{8,0},{12,4},{1,9},{5,13},{9,1},{13,5},{2,10},{6,14},... | collective-permute-start | bytes 1572872 | tf_op jit(solution)/shard_map/ppermute | solution.py:97
  3.3 4.2 %fusion.10 = f32[1024,512]{0,1:T(8,128)} fusion(bf16[512,1024]{1,0:T(8,128)(2,1)S(1)} %copy-done.2, bf16[4096,3,1024]{2,0,1:T(8,128)(2,1)} %param.10, s32[]{:T(128)S(6)} %select_n.109), kind=kOutput, calls=%fused_computation.10 | convolution fusion | flops 1073741824 | bytes 5242884 | tf_op jit(solution)/shard_map/dot_general | solution.py:123
  7.5 4.2 %fusion.22 = f32[1024,512]{0,1:T(8,128)} fusion(bf16[512,1024]{1,0:T(8,128)(2,1)S(1)} %copy-done.2, bf16[4096,3,1024]{2,0,1:T(8,128)(2,1)} %param.10, s32[]{:T(128)S(6)} %select_n.109), kind=kOutput, calls=%fused_computation.22 | convolution fusion | flops 1073741824 | bytes 5242884 | tf_op jit(solution)/shard_map/dot_general | solution.py:123
  11.6 4.3 %fusion.34 = f32[1024,512]{1,0:T(8,128)} fusion(bf16[512,1024]{1,0:T(8,128)(2,1)S(1)} %copy-done.2, bf16[4096,3,1024]{2,0,1:T(8,128)(2,1)} %param.10, s32[]{:T(128)S(6)} %select_n.109), kind=kOutput, calls=%fused_computation.34 | convolution fusion | flops 1073741824 | bytes 5242884 | tf_op jit(solution)/shard_map/dot_general | solution.py:123
  15.9 0.8 dynamic_slice.109
  16.7 1.3 constant_dynamic-slice_fusion.refs_8_
  18.9 2.3 %fusion.88 = f32[256,1024]{1,0:T(8,128)S(1)} fusion(bf16[256,1024]{1,0:T(8,128)(2,1)S(1)} %collective-permute-done.1, bf16[4096,3,1024]{2,0,1:T(8,128)(2,1)} %param.10, s32[]{:T(128)S(6)} %select_n.111), kind=kOutput, calls=%fused_computation.77 | convolution fusion | flops 536870912 | bytes 3670020 | tf_op jit(solution)/shard_map/dot_general | solution.py:123
  21.2 2.3 %fusion.82 = f32[256,1024]{1,0:T(8,128)S(1)} fusion(bf16[256,1024]{1,0:T(8,128)(2,1)S(1)} %collective-permute-done.1, bf16[4096,3,1024]{2,0,1:T(8,128)(2,1)} %param.10, s32[]{:T(128)S(6)} %select_n.111), kind=kOutput, calls=%fused_computation.75 | convolution fusion | flops 536870912 | bytes 3670020 | tf_op jit(solution)/shard_map/dot_general | solution.py:123
  23.5 2.5 %fusion.76 = f32[256,1024]{0,1:T(8,128)S(1)} fusion(bf16[256,1024]{1,0:T(8,128)(2,1)S(1)} %collective-permute-done.1, bf16[4096,3,1024]{2,0,1:T(8,128)(2,1)} %param.10, s32[]{:T(128)S(6)} %select_n.111), kind=kOutput, calls=%fused_computation.73 | convolution fusion | flops 536870912 | bytes 3670020 | tf_op jit(solution)/shard_map/dot_general | solution.py:123
  26.1 3.3 %add_bitcast_fusion = f32[512,1024]{1,0:T(8,128)S(1)} fusion(f32[1024,512]{0,1:T(8,128)S(1)} %copy-done.4, bf16[512,1024]{1,0:T(8,128)(2,1)} %collective-permute-done, bf16[4096,3,1024]{2,0,1:T(8,128)(2,1)} %param.10, s32[]{:T(128)S(6)} %select_n.110), kind=kOutput, calls=%fused_computation.36 | convolution fusion | flops 1074266112 | bytes 7340036 | tf_op jit(solution)/shard_map/dot_general | solution.py:123
  29.4 3.2 %add_bitcast_fusion.1 = f32[512,1024]{1,0:T(8,128)S(1)} fusion(f32[1024,512]{0,1:T(8,128)S(1)} %copy-done.3, bf16[512,1024]{1,0:T(8,128)(2,1)} %collective-permute-done, bf16[4096,3,1024]{2,0,1:T(8,128)(2,1)} %param.10, s32[]{:T(128)S(6)} %select_n.110), kind=kOutput, calls=%fused_computation.39 | convolution fusion | flops 1074266112 | bytes 7340036 | tf_op jit(solution)/shard_map/dot_general | solution.py:123
  32.6 2.4 %fusion.94 = f32[256,1024]{1,0:T(8,128)S(1)} fusion(bf16[256,1024]{1,0:T(8,128)(2,1)S(1)} %collective-permute-done.2, bf16[4096,3,1024]{2,0,1:T(8,128)(2,1)} %param.10, s32[]{:T(128)S(6)} %select_n.112, f32[256,1024]{1,0:T(8,128)S(1)} %fusion.88, f32[512,1024]{1,0:T(8,128)S(1)} %add_bitcast_fusion), kind=kOutput, calls=%fused_computation.79 | convolution fusion | flops 537395200 | bytes 5767172 | tf_op jit(solution)/shard_map/dot_general | solution.py:123
  35.0 2.4 %fusion.151 = bf16[256,1024]{1,0:T(8,128)(2,1)S(1)} fusion(f32[256,1024]{1,0:T(8,128)S(1)} %fusion.94, bf16[256,1024]{1,0:T(8,128)(2,1)S(1)} %collective-permute-done.2, bf16[4096,3,1024]{2,0,1:T(8,128)(2,1)} %param.10, s32[]{:T(128)S(6)} %select_n.112, f32[256,1024]{1,0:T(8,128)S(1)} %fusion.82, f32[512,1024]{1,0:T(8,128)S(1)} %add_bitcast_fusion.1), kind=kOutput, calls=%fused_computation.98 | convolution fusion | flops 537919488 | bytes 6291460 | tf_op jit(solution)/shard_map/dot_general | solution.py:123
  37.5 1.3 %collective-permute-start.5 = (bf16[256,256]{1,0:T(8,128)(2,1)S(1)}, bf16[256,256]{1,0:T(8,128)(2,1)S(1)}, u32[]{:S(2)}, u32[]{:S(2)}) collective-permute-start(bf16[256,256]{1,0:T(8,128)(2,1)S(1)} %get-tuple-element.55), channel_id=1, source_target_pairs={{0,1},{1,2},{2,3},{3,0},{4,5},{5,6},{6,7},{7,4},{8,9},{9,10},{10,1... | collective-permute-start | bytes 393224 | tf_op jit(solution)/shard_map/ppermute | solution.py:93
  38.8 1.1 collective-permute-start.7
  39.9 1.4 %collective-permute-start.9 = (bf16[256,256]{1,0:T(8,128)(2,1)S(1)}, bf16[256,256]{1,0:T(8,128)(2,1)S(1)}, u32[]{:S(2)}, u32[]{:S(2)}) collective-permute-start(bf16[256,256]{1,0:T(8,128)(2,1)S(1)} %get-tuple-element.53), channel_id=1, source_target_pairs={{0,3},{1,0},{2,1},{3,2},{4,7},{5,4},{6,5},{7,6},{8,11},{9,8},{10,9... | collective-permute-start | bytes 393224 | tf_op jit(solution)/shard_map/ppermute | solution.py:93
  41.3 2.3 %fusion.4 = f32[256,1024]{1,0:T(8,128)S(1)} fusion(bf16[256,1024]{1,0:T(8,128)(2,1)S(1)} %collective-permute-done.3, bf16[4096,3,1024]{2,0,1:T(8,128)(2,1)} %param.10, s32[]{:T(128)S(6)} %select_n.111), kind=kOutput, calls=%fused_computation.4 | convolution fusion | flops 536870912 | bytes 3670020 | tf_op jit(solution)/shard_map/dot_general | solution.py:123
  43.6 0.9 collective-permute-start.4
  44.5 2.3 %fusion.16 = f32[256,1024]{1,0:T(8,128)S(1)} fusion(bf16[256,1024]{1,0:T(8,128)(2,1)S(1)} %collective-permute-done.3, bf16[4096,3,1024]{2,0,1:T(8,128)(2,1)} %param.10, s32[]{:T(128)S(6)} %select_n.111), kind=kOutput, calls=%fused_computation.16 | convolution fusion | flops 536870912 | bytes 3670020 | tf_op jit(solution)/shard_map/dot_general | solution.py:123
  46.8 3.2 %add_bitcast_fusion.2 = f32[512,1024]{0,1:T(8,128)S(1)} fusion(f32[1024,512]{1,0:T(8,128)S(1)} %copy-done.5, bf16[512,1024]{1,0:T(8,128)(2,1)} %collective-permute-done, bf16[4096,3,1024]{2,0,1:T(8,128)(2,1)} %param.10, s32[]{:T(128)S(6)} %select_n.110), kind=kOutput, calls=%fused_computation.42 | convolution fusion | flops 1074266112 | bytes 7340036 | tf_op jit(solution)/shard_map/dot_general | solution.py:123
  50.0 2.5 %fusion.28 = f32[256,1024]{0,1:T(8,128)S(1)} fusion(bf16[256,1024]{1,0:T(8,128)(2,1)S(1)} %collective-permute-done.3, bf16[4096,3,1024]{2,0,1:T(8,128)(2,1)} %param.10, s32[]{:T(128)S(6)} %select_n.111), kind=kOutput, calls=%fused_computation.28 | convolution fusion | flops 536870912 | bytes 3670020 | tf_op jit(solution)/shard_map/dot_general | solution.py:123
  52.6 2.4 %fusion.148 = bf16[256,1024]{0,1:T(8,128)(2,1)S(1)} fusion(bf16[256,1024]{1,0:T(8,128)(2,1)S(1)} %collective-permute-done.2, bf16[4096,3,1024]{2,0,1:T(8,128)(2,1)} %param.10, s32[]{:T(128)S(6)} %select_n.112, f32[256,1024]{0,1:T(8,128)S(1)} %fusion.76, f32[512,1024]{0,1:T(8,128)S(1)} %add_bitcast_fusion.2), kind=kOutput, calls=%fused_computation.97 | convolution fusion | flops 537657344 | bytes 5242884 | tf_op jit(solution)/shard_map/dot_general | solution.py:123
  55.0 2.4 %fusion.133 = f32[256,1024]{1,0:T(8,128)S(1)} fusion(bf16[256,1024]{1,0:T(8,128)(2,1)S(1)} %collective-permute-done.4, bf16[4096,3,1024]{2,0,1:T(8,128)(2,1)} %param.10, s32[]{:T(128)S(6)} %select_n.112, f32[256,1024]{1,0:T(8,128)S(1)} %fusion.4, f32[512,1024]{1,0:T(8,128)S(1)} %add_bitcast_fusion), kind=kOutput, calls=%fused_computation.92 | convolution fusion | flops 537395200 | bytes 5767172 | tf_op jit(solution)/shard_map/dot_general | solution.py:123
  57.4 2.4 %fusion.136 = bf16[256,1024]{1,0:T(8,128)(2,1)S(1)} fusion(f32[256,1024]{1,0:T(8,128)S(1)} %fusion.133, bf16[256,1024]{1,0:T(8,128)(2,1)S(1)} %collective-permute-done.4, bf16[4096,3,1024]{2,0,1:T(8,128)(2,1)} %param.10, s32[]{:T(128)S(6)} %select_n.112, f32[256,1024]{1,0:T(8,128)S(1)} %fusion.16, f32[512,1024]{1,0:T(8,128)S(1)} %add_bitcast_fusion.1), kind=kOutput, calls=%fused_computation.93 | convolution fusion | flops 537919488 | bytes 6291460 | tf_op jit(solution)/shard_map/dot_general | solution.py:123
  59.8 1.1 collective-permute-start.10
  61.4 1.9 %collective-permute-start.8 = (bf16[256,256]{1,0:T(8,128)(2,1)S(1)}, bf16[256,256]{1,0:T(8,128)(2,1)S(1)}, u32[]{:S(2)}, u32[]{:S(2)}) collective-permute-start(bf16[256,256]{1,0:T(8,128)(2,1)S(1)} %get-tuple-element.50), channel_id=1, source_target_pairs={{0,2},{1,3},{2,0},{3,1},{4,6},{5,7},{6,4},{7,5},{8,10},{9,11},{10,... | collective-permute-start | bytes 393224 | tf_op jit(solution)/shard_map/ppermute | solution.py:93
  63.2 2.6 %fusion.139 = bf16[256,1024]{0,1:T(8,128)(2,1)S(1)} fusion(bf16[256,1024]{1,0:T(8,128)(2,1)S(1)} %collective-permute-done.4, bf16[4096,3,1024]{2,0,1:T(8,128)(2,1)} %param.10, s32[]{:T(128)S(6)} %select_n.112, f32[256,1024]{0,1:T(8,128)S(1)} %fusion.28, f32[512,1024]{0,1:T(8,128)S(1)} %add_bitcast_fusion.2), kind=kOutput, calls=%fused_computation.94 | convolution fusion | flops 537657344 | bytes 5242884 | tf_op jit(solution)/shard_map/dot_general | solution.py:123
  65.8 1.6 %collective-permute-done.6.refs_3_ = bf16[256,256]{1,0:T(8,128)(2,1)S(1)} collective-permute-done((bf16[256,256]{1,0:T(8,128)(2,1)S(1)}, bf16[256,256]{1,0:T(8,128)(2,1)S(1)}, u32[]{:S(2)}, u32[]{:S(2)}) %collective-permute-start.6) | collective-permute-done | bytes 131104 | tf_op jit(solution)/shard_map/ppermute | solution.py:93
  67.4 5.1 %collective-permute-done.8.refs_5_ = bf16[256,256]{1,0:T(8,128)(2,1)S(1)} collective-permute-done((bf16[256,256]{1,0:T(8,128)(2,1)S(1)}, bf16[256,256]{1,0:T(8,128)(2,1)S(1)}, u32[]{:S(2)}, u32[]{:S(2)}) %collective-permute-start.8) | collective-permute-done | bytes 131104 | tf_op jit(solution)/shard_map/ppermute | solution.py:93
  72.5 5.3 %shard_map.73 = (bf16[256,256]{1,0:T(8,128)(2,1)S(1)}, bf16[256,256]{1,0:T(8,128)(2,1)S(1)}, bf16[256,256]{1,0:T(8,128)(2,1)S(1)}, bf16[256,256]{1,0:T(8,128)(2,...) custom-call(bf16[256,256]{1,0:T(8,128)(2,1)S(1)} %get-tuple-element., ...), custom_call_target="tpu_custom_call" | custom-call | flops 6000000000 | bytes 4000000 | tf_op jit(solution)/shard_map/pallas_call | solution.py:81
  78.0 4.1 %collective-permute-start.12 = (bf16[256,256]{1,0:T(8,128)(2,1)S(1)}, bf16[256,256]{1,0:T(8,128)(2,1)S(1)}, u32[]{:S(2)}, u32[]{:S(2)}) collective-permute-start(bf16[256,256]{1,0:T(8,128)(2,1)S(1)} %get-tuple-element.37), channel_id=1, source_target_pairs={{0,2},{1,3},{2,0},{3,1},{4,6},{5,7},{6,4},{7,5},{8,10},{9,11},{10,... | collective-permute-start | bytes 393224 | tf_op jit(solution)/shard_map/ppermute | solution.py:93
  82.9 7.7 %collective-permute-done.12 = bf16[256,256]{1,0:T(8,128)(2,1)S(1)} collective-permute-done((bf16[256,256]{1,0:T(8,128)(2,1)S(1)}, bf16[256,256]{1,0:T(8,128)(2,1)S(1)}, u32[]{:S(2)}, u32[]{:S(2)}) %collective-permute-start.12) | collective-permute-done | bytes 131104 | tf_op jit(solution)/shard_map/ppermute | solution.py:93
  90.7 2.6 %collective-permute-done.13 = bf16[256,256]{1,0:T(8,128)(2,1)S(1)} collective-permute-done((bf16[256,256]{1,0:T(8,128)(2,1)S(1)}, bf16[256,256]{1,0:T(8,128)(2,1)S(1)}, u32[]{:S(2)}, u32[]{:S(2)}) %collective-permute-start.13) | collective-permute-done | bytes 131104 | tf_op jit(solution)/shard_map/ppermute | solution.py:93
  93.6 1.3 %collective-permute-start.15 = (bf16[256,1024]{0,1:T(8,128)(2,1)S(1)}, bf16[256,1024]{0,1:T(8,128)(2,1)}, u32[]{:S(2)}, u32[]{:S(2)}) collective-permute-start(bf16[256,1024]{0,1:T(8,128)(2,1)S(1)} %multiply_convert_fusion.1), channel_id=1, source_target_pairs={{0,8},{4,12},{8,0},{12,4},{1,9},{5,13},{9,1},{13,5},{2,10},{6,14},... | collective-permute-start | bytes 1572872 | tf_op jit(solution)/shard_map/ppermute | solution.py:97
  94.9 1.3 collective-permute-start.14
  96.2 2.3 %fusion.56 = f32[256,1024]{1,0:T(8,128)S(1)} fusion(bf16[256,1024]{0,1:T(8,128)(2,1)S(1)} %multiply_convert_fusion.1, bf16[4096,1024]{1,0:T(8,128)(2,1)} %param.11, s32[]{:T(128)S(6)} %select_n.109), kind=kOutput, calls=%fused_computation.59 | convolution fusion | flops 536870912 | bytes 3670020 | tf_op jit(solution)/shard_map/dot_general | solution.py:180
  98.6 1.2 collective-permute-start.18
  100.5 0.9 collective-permute-done.17
  101.5 6.8 %collective-permute-done.18 = bf16[256,256]{1,0:T(8,128)(2,1)S(1)} collective-permute-done((bf16[256,256]{1,0:T(8,128)(2,1)S(1)}, bf16[256,256]{1,0:T(8,128)(2,1)S(1)}, u32[]{:S(2)}, u32[]{:S(2)}) %collective-permute-start.18) | collective-permute-done | bytes 131104 | tf_op jit(solution)/shard_map/ppermute | solution.py:93
  108.5 2.1 %collective-permute-done.19 = bf16[256,256]{1,0:T(8,128)(2,1)S(1)} collective-permute-done((bf16[256,256]{1,0:T(8,128)(2,1)S(1)}, bf16[256,256]{1,0:T(8,128)(2,1)S(1)}, u32[]{:S(2)}, u32[]{:S(2)}) %collective-permute-start.19) | collective-permute-done | bytes 131104 | tf_op jit(solution)/shard_map/ppermute | solution.py:93
  111.9 2.5 %fusion.54 = f32[256,1024]{1,0:T(8,128)S(1)} fusion(bf16[256,1024]{0,1:T(8,128)(2,1)S(1)} %multiply_convert_fusion, bf16[4096,1024]{1,0:T(8,128)(2,1)} %param.11, s32[]{:T(128)S(6)} %select_n.109), kind=kOutput, calls=%fused_computation.57 | convolution fusion | flops 536870912 | bytes 3670020 | tf_op jit(solution)/shard_map/dot_general | solution.py:180
  114.5 2.5 %fusion.48 = f32[256,1024]{1,0:T(8,128)S(1)} fusion(bf16[256,1024]{0,1:T(8,128)(2,1)} %collective-permute-done.15, bf16[4096,1024]{1,0:T(8,128)(2,1)} %param.11, s32[]{:T(128)S(6)} %select_n.111), kind=kOutput, calls=%fused_computation.51 | convolution fusion | flops 536870912 | bytes 3670020 | tf_op jit(solution)/shard_map/dot_general | solution.py:180
  117.0 2.7 %fusion.109 = f32[256,1024]{1,0:T(8,128)S(1)} fusion(f32[256,1024]{1,0:T(8,128)S(1)} %fusion.48, f32[256,1024]{1,0:T(8,128)S(1)} %fusion.56, bf16[256,1024]{0,1:T(8,128)(2,1)} %collective-permute-done.14, bf16[4096,1024]{1,0:T(8,128)(2,1)} %param.11, s32[]{:T(128)S(6)} %select_n.110), kind=kOutput, calls=%fused_computation.84 | convolution fusion | flops 537395200 | bytes 5767172 | tf_op jit(solution)/shard_map/dot_general | solution.py:180
  119.7 4.3 %collective-permute-done.21 = bf16[256,1024]{0,1:T(8,128)(2,1)S(1)} collective-permute-done((bf16[256,1024]{0,1:T(8,128)(2,1)S(1)}, bf16[256,1024]{0,1:T(8,128)(2,1)S(1)}, u32[]{:S(2)}, u32[]{:S(2)}) %collective-permute-start.21) | collective-permute-done | bytes 524320 | tf_op jit(solution)/shard_map/ppermute | solution.py:97
  124.0 1.3 %collective-permute-start.22 = (bf16[256,1024]{0,1:T(8,128)(2,1)S(1)}, bf16[256,1024]{0,1:T(8,128)(2,1)S(1)}, u32[]{:S(2)}, u32[]{:S(2)}) collective-permute-start(bf16[256,1024]{0,1:T(8,128)(2,1)S(1)} %collective-permute-done.21), channel_id=1, source_target_pairs={{0,4},{4,0},{8,12},{12,8},{1,5},{5,1},{9,13},{13,9},{2,6},{6,2},{1... | collective-permute-start | bytes 1572872 | tf_op jit(solution)/shard_map/ppermute | solution.py:97
  125.3 2.3 %fusion.46 = f32[256,1024]{1,0:T(8,128)S(1)} fusion(bf16[256,1024]{0,1:T(8,128)(2,1)S(1)} %collective-permute-done.21, bf16[4096,1024]{1,0:T(8,128)(2,1)} %param.11, s32[]{:T(128)S(6)} %select_n.111), kind=kOutput, calls=%fused_computation.49 | convolution fusion | flops 536870912 | bytes 3670020 | tf_op jit(solution)/shard_map/dot_general | solution.py:180
  129.9 1.0 pad_maximum_fusion
  (68 shorter events, 8.1 us)
Async XLA Ops:
  0.0 3.3 %copy-start.2 = (bf16[512,1024]{1,0:T(8,128)(2,1)S(1)}, bf16[512,1024]{1,0:T(8,128)(2,1)}, u32[]{:S(2)}) copy-start(bf16[512,1024]{1,0:T(8,128)(2,1)} %param.7) | copy-start | bytes 3145732
  0.0 26.0 %collective-permute-start = (bf16[512,1024]{1,0:T(8,128)(2,1)}, bf16[512,1024]{1,0:T(8,128)(2,1)}, u32[]{:S(2)}, u32[]{:S(2)}) collective-permute-start(bf16[512,1024]{1,0:T(8,128)(2,1)} %param.7), channel_id=1, source_target_pairs={{0,4},{4,0},{8,12},{12,8},{1,5},{5,1},{9,13},{13,9},{2,6},{6,2},{1... | collective-permute-start | bytes 3145736 | tf_op jit(solution)/shard_map/ppermute | solution.py:97
  1.9 16.0 %collective-permute-start.1 = (bf16[256,1024]{1,0:T(8,128)(2,1)S(1)}, bf16[256,1024]{1,0:T(8,128)(2,1)S(1)}, u32[]{:S(2)}, u32[]{:S(2)}) collective-permute-start(bf16[256,1024]{1,0:T(8,128)(2,1)S(1)} %get-tuple-element.48), channel_id=1, source_target_pairs={{0,8},{4,12},{8,0},{12,4},{1,9},{5,13},{9,1},{13,5},{2,10},{6,14},... | collective-permute-start | bytes 1572872 | tf_op jit(solution)/shard_map/ppermute | solution.py:97
  18.0 23.3 %collective-permute-start.3 = (bf16[256,1024]{1,0:T(8,128)(2,1)S(1)}, bf16[256,1024]{1,0:T(8,128)(2,1)S(1)}, u32[]{:S(2)}, u32[]{:S(2)}) collective-permute-start(bf16[256,1024]{1,0:T(8,128)(2,1)S(1)} %get-tuple-element.26), channel_id=1, source_target_pairs={{0,8},{4,12},{8,0},{12,4},{1,9},{5,13},{9,1},{13,5},{2,10},{6,14},... | collective-permute-start | bytes 1572872 | tf_op jit(solution)/shard_map/ppermute | solution.py:97
  18.3 14.4 %collective-permute-start.2 = (bf16[256,1024]{1,0:T(8,128)(2,1)S(1)}, bf16[256,1024]{1,0:T(8,128)(2,1)S(1)}, u32[]{:S(2)}, u32[]{:S(2)}) collective-permute-start(bf16[256,1024]{1,0:T(8,128)(2,1)S(1)} %collective-permute-done.1), channel_id=1, source_target_pairs={{0,4},{4,0},{8,12},{12,8},{1,5},{5,1},{9,13},{13,9},{2,6},{6,2},{1... | collective-permute-start | bytes 1572872 | tf_op jit(solution)/shard_map/ppermute | solution.py:97
  23.5 2.5 %copy-start.4 = (f32[1024,512]{0,1:T(8,128)S(1)}, f32[1024,512]{0,1:T(8,128)}, u32[]{:S(2)}) copy-start(f32[1024,512]{0,1:T(8,128)} %fusion.10) | copy-start | bytes 6291460
  26.0 3.4 %copy-start.3 = (f32[1024,512]{0,1:T(8,128)S(1)}, f32[1024,512]{0,1:T(8,128)}, u32[]{:S(2)}) copy-start(f32[1024,512]{0,1:T(8,128)} %fusion.22) | copy-start | bytes 6291460
  37.5 23.9 %collective-permute-start.5 = (bf16[256,256]{1,0:T(8,128)(2,1)S(1)}, bf16[256,256]{1,0:T(8,128)(2,1)S(1)}, u32[]{:S(2)}, u32[]{:S(2)}) collective-permute-start(bf16[256,256]{1,0:T(8,128)(2,1)S(1)} %get-tuple-element.55), channel_id=1, source_target_pairs={{0,1},{1,2},{2,3},{3,0},{4,5},{5,6},{6,7},{7,4},{8,9},{9,10},{10,1... | collective-permute-start | bytes 393224 | tf_op jit(solution)/shard_map/ppermute | solution.py:93
  38.8 27.0 %collective-permute-start.7 = (bf16[256,256]{1,0:T(8,128)(2,1)S(1)}, bf16[256,256]{1,0:T(8,128)(2,1)S(1)}, u32[]{:S(2)}, u32[]{:S(2)}) collective-permute-start(bf16[256,256]{1,0:T(8,128)(2,1)S(1)} %get-tuple-element.54), channel_id=1, source_target_pairs={{0,2},{1,3},{2,0},{3,1},{4,6},{5,7},{6,4},{7,5},{8,10},{9,11},{10,... | collective-permute-start | bytes 393224 | tf_op jit(solution)/shard_map/ppermute | solution.py:93
  39.9 25.9 %collective-permute-start.9 = (bf16[256,256]{1,0:T(8,128)(2,1)S(1)}, bf16[256,256]{1,0:T(8,128)(2,1)S(1)}, u32[]{:S(2)}, u32[]{:S(2)}) collective-permute-start(bf16[256,256]{1,0:T(8,128)(2,1)S(1)} %get-tuple-element.53), channel_id=1, source_target_pairs={{0,3},{1,0},{2,1},{3,2},{4,7},{5,4},{6,5},{7,6},{8,11},{9,8},{10,9... | collective-permute-start | bytes 393224 | tf_op jit(solution)/shard_map/ppermute | solution.py:93
  43.6 3.2 %copy-start.5 = (f32[1024,512]{1,0:T(8,128)S(1)}, f32[1024,512]{1,0:T(8,128)}, u32[]{:S(2)}) copy-start(f32[1024,512]{1,0:T(8,128)} %fusion.34) | copy-start | bytes 6291460
  43.6 11.4 %collective-permute-start.4 = (bf16[256,1024]{1,0:T(8,128)(2,1)S(1)}, bf16[256,1024]{1,0:T(8,128)(2,1)S(1)}, u32[]{:S(2)}, u32[]{:S(2)}) collective-permute-start(bf16[256,1024]{1,0:T(8,128)(2,1)S(1)} %collective-permute-done.3), channel_id=1, source_target_pairs={{0,4},{4,0},{8,12},{12,8},{1,5},{5,1},{9,13},{13,9},{2,6},{6,2},{1... | collective-permute-start | bytes 1572872 | tf_op jit(solution)/shard_map/ppermute | solution.py:97
  59.8 6.0 %collective-permute-start.10 = (bf16[256,256]{1,0:T(8,128)(2,1)S(1)}, bf16[256,256]{1,0:T(8,128)(2,1)S(1)}, u32[]{:S(2)}, u32[]{:S(2)}) collective-permute-start(bf16[256,256]{1,0:T(8,128)(2,1)S(1)} %get-tuple-element.49), channel_id=1, source_target_pairs={{0,3},{1,0},{2,1},{3,2},{4,7},{5,4},{6,5},{7,6},{8,11},{9,8},{10,9... | collective-permute-start | bytes 393224 | tf_op jit(solution)/shard_map/ppermute | solution.py:93
  61.0 6.5 %collective-permute-start.6 = (bf16[256,256]{1,0:T(8,128)(2,1)S(1)}, bf16[256,256]{1,0:T(8,128)(2,1)S(1)}, u32[]{:S(2)}, u32[]{:S(2)}) collective-permute-start(bf16[256,256]{1,0:T(8,128)(2,1)S(1)} %get-tuple-element.51), channel_id=1, source_target_pairs={{0,1},{1,2},{2,3},{3,0},{4,5},{5,6},{6,7},{7,4},{8,9},{9,10},{10,1... | collective-permute-start | bytes 393224 | tf_op jit(solution)/shard_map/ppermute | solution.py:93
  61.4 11.1 %copy-start = (bf16[512,512]{1,0:T(8,128)(2,1)S(1)}, bf16[512,512]{1,0:T(8,128)(2,1)}, u32[]{:S(2)}) copy-start(bf16[512,512]{1,0:T(8,128)(2,1)} %constant.88.clone.refs_10_) | copy-start | bytes 1572868
  61.4 11.1 %copy-start.1 = (bf16[256,512]{1,0:T(8,128)(2,1)S(1)}, bf16[256,512]{1,0:T(8,128)(2,1)}, u32[]{:S(2)}) copy-start(bf16[256,512]{1,0:T(8,128)(2,1)} %constant.89.clone.refs_11_) | copy-start | bytes 786436
  61.4 11.1 %collective-permute-start.8 = (bf16[256,256]{1,0:T(8,128)(2,1)S(1)}, bf16[256,256]{1,0:T(8,128)(2,1)S(1)}, u32[]{:S(2)}, u32[]{:S(2)}) collective-permute-start(bf16[256,256]{1,0:T(8,128)(2,1)S(1)} %get-tuple-element.50), channel_id=1, source_target_pairs={{0,2},{1,3},{2,0},{3,1},{4,6},{5,7},{6,4},{7,5},{8,10},{9,11},{10,... | collective-permute-start | bytes 393224 | tf_op jit(solution)/shard_map/ppermute | solution.py:93
  77.8 4.9 %collective-permute-start.11 = (bf16[256,256]{1,0:T(8,128)(2,1)S(1)}, bf16[256,256]{1,0:T(8,128)(2,1)S(1)}, u32[]{:S(2)}, u32[]{:S(2)}) collective-permute-start(bf16[256,256]{1,0:T(8,128)(2,1)S(1)} %get-tuple-element.36), channel_id=1, source_target_pairs={{0,1},{1,2},{2,3},{3,0},{4,5},{5,6},{6,7},{7,4},{8,9},{9,10},{10,1... | collective-permute-start | bytes 393224 | tf_op jit(solution)/shard_map/ppermute | solution.py:93
  78.0 12.6 %collective-permute-start.12 = (bf16[256,256]{1,0:T(8,128)(2,1)S(1)}, bf16[256,256]{1,0:T(8,128)(2,1)S(1)}, u32[]{:S(2)}, u32[]{:S(2)}) collective-permute-start(bf16[256,256]{1,0:T(8,128)(2,1)S(1)} %get-tuple-element.37), channel_id=1, source_target_pairs={{0,2},{1,3},{2,0},{3,1},{4,6},{5,7},{6,4},{7,5},{8,10},{9,11},{10,... | collective-permute-start | bytes 393224 | tf_op jit(solution)/shard_map/ppermute | solution.py:93
  82.1 11.2 %collective-permute-start.13 = (bf16[256,256]{1,0:T(8,128)(2,1)S(1)}, bf16[256,256]{1,0:T(8,128)(2,1)S(1)}, u32[]{:S(2)}, u32[]{:S(2)}) collective-permute-start(bf16[256,256]{1,0:T(8,128)(2,1)S(1)} %get-tuple-element.38), channel_id=1, source_target_pairs={{0,3},{1,0},{2,1},{3,2},{4,7},{5,4},{6,5},{7,6},{8,11},{9,8},{10,9... | collective-permute-start | bytes 393224 | tf_op jit(solution)/shard_map/ppermute | solution.py:93
  93.6 20.8 %collective-permute-start.15 = (bf16[256,1024]{0,1:T(8,128)(2,1)S(1)}, bf16[256,1024]{0,1:T(8,128)(2,1)}, u32[]{:S(2)}, u32[]{:S(2)}) collective-permute-start(bf16[256,1024]{0,1:T(8,128)(2,1)S(1)} %multiply_convert_fusion.1), channel_id=1, source_target_pairs={{0,8},{4,12},{8,0},{12,4},{1,9},{5,13},{9,1},{13,5},{2,10},{6,14},... | collective-permute-start | bytes 1572872 | tf_op jit(solution)/shard_map/ppermute | solution.py:97
  94.9 22.1 %collective-permute-start.14 = (bf16[256,1024]{0,1:T(8,128)(2,1)S(1)}, bf16[256,1024]{0,1:T(8,128)(2,1)}, u32[]{:S(2)}, u32[]{:S(2)}) collective-permute-start(bf16[256,1024]{0,1:T(8,128)(2,1)S(1)} %multiply_convert_fusion.1), channel_id=1, source_target_pairs={{0,4},{4,0},{8,12},{12,8},{1,5},{5,1},{9,13},{13,9},{2,6},{6,2},{1... | collective-permute-start | bytes 1572872 | tf_op jit(solution)/shard_map/ppermute | solution.py:97
  96.2 5.2 %collective-permute-start.17 = (bf16[256,256]{1,0:T(8,128)(2,1)S(1)}, bf16[256,256]{1,0:T(8,128)(2,1)S(1)}, u32[]{:S(2)}, u32[]{:S(2)}) collective-permute-start(bf16[256,256]{1,0:T(8,128)(2,1)S(1)} %get-tuple-element.44), channel_id=1, source_target_pairs={{0,1},{1,2},{2,3},{3,0},{4,5},{5,6},{6,7},{7,4},{8,9},{9,10},{10,1... | collective-permute-start | bytes 393224 | tf_op jit(solution)/shard_map/ppermute | solution.py:93
  98.6 9.8 %collective-permute-start.18 = (bf16[256,256]{1,0:T(8,128)(2,1)S(1)}, bf16[256,256]{1,0:T(8,128)(2,1)S(1)}, u32[]{:S(2)}, u32[]{:S(2)}) collective-permute-start(bf16[256,256]{1,0:T(8,128)(2,1)S(1)} %get-tuple-element.45), channel_id=1, source_target_pairs={{0,2},{1,3},{2,0},{3,1},{4,6},{5,7},{6,4},{7,5},{8,10},{9,11},{10,... | collective-permute-start | bytes 393224 | tf_op jit(solution)/shard_map/ppermute | solution.py:93
  99.8 10.8 %collective-permute-start.19 = (bf16[256,256]{1,0:T(8,128)(2,1)S(1)}, bf16[256,256]{1,0:T(8,128)(2,1)S(1)}, u32[]{:S(2)}, u32[]{:S(2)}) collective-permute-start(bf16[256,256]{1,0:T(8,128)(2,1)S(1)} %get-tuple-element.46), channel_id=1, source_target_pairs={{0,3},{1,0},{2,1},{3,2},{4,7},{5,4},{6,5},{7,6},{8,11},{9,8},{10,9... | collective-permute-start | bytes 393224 | tf_op jit(solution)/shard_map/ppermute | solution.py:93
  110.9 13.1 %collective-permute-start.21 = (bf16[256,1024]{0,1:T(8,128)(2,1)S(1)}, bf16[256,1024]{0,1:T(8,128)(2,1)S(1)}, u32[]{:S(2)}, u32[]{:S(2)}) collective-permute-start(bf16[256,1024]{0,1:T(8,128)(2,1)S(1)} %multiply_convert_fusion), channel_id=1, source_target_pairs={{0,8},{4,12},{8,0},{12,4},{1,9},{5,13},{9,1},{13,5},{2,10},{6,14},... | collective-permute-start | bytes 1572872 | tf_op jit(solution)/shard_map/ppermute | solution.py:97
  111.2 16.4 %collective-permute-start.20 = (bf16[256,1024]{0,1:T(8,128)(2,1)S(1)}, bf16[256,1024]{0,1:T(8,128)(2,1)S(1)}, u32[]{:S(2)}, u32[]{:S(2)}) collective-permute-start(bf16[256,1024]{0,1:T(8,128)(2,1)S(1)} %multiply_convert_fusion), channel_id=1, source_target_pairs={{0,4},{4,0},{8,12},{12,8},{1,5},{5,1},{9,13},{13,9},{2,6},{6,2},{1... | collective-permute-start | bytes 1572872 | tf_op jit(solution)/shard_map/ppermute | solution.py:97
  111.9 15.7 %slice-start = ((s8[8388608]{0:T(1024)(128)(4,1)}), s8[4194304]{0:T(1024)(128)(4,1)S(1)}, s32[]{:S(2)}) async-start(s8[8388608]{0:T(1024)(128)(4,1)} %bitcast.148), calls=%async_computation | async-start | bytes 8388608
  114.4 14.0 %collective-permute-start.16 = (bf16[256,1024]{0,1:T(8,128)(2,1)}, bf16[256,1024]{0,1:T(8,128)(2,1)S(1)}, u32[]{:S(2)}, u32[]{:S(2)}) collective-permute-start(bf16[256,1024]{0,1:T(8,128)(2,1)} %collective-permute-done.15), channel_id=1, source_target_pairs={{0,4},{4,0},{8,12},{12,8},{1,5},{5,1},{9,13},{13,9},{2,6},{6,2},{1... | collective-permute-start | bytes 1572872 | tf_op jit(solution)/shard_map/ppermute | solution.py:97
  117.0 10.7 %slice-start.1 = ((s8[8388608]{0:T(1024)(128)(4,1)}), s8[4194304]{0:T(1024)(128)(4,1)S(1)}, s32[]{:S(2)}) async-start(s8[8388608]{0:T(1024)(128)(4,1)} %bitcast.148), calls=%async_computation.1 | async-start | bytes 8388608
  124.0 5.2 %collective-permute-start.22 = (bf16[256,1024]{0,1:T(8,128)(2,1)S(1)}, bf16[256,1024]{0,1:T(8,128)(2,1)S(1)}, u32[]{:S(2)}, u32[]{:S(2)}) collective-permute-start(bf16[256,1024]{0,1:T(8,128)(2,1)S(1)} %collective-permute-done.21), channel_id=1, source_target_pairs={{0,4},{4,0},{8,12},{12,8},{1,5},{5,1},{9,13},{13,9},{2,6},{6,2},{1... | collective-permute-start | bytes 1572872 | tf_op jit(solution)/shard_map/ppermute | solution.py:97

commit v3 on v2

--- a/solution.py
+++ b/solution.py
@@ -72,6 +72,64 @@
             out_refs[s * per + t][...] = (conv + skip_ref[...] * held).astype(jnp.bfloat16)
 
 
+def project_kernel(mats, ops, mode, *refs):
+    refs = refs[1:]
+    pieces, weights = refs[:ops], refs[ops : ops + ops * mats]
+    outs = refs[ops + ops * mats :]
+    sums = []
+    for m in range(mats):
+        total = outs[m][0] if mode != "near" else None
+        for p in range(ops):
+            term = jnp.dot(pieces[p][...], weights[m * ops + p][0], preferred_element_type=jnp.float32)
+            total = term if total is None else total + term
+        sums.append(total)
+    if mode == "near":
+        for m in range(mats):
+            outs[m][0] = sums[m]
+
+        @pl.when(pl.program_id(0) == 0)
+        def _():
+            outs[mats][...] = pieces[0][BLOCK:]
+    elif mode == "mix":
+        outs[mats][0] = (sums[0] * sums[1]).astype(jnp.bfloat16)
+    else:
+        outs[mats][0] = sums[0].astype(jnp.bfloat16)
+
+
+def project(mode, where, pieces, distances, weight, mats, near, t, n):
+    rows, width = pieces[0].shape
+    channels = weight.shape[2]
+    cc = channels // n
+
+    def weight_spec(mat, far):
+        return pl.BlockSpec((1, width, cc), lambda s, at: (mat, at[1] ^ far, lax.rem(at[0] + s, n)))
+
+    specs = [pl.BlockSpec((rows, width), lambda s, at: (0, 0))] * len(pieces)
+    specs += [weight_spec(mat, far) for mat in mats for far in distances]
+    specs += [pl.BlockSpec((1, rows, cc), lambda s, at: (s, t, 0))] * len(near)
+    out_spec = pl.BlockSpec((1, rows, cc), lambda s, at: (s, 0, 0))
+    if mode == "near":
+        shapes = [jax.ShapeDtypeStruct((n, rows, cc), jnp.float32)] * len(mats)
+        later = jax.ShapeDtypeStruct((rows - BLOCK, width), jnp.bfloat16)
+    else:
+        shapes = [jax.ShapeDtypeStruct((n, rows, cc), jnp.bfloat16)]
+        later = None
+    out_specs = [out_spec] * len(shapes)
+    if later is not None:
+        shapes.append(later)
+        out_specs.append(pl.BlockSpec(later.shape, lambda s, at: (0, 0)))
+    flops = 2 * rows * width * channels * len(pieces) * len(mats)
+    return pl.pallas_call(
+        functools.partial(project_kernel, len(mats), len(pieces), mode),
+        out_shape=shapes,
+        grid_spec=pltpu.PrefetchScalarGridSpec(
+            num_scalar_prefetch=1, grid=(n,), in_specs=specs, out_specs=out_specs
+        ),
+        compiler_params=pltpu.CompilerParams(vmem_limit_bytes=36 * 1024 * 1024),
+        cost_estimate=pl.CostEstimate(flops=flops, bytes_accessed=flops // rows, transcendentals=0),
+    )(where, *pieces, *([weight] * (len(mats) * len(distances))), *near)
+
+
 def convolve(n, per, x, taps, skip):
     cc = taps.shape[1]
     forward, inverse = tables(BLOCK)
@@ -110,7 +168,6 @@
     n_ctx, n_chan = lax.axis_size("ctx"), lax.axis_size("chan")
     ctx, chan = lax.axis_index("ctx"), lax.axis_index("chan")
     rows, channels = features.shape[0], in_weight.shape[2]
-    width = features.shape[1]
     cc = channels // n_ctx
     per = rows // BLOCK
     paired = n_chan == 4
@@ -118,41 +175,36 @@
     skip = lax.dynamic_slice_in_dim(skip_gain, ctx * cc, cc, 0)[None, :]
     parts = range(per)
 
-    def into(piece, owner, s):
-        weight = lax.dynamic_slice(in_weight, (owner * width, s, 0), (width, 1, channels))[:, 0]
-        return jnp.dot(piece, weight, preferred_element_type=f32)
-
     def chunk(x, t):
         return x[t * BLOCK : (t + 1) * BLOCK]
 
-    if paired:
-        across, last = [], None
+    got, query = [], []
+    if paired and cc % 128 == 0:
+        where = jnp.stack([ctx, chan]).astype(jnp.int32)
+        weight = jnp.transpose(in_weight, (1, 0, 2))
+        first = flip(chunk(features, 0), n_chan, 2)
+        beside = flip(features, n_chan, 1)
+        *near, later = project("near", where, [features, beside], (0, 1), weight, (1, 2, 0), [], 0, n_ctx)
+        across = [first]
+        for t in parts[1:]:
+            across.append(flip(after(chunk(later, t - 1), across[-1]), n_chan, 2))
+        far = [[across[t], flip(across[t], n_chan, 1)] for t in parts]
         for t in parts:
-            sent = chunk(features, t)
-            across.append(flip(sent if last is None else after(sent, last), n_chan, 2))
-            last = across[-1]
-        beside = flip(features, n_chan, 1)
-        near = [into(features, chan, s) + into(beside, chan ^ 1, s) for s in range(3)]
-        far = [[(chan ^ 2, across[t]), (chan ^ 3, flip(across[t], n_chan, 1))] for t in parts]
+            mixed = project("mix", where, far[t], (2, 3), weight, (1, 2), near[:2], t, n_ctx)[0]
+            got.append(exchange([mixed[s] for s in range(n_ctx)], n_ctx))
+        held = got[-1][0]
+        for t in parts:
+            pieces = lax.optimization_barrier((*far[t], held))[:2]
+            query.append(project("query", where, pieces, (2, 3), weight, (0,), near[2:], t, n_ctx)[0])
     else:
         whole = lax.all_gather(features, "chan", axis=1, tiled=True)
-        near = [into(whole[:, :width], 0, s) for s in range(3)]
-        far = [[(j, chunk(whole, t)[:, j * width : (j + 1) * width]) for j in range(1, n_chan)] for t in parts]
-
-    def project(t, s):
-        total = chunk(near[s], t)
-        for owner, piece in far[t]:
-            total = total + into(piece, owner, s)
-        return total
-
-    got = []
-    for t in parts:
-        mixed = (project(t, 1) * project(t, 2)).astype(jnp.bfloat16)
-        sends = [
-            lax.dynamic_slice_in_dim(mixed, ((ctx + s) % n_ctx) * cc, cc, 1) for s in range(n_ctx)
-        ]
-        got.append(exchange(sends, n_ctx))
-    query = [project(t, 0).astype(jnp.bfloat16) for t in parts]
+        turned = [jnp.roll(in_weight[:, s], -ctx * cc, axis=1) for s in range(3)]
+        for t in parts:
+            q, k, v = [jnp.dot(chunk(whole, t), w, preferred_element_type=f32) for w in turned]
+            mixed = (k * v).astype(jnp.bfloat16)
+            got.append(exchange([mixed[:, s * cc : (s + 1) * cc] for s in range(n_ctx)], n_ctx))
+            q = q.astype(jnp.bfloat16)
+            query.append(jnp.stack([q[:, s * cc : (s + 1) * cc] for s in range(n_ctx)]))
     x = [got[t][s] for s in range(n_ctx) for t in parts]
     x = lax.optimization_barrier((*x, *query))[: len(x)]
     y = convolve(n_ctx, per, x, taps, skip)
@@ -163,10 +215,11 @@
         if last is not None:
             sends = lax.optimization_barrier((*sends, *last))[:n_ctx]
         back = last = exchange(sends, n_ctx)
-        summed = jnp.zeros((BLOCK, channels), jnp.bfloat16)
+        gated = jnp.zeros((BLOCK, channels), jnp.bfloat16)
         for s in range(n_ctx):
-            summed = lax.dynamic_update_slice(summed, back[s], (0, ((ctx - s + n_ctx) % n_ctx) * cc))
-        gated = (query[t].astype(f32) * summed.astype(f32)).astype(jnp.bfloat16)
+            piece = query[t][(n_ctx - s) % n_ctx].astype(f32) * back[s].astype(f32)
+            start = ((ctx - s + n_ctx) % n_ctx) * cc
+            gated = lax.dynamic_update_slice(gated, piece.astype(jnp.bfloat16), (0, start))
         if paired:
             far_side = flip(gated, n_chan, 2)
             pieces = [(chan, gated), (chan ^ 1, flip(gated, n_chan, 1))]

time: 132 us -> 129 us (0.977)
  matrix products: 65.5 us -> 6.05 us
  Pallas kernels: 5.3 us -> 37.9 us
  waiting for transfers between devices: 31.2 us -> 45.4 us
  local copies, waits for them, and re-layouts: 4.51 us -> 13.6 us
  starting transfers between devices: 22.6 us -> 24 us
    dot_general x18 -> x0, matrix products: 51 us -> none  [into(): return jnp.dot(piece, weight, preferred_element_type=f32)]
    pallas_call x0 -> x5, Pallas kernels: none -> 32.6 us  [project(): pl.pallas_call(functools.partial(project_kernel, len(mats), len(pieces),...]
    ppermute x11, waiting for transfers between devices: 4.34 us -> 22.2 us  [flip(): return lax.ppermute(x, 'chan', [(i, i ^ bit) for i in range(n)])]
    unnamed x16 -> x24, local copies, waits for them, and re-layouts: 0.04 us -> 9.32 us
    dot_general x8, matrix products: 14.5 us -> 6.05 us  [shards(): term = jnp.dot(piece, weight, preferred_element_type=f32)]
    ppermute x12, waiting for transfers between devices: 26.9 us -> 23.2 us  [shift(): return lax.ppermute(x, axis, [(i, (i + by) % n) for i in range(n)])]
  transfers between devices with their start and end apart: 23 -> 23, of which waited for: 8 -> 9; matrix products, arithmetic and copies ran while one was open for 53% -> 8% of each run, Pallas kernels for 0% -> 25%
where the time goes in v3:
time: 129 us
  waiting for transfers between devices  45.4 us (35%)
  Pallas kernels  37.9 us (29%)
  starting transfers between devices  24 us (19%)
  local copies, waits for them, and re-layouts  13.6 us (11%)
  matrix products  6.05 us (5%)
  other arithmetic  1.4 us (1%)
    pallas_call x5, Pallas kernels, project(): pl.pallas_call(functools.partial(project_kernel, len(mats), len(pieces),...  32.6 us
    ppermute x12, waiting for transfers between devices, shift(): return lax.ppermute(x, axis, [(i, (i + by) % n) for i in range(n)])  23.2 us
    ppermute x11, waiting for transfers between devices, flip(): return lax.ppermute(x, 'chan', [(i, i ^ bit) for i in range(n)])  22.2 us
    ppermute x12, starting transfers between devices, shift(): return lax.ppermute(x, axis, [(i, (i + by) % n) for i in range(n)])  14.4 us
    ppermute x11, starting transfers between devices, flip(): return lax.ppermute(x, 'chan', [(i, i ^ bit) for i in range(n)])  9.68 us
    unnamed x24, local copies, waits for them, and re-layouts  9.32 us
    dot_general x8, matrix products, shards(): term = jnp.dot(piece, weight, preferred_element_type=f32)  6.05 us
    pallas_call x1, Pallas kernels, convolve(): pl.pallas_call(functools.partial(conv_kernel, n, per), out_shape=[jax.Sha...  5.26 us
  transfers between devices with their start and end apart: 23, of which 9 were waited for; matrix products, arithmetic and copies ran while one was open for 8% of the time, Pallas kernels for 25%

profile of v3, /device:TPU:11, one launch (start us, length us, event | category | flops | bytes accessed | tf_op | source)
XLA Modules:
  0.0 128.7 jit_solution(3934338061459960190)
XLA Ops:
  0.7 1.1 slice.51
  1.8 1.3 %collective-permute-start = (bf16[256,1024]{1,0:T(8,128)(2,1)S(1)}, bf16[256,1024]{1,0:T(8,128)(2,1)S(1)}, u32[]{:S(2)}, u32[]{:S(2)}) collective-permute-start(bf16[256,1024]{1,0:T(8,128)(2,1)S(1)} %slice.51), channel_id=1, source_target_pairs={{0,8},{4,12},{8,0},{12,4},{1,9},{5,13},{9,1},{13,5},{2,10},{6,14},... | collective-permute-start | bytes 1572872 | tf_op jit(solution)/shard_map/ppermute | solution.py:155
  3.2 1.0 copy-done.5
  4.1 1.2 copy-done.4
  5.4 1.2 copy-done.6
  6.6 10.7 %shard_map.73 = (f32[4,512,256]{2,1,0:T(8,128)S(1)}, f32[4,512,256]{2,1,0:T(8,128)S(1)}, f32[4,512,256]{2,1,0:T(8,128)S(1)}, bf16[256,1024]{1,0:T(8,128)(2,1)}) custom-call(s32[2]{0:T(128)S(1)} %pad_add_fusion.refs_0_, bf16[512,1024]{1,0:T(8,128)(2,1)S(1)} %copy-done.4, bf16[512,1024]{1,0:T(8,128)(2,1)S(1)} %copy-done.6, bf16[3,4096,1024]{2,1,0:T(8,128)(2,1)} %bitcast.69, ...), custom_call_target="tpu_custom_call" | custom-call | flops 6442450944 | bytes 12582912 | tf_op jit(solution)/shard_map/pallas_call | solution.py:122
  17.3 1.4 %copy-done = f32[4,512,256]{2,1,0:T(8,128)} copy-done((f32[4,512,256]{2,1,0:T(8,128)}, f32[4,512,256]{2,1,0:T(8,128)S(1)}, u32[]{:S(2)}) %copy-start) | copy-done | bytes 2097176
  18.7 1.3 %copy-done.2 = f32[4,512,256]{2,1,0:T(8,128)} copy-done((f32[4,512,256]{2,1,0:T(8,128)}, f32[4,512,256]{2,1,0:T(8,128)S(1)}, u32[]{:S(2)}) %copy-start.2) | copy-done | bytes 2097176
  20.0 1.2 collective-permute-start.3
  21.9 11.6 %collective-permute-done.3.refs_1_ = bf16[256,1024]{1,0:T(8,128)(2,1)} collective-permute-done((bf16[256,1024]{1,0:T(8,128)(2,1)}, bf16[256,1024]{1,0:T(8,128)(2,1)}, u32[]{:S(2)}, u32[]{:S(2)}) %collective-permute-start.3) | collective-permute-done | bytes 524320 | tf_op jit(solution)/shard_map/ppermute | solution.py:155
  33.5 1.2 collective-permute-start.4
  34.7 2.3 %constant_dynamic-slice_fusion.refs_8_ = bf16[2048,256]{1,0:T(8,128)(2,1)} fusion(bf16[2048,1024]{1,0:T(8,128)(2,1)} %param.8, s32[]{:T(128)S(6)} %select_n.63), kind=kLoop, calls=%fused_computation.73 | loop fusion | bytes 2097156 | tf_op jit(solution)/shard_map/dynamic_slice | solution.py:174
  36.9 0.8 dynamic_slice.23
  37.7 1.6 %copy-done.1 = f32[4,512,256]{2,1,0:T(8,128)S(1)} copy-done((f32[4,512,256]{2,1,0:T(8,128)S(1)}, f32[4,512,256]{2,1,0:T(8,128)}, u32[]{:S(2)}) %copy-start.1) | copy-done | bytes 2097176
  39.3 1.6 %copy-done.3 = f32[4,512,256]{2,1,0:T(8,128)S(1)} copy-done((f32[4,512,256]{2,1,0:T(8,128)S(1)}, f32[4,512,256]{2,1,0:T(8,128)}, u32[]{:S(2)}) %copy-start.3) | copy-done | bytes 2097176
  40.9 6.1 %shard_map.76 = bf16[4,256,256]{2,1,0:T(8,128)(2,1)S(1)} custom-call(s32[2]{0:T(128)S(1)} %pad_add_fusion.refs_0_, bf16[256,1024]{1,0:T(8,128)(2,1)S(1)} %collective-permute-done.refs_1_, bf16[256,1024]{1,0:T(8,128)(2,1)S(1)} %collective-permute-done.1.refs_2_, bf16[3,4096,1024]{2,1,0:T(8,128)(2,1)} %bitcast.75, bf16[3,4096,1024]{2,1,0:T(8,128)(2,1)} %bitcast.76, ...), custom_call_target="tpu_custom_call" | custom-call | flops 2147483648 | bytes 8388608 | tf_op jit(solution)/shard_map/pallas_call | solution.py:122
  47.0 1.3 %collective-permute-start.5 = (bf16[256,256]{1,0:T(8,128)(2,1)S(1)}, bf16[256,256]{1,0:T(8,128)(2,1)S(1)}, u32[]{:S(2)}, u32[]{:S(2)}) collective-permute-start(bf16[256,256]{1,0:T(8,128)(2,1)S(1)} %get-tuple-element.69), channel_id=1, source_target_pairs={{0,1},{1,2},{2,3},{3,0},{4,5},{5,6},{6,7},{7,4},{8,9},{9,10},{10,1... | collective-permute-start | bytes 393224 | tf_op jit(solution)/shard_map/ppermute | solution.py:151
  48.3 1.1 collective-permute-start.7
  49.4 1.4 %collective-permute-start.9 = (bf16[256,256]{1,0:T(8,128)(2,1)S(1)}, bf16[256,256]{1,0:T(8,128)(2,1)S(1)}, u32[]{:S(2)}, u32[]{:S(2)}) collective-permute-start(bf16[256,256]{1,0:T(8,128)(2,1)S(1)} %get-tuple-element.67), channel_id=1, source_target_pairs={{0,3},{1,0},{2,1},{3,2},{4,7},{5,4},{6,5},{7,6},{8,11},{9,8},{10,9... | collective-permute-start | bytes 393224 | tf_op jit(solution)/shard_map/ppermute | solution.py:151
  50.8 6.6 %shard_map.74 = bf16[4,256,256]{2,1,0:T(8,128)(2,1)S(1)} custom-call(s32[2]{0:T(128)S(1)} %pad_add_fusion.refs_0_, bf16[256,1024]{1,0:T(8,128)(2,1)} %collective-permute-done.3.refs_1_, bf16[256,1024]{1,0:T(8,128)(2,1)} %collective-permute-done.4.refs_2_, bf16[3,4096,1024]{2,1,0:T(8,128)(2,1)} %bitcast.79, bf16[3,4096,1024]{2,1,0:T(8,128)(2,1)} %bitcast.80, ...), custom_call_target="tpu_custom_call" | custom-call | flops 2147483648 | bytes 8388608 | tf_op jit(solution)/shard_map/pallas_call | solution.py:122
  57.4 1.1 collective-permute-start.10
  59.0 1.9 %collective-permute-start.8 = (bf16[256,256]{1,0:T(8,128)(2,1)S(1)}, bf16[256,256]{1,0:T(8,128)(2,1)S(1)}, u32[]{:S(2)}, u32[]{:S(2)}) collective-permute-start(bf16[256,256]{1,0:T(8,128)(2,1)S(1)} %get-tuple-element.64), channel_id=1, source_target_pairs={{0,2},{1,3},{2,0},{3,1},{4,6},{5,7},{6,4},{7,5},{8,10},{9,11},{10,... | collective-permute-start | bytes 393224 | tf_op jit(solution)/shard_map/ppermute | solution.py:151
  60.8 4.8 %shard_map.77 = bf16[4,256,256]{2,1,0:T(8,128)(2,1)S(1)} custom-call(s32[2]{0:T(128)S(1)} %pad_add_fusion.refs_0_, bf16[256,1024]{1,0:T(8,128)(2,1)} %collective-permute-done.3.refs_1_, bf16[256,1024]{1,0:T(8,128)(2,1)} %collective-permute-done.4.refs_2_, bf16[3,4096,1024]{2,1,0:T(8,128)(2,1)} %bitcast.83, bf16[3,4096,1024]{2,1,0:T(8,128)(2,1)} %bitcast.84, ...), custom_call_target="tpu_custom_call" | custom-call | flops 1073741824 | bytes 4194304 | tf_op jit(solution)/shard_map/pallas_call | solution.py:122
  65.7 4.5 %shard_map.75 = bf16[4,256,256]{2,1,0:T(8,128)(2,1)S(1)} custom-call(s32[2]{0:T(128)S(1)} %pad_add_fusion.refs_0_, bf16[256,1024]{1,0:T(8,128)(2,1)S(1)} %collective-permute-done.refs_1_, bf16[256,1024]{1,0:T(8,128)(2,1)S(1)} %collective-permute-done.1.refs_2_, bf16[3,4096,1024]{2,1,0:T(8,128)(2,1)} %bitcast.85, bf16[3,4096,1024]{2,1,0:T(8,128)(2,1)} %bitcast.86, ...), custom_call_target="tpu_custom_call" | custom-call | flops 1073741824 | bytes 4194304 | tf_op jit(solution)/shard_map/pallas_call | solution.py:122
  70.2 0.8 collective-permute-done.8.refs_5_
  71.0 5.3 %shard_map.78 = (bf16[256,256]{1,0:T(8,128)(2,1)S(1)}, bf16[256,256]{1,0:T(8,128)(2,1)S(1)}, bf16[256,256]{1,0:T(8,128)(2,1)S(1)}, bf16[256,256]{1,0:T(8,128)(2,...) custom-call(bf16[256,256]{1,0:T(8,128)(2,1)S(1)} %get-tuple-element., ...), custom_call_target="tpu_custom_call" | custom-call | flops 6000000000 | bytes 4000000 | tf_op jit(solution)/shard_map/pallas_call | solution.py:139
  76.3 1.3 %collective-permute-start.11 = (bf16[256,256]{1,0:T(8,128)(2,1)S(1)}, bf16[256,256]{1,0:T(8,128)(2,1)S(1)}, u32[]{:S(2)}, u32[]{:S(2)}) collective-permute-start(bf16[256,256]{1,0:T(8,128)(2,1)S(1)} %get-tuple-element.52), channel_id=1, source_target_pairs={{0,1},{1,2},{2,3},{3,0},{4,5},{5,6},{6,7},{7,4},{8,9},{9,10},{10,1... | collective-permute-start | bytes 393224 | tf_op jit(solution)/shard_map/ppermute | solution.py:151
  77.6 4.0 %collective-permute-start.12 = (bf16[256,256]{1,0:T(8,128)(2,1)S(1)}, bf16[256,256]{1,0:T(8,128)(2,1)S(1)}, u32[]{:S(2)}, u32[]{:S(2)}) collective-permute-start(bf16[256,256]{1,0:T(8,128)(2,1)S(1)} %get-tuple-element.53), channel_id=1, source_target_pairs={{0,2},{1,3},{2,0},{3,1},{4,6},{5,7},{6,4},{7,5},{8,10},{9,11},{10,... | collective-permute-start | bytes 393224 | tf_op jit(solution)/shard_map/ppermute | solution.py:151
  81.7 1.3 collective-permute-done.11
  83.0 6.8 %collective-permute-done.12 = bf16[256,256]{1,0:T(8,128)(2,1)S(1)} collective-permute-done((bf16[256,256]{1,0:T(8,128)(2,1)S(1)}, bf16[256,256]{1,0:T(8,128)(2,1)S(1)}, u32[]{:S(2)}, u32[]{:S(2)}) %collective-permute-start.12) | collective-permute-done | bytes 131104 | tf_op jit(solution)/shard_map/ppermute | solution.py:151
  89.9 2.5 %collective-permute-done.13 = bf16[256,256]{1,0:T(8,128)(2,1)S(1)} collective-permute-done((bf16[256,256]{1,0:T(8,128)(2,1)S(1)}, bf16[256,256]{1,0:T(8,128)(2,1)S(1)}, u32[]{:S(2)}, u32[]{:S(2)}) %collective-permute-start.13) | collective-permute-done | bytes 131104 | tf_op jit(solution)/shard_map/ppermute | solution.py:151
  92.4 1.4 %collective-permute-start.14 = (bf16[256,1024]{1,0:T(8,128)(2,1)S(1)}, bf16[256,1024]{1,0:T(8,128)(2,1)S(1)}, u32[]{:S(2)}, u32[]{:S(2)}) collective-permute-start(bf16[256,1024]{1,0:T(8,128)(2,1)S(1)} %fusion.51), channel_id=1, source_target_pairs={{0,4},{4,0},{8,12},{12,8},{1,5},{5,1},{9,13},{13,9},{2,6},{6,2},{1... | collective-permute-start | bytes 1572872 | tf_op jit(solution)/shard_map/ppermute | solution.py:155
  93.8 1.3 collective-permute-start.15
  95.1 1.4 %collective-permute-start.18 = (bf16[256,256]{1,0:T(8,128)(2,1)S(1)}, bf16[256,256]{1,0:T(8,128)(2,1)S(1)}, u32[]{:S(2)}, u32[]{:S(2)}) collective-permute-start(bf16[256,256]{1,0:T(8,128)(2,1)S(1)} %get-tuple-element.61), channel_id=1, source_target_pairs={{0,2},{1,3},{2,0},{3,1},{4,6},{5,7},{6,4},{7,5},{8,10},{9,11},{10,... | collective-permute-start | bytes 393224 | tf_op jit(solution)/shard_map/ppermute | solution.py:151
  97.0 2.8 %collective-permute-done.17 = bf16[256,256]{1,0:T(8,128)(2,1)S(1)} collective-permute-done((bf16[256,256]{1,0:T(8,128)(2,1)S(1)}, bf16[256,256]{1,0:T(8,128)(2,1)S(1)}, u32[]{:S(2)}, u32[]{:S(2)}) %collective-permute-start.17) | collective-permute-done | bytes 131104 | tf_op jit(solution)/shard_map/ppermute | solution.py:151
  99.8 6.5 %collective-permute-done.18 = bf16[256,256]{1,0:T(8,128)(2,1)S(1)} collective-permute-done((bf16[256,256]{1,0:T(8,128)(2,1)S(1)}, bf16[256,256]{1,0:T(8,128)(2,1)S(1)}, u32[]{:S(2)}, u32[]{:S(2)}) %collective-permute-start.18) | collective-permute-done | bytes 131104 | tf_op jit(solution)/shard_map/ppermute | solution.py:151
  106.4 2.5 %collective-permute-done.19 = bf16[256,256]{1,0:T(8,128)(2,1)S(1)} collective-permute-done((bf16[256,256]{1,0:T(8,128)(2,1)S(1)}, bf16[256,256]{1,0:T(8,128)(2,1)S(1)}, u32[]{:S(2)}, u32[]{:S(2)}) %collective-permute-start.19) | collective-permute-done | bytes 131104 | tf_op jit(solution)/shard_map/ppermute | solution.py:151
  110.0 0.7 fusion.6
  110.8 0.7 fusion.10
  111.5 0.8 fusion.19
  112.3 10.6 %collective-permute-done.21 = bf16[256,1024]{1,0:T(8,128)(2,1)S(1)} collective-permute-done((bf16[256,1024]{1,0:T(8,128)(2,1)S(1)}, bf16[256,1024]{1,0:T(8,128)(2,1)S(1)}, u32[]{:S(2)}, u32[]{:S(2)}) %collective-permute-start.21) | collective-permute-done | bytes 524320 | tf_op jit(solution)/shard_map/ppermute | solution.py:155
  122.9 0.8 collective-permute-start.22
  123.8 0.7 fusion.4
  124.5 0.7 fusion.8
  125.3 0.8 fusion.25
  126.1 0.8 fusion.37
  126.9 0.8 fusion.34
  127.6 1.0 pad_maximum_fusion
  (54 shorter events, 3.9 us)
Async XLA Ops:
  0.0 3.2 %collective-permute-start.2 = (bf16[512,1024]{1,0:T(8,128)(2,1)}, bf16[512,1024]{1,0:T(8,128)(2,1)S(1)}, u32[]{:S(2)}, u32[]{:S(2)}) collective-permute-start(bf16[512,1024]{1,0:T(8,128)(2,1)} %refs_1_.1), channel_id=1, source_target_pairs={{0,4},{4,0},{8,12},{12,8},{1,5},{5,1},{9,13},{13,9},{2,6},{6,2},{1... | collective-permute-start | bytes 3145736 | tf_op jit(solution)/shard_map/ppermute | solution.py:155
  1.8 18.3 %collective-permute-start = (bf16[256,1024]{1,0:T(8,128)(2,1)S(1)}, bf16[256,1024]{1,0:T(8,128)(2,1)S(1)}, u32[]{:S(2)}, u32[]{:S(2)}) collective-permute-start(bf16[256,1024]{1,0:T(8,128)(2,1)S(1)} %slice.51), channel_id=1, source_target_pairs={{0,8},{4,12},{8,0},{12,4},{1,9},{5,13},{9,1},{13,5},{2,10},{6,14},... | collective-permute-start | bytes 1572872 | tf_op jit(solution)/shard_map/ppermute | solution.py:155
  3.2 1.0 copy-start.5
  4.1 1.2 copy-start.4
  5.4 1.2 copy-start.6
  17.3 1.4 %copy-start = (f32[4,512,256]{2,1,0:T(8,128)}, f32[4,512,256]{2,1,0:T(8,128)S(1)}, u32[]{:S(2)}) copy-start(f32[4,512,256]{2,1,0:T(8,128)S(1)} %get-tuple-element.36.refs_7_) | copy-start | bytes 6291460
  18.7 1.3 %copy-start.2 = (f32[4,512,256]{2,1,0:T(8,128)}, f32[4,512,256]{2,1,0:T(8,128)S(1)}, u32[]{:S(2)}) copy-start(f32[4,512,256]{2,1,0:T(8,128)S(1)} %get-tuple-element.37.refs_8_) | copy-start | bytes 6291460
  20.0 13.5 %collective-permute-start.3 = (bf16[256,1024]{1,0:T(8,128)(2,1)}, bf16[256,1024]{1,0:T(8,128)(2,1)}, u32[]{:S(2)}, u32[]{:S(2)}) collective-permute-start(bf16[256,1024]{1,0:T(8,128)(2,1)} %get-tuple-element.35), channel_id=1, source_target_pairs={{0,8},{4,12},{8,0},{12,4},{1,9},{5,13},{9,1},{13,5},{2,10},{6,14},... | collective-permute-start | bytes 1572872 | tf_op jit(solution)/shard_map/ppermute | solution.py:155
  21.3 16.4 %collective-permute-start.1 = (bf16[256,1024]{1,0:T(8,128)(2,1)S(1)}, bf16[256,1024]{1,0:T(8,128)(2,1)S(1)}, u32[]{:S(2)}, u32[]{:S(2)}) collective-permute-start(bf16[256,1024]{1,0:T(8,128)(2,1)S(1)} %collective-permute-done.refs_1_), channel_id=1, source_target_pairs={{0,4},{4,0},{8,12},{12,8},{1,5},{5,1},{9,13},{13,9},{2,6},{6,2},{1... | collective-permute-start | bytes 1572872 | tf_op jit(solution)/shard_map/ppermute | solution.py:155
  33.5 17.3 %collective-permute-start.4 = (bf16[256,1024]{1,0:T(8,128)(2,1)}, bf16[256,1024]{1,0:T(8,128)(2,1)}, u32[]{:S(2)}, u32[]{:S(2)}) collective-permute-start(bf16[256,1024]{1,0:T(8,128)(2,1)} %collective-permute-done.3.refs_1_), channel_id=1, source_target_pairs={{0,4},{4,0},{8,12},{12,8},{1,5},{5,1},{9,13},{13,9},{2,6},{6,2},{1... | collective-permute-start | bytes 1572872 | tf_op jit(solution)/shard_map/ppermute | solution.py:155
  37.7 1.6 %copy-start.1 = (f32[4,512,256]{2,1,0:T(8,128)S(1)}, f32[4,512,256]{2,1,0:T(8,128)}, u32[]{:S(2)}) copy-start(f32[4,512,256]{2,1,0:T(8,128)} %copy-done) | copy-start | bytes 6291460
  39.3 1.6 %copy-start.3 = (f32[4,512,256]{2,1,0:T(8,128)S(1)}, f32[4,512,256]{2,1,0:T(8,128)}, u32[]{:S(2)}) copy-start(f32[4,512,256]{2,1,0:T(8,128)} %copy-done.2) | copy-start | bytes 6291460
  47.0 12.0 %collective-permute-start.5 = (bf16[256,256]{1,0:T(8,128)(2,1)S(1)}, bf16[256,256]{1,0:T(8,128)(2,1)S(1)}, u32[]{:S(2)}, u32[]{:S(2)}) collective-permute-start(bf16[256,256]{1,0:T(8,128)(2,1)S(1)} %get-tuple-element.69), channel_id=1, source_target_pairs={{0,1},{1,2},{2,3},{3,0},{4,5},{5,6},{6,7},{7,4},{8,9},{9,10},{10,1... | collective-permute-start | bytes 393224 | tf_op jit(solution)/shard_map/ppermute | solution.py:151
  48.3 21.8 %collective-permute-start.7 = (bf16[256,256]{1,0:T(8,128)(2,1)S(1)}, bf16[256,256]{1,0:T(8,128)(2,1)S(1)}, u32[]{:S(2)}, u32[]{:S(2)}) collective-permute-start(bf16[256,256]{1,0:T(8,128)(2,1)S(1)} %get-tuple-element.68), channel_id=1, source_target_pairs={{0,2},{1,3},{2,0},{3,1},{4,6},{5,7},{6,4},{7,5},{8,10},{9,11},{10,... | collective-permute-start | bytes 393224 | tf_op jit(solution)/shard_map/ppermute | solution.py:151
  49.4 20.7 %collective-permute-start.9 = (bf16[256,256]{1,0:T(8,128)(2,1)S(1)}, bf16[256,256]{1,0:T(8,128)(2,1)S(1)}, u32[]{:S(2)}, u32[]{:S(2)}) collective-permute-start(bf16[256,256]{1,0:T(8,128)(2,1)S(1)} %get-tuple-element.67), channel_id=1, source_target_pairs={{0,3},{1,0},{2,1},{3,2},{4,7},{5,4},{6,5},{7,6},{8,11},{9,8},{10,9... | collective-permute-start | bytes 393224 | tf_op jit(solution)/shard_map/ppermute | solution.py:151
  57.4 12.8 %collective-permute-start.10 = (bf16[256,256]{1,0:T(8,128)(2,1)S(1)}, bf16[256,256]{1,0:T(8,128)(2,1)S(1)}, u32[]{:S(2)}, u32[]{:S(2)}) collective-permute-start(bf16[256,256]{1,0:T(8,128)(2,1)S(1)} %get-tuple-element.63), channel_id=1, source_target_pairs={{0,3},{1,0},{2,1},{3,2},{4,7},{5,4},{6,5},{7,6},{8,11},{9,8},{10,9... | collective-permute-start | bytes 393224 | tf_op jit(solution)/shard_map/ppermute | solution.py:151
  58.6 11.6 %collective-permute-start.6 = (bf16[256,256]{1,0:T(8,128)(2,1)S(1)}, bf16[256,256]{1,0:T(8,128)(2,1)S(1)}, u32[]{:S(2)}, u32[]{:S(2)}) collective-permute-start(bf16[256,256]{1,0:T(8,128)(2,1)S(1)} %get-tuple-element.65), channel_id=1, source_target_pairs={{0,1},{1,2},{2,3},{3,0},{4,5},{5,6},{6,7},{7,4},{8,9},{9,10},{10,1... | collective-permute-start | bytes 393224 | tf_op jit(solution)/shard_map/ppermute | solution.py:151
  59.0 12.0 %collective-permute-start.8 = (bf16[256,256]{1,0:T(8,128)(2,1)S(1)}, bf16[256,256]{1,0:T(8,128)(2,1)S(1)}, u32[]{:S(2)}, u32[]{:S(2)}) collective-permute-start(bf16[256,256]{1,0:T(8,128)(2,1)S(1)} %get-tuple-element.64), channel_id=1, source_target_pairs={{0,2},{1,3},{2,0},{3,1},{4,6},{5,7},{6,4},{7,5},{8,10},{9,11},{10,... | collective-permute-start | bytes 393224 | tf_op jit(solution)/shard_map/ppermute | solution.py:151
  65.6 5.4 %copy-start.7 = (bf16[2048,256]{1,0:T(8,128)(2,1)S(1)}, bf16[2048,256]{1,0:T(8,128)(2,1)}, u32[]{:S(2)}) copy-start(bf16[2048,256]{1,0:T(8,128)(2,1)} %constant_dynamic-slice_fusion.refs_8_) | copy-start | bytes 3145732
  65.6 5.3 %copy-start.8 = (bf16[512,512]{1,0:T(8,128)(2,1)S(1)}, bf16[512,512]{1,0:T(8,128)(2,1)}, u32[]{:S(2)}) copy-start(bf16[512,512]{1,0:T(8,128)(2,1)} %constant.64.clone.refs_10_) | copy-start | bytes 1572868
  65.6 5.3 %copy-start.9 = (bf16[256,512]{1,0:T(8,128)(2,1)S(1)}, bf16[256,512]{1,0:T(8,128)(2,1)}, u32[]{:S(2)}) copy-start(bf16[256,512]{1,0:T(8,128)(2,1)} %constant.65.clone.refs_11_) | copy-start | bytes 786436
  71.0 39.1 %slice-start = ((s8[8388608]{0:T(1024)(128)(4,1)}), s8[4194304]{0:T(1024)(128)(4,1)S(1)}, s32[]{:S(2)}) async-start(s8[8388608]{0:T(1024)(128)(4,1)} %bitcast.87), calls=%async_computation | async-start | bytes 8388608
  71.0 39.0 %slice-start.1 = ((s8[8388608]{0:T(1024)(128)(4,1)}), s8[4194304]{0:T(1024)(128)(4,1)S(1)}, s32[]{:S(2)}) async-start(s8[8388608]{0:T(1024)(128)(4,1)} %bitcast.87), calls=%async_computation.1 | async-start | bytes 8388608
  76.3 6.7 %collective-permute-start.11 = (bf16[256,256]{1,0:T(8,128)(2,1)S(1)}, bf16[256,256]{1,0:T(8,128)(2,1)S(1)}, u32[]{:S(2)}, u32[]{:S(2)}) collective-permute-start(bf16[256,256]{1,0:T(8,128)(2,1)S(1)} %get-tuple-element.52), channel_id=1, source_target_pairs={{0,1},{1,2},{2,3},{3,0},{4,5},{5,6},{6,7},{7,4},{8,9},{9,10},{10,1... | collective-permute-start | bytes 393224 | tf_op jit(solution)/shard_map/ppermute | solution.py:151
  77.6 12.2 %collective-permute-start.12 = (bf16[256,256]{1,0:T(8,128)(2,1)S(1)}, bf16[256,256]{1,0:T(8,128)(2,1)S(1)}, u32[]{:S(2)}, u32[]{:S(2)}) collective-permute-start(bf16[256,256]{1,0:T(8,128)(2,1)S(1)} %get-tuple-element.53), channel_id=1, source_target_pairs={{0,2},{1,3},{2,0},{3,1},{4,6},{5,7},{6,4},{7,5},{8,10},{9,11},{10,... | collective-permute-start | bytes 393224 | tf_op jit(solution)/shard_map/ppermute | solution.py:151
  81.6 10.8 %collective-permute-start.13 = (bf16[256,256]{1,0:T(8,128)(2,1)S(1)}, bf16[256,256]{1,0:T(8,128)(2,1)S(1)}, u32[]{:S(2)}, u32[]{:S(2)}) collective-permute-start(bf16[256,256]{1,0:T(8,128)(2,1)S(1)} %get-tuple-element.54), channel_id=1, source_target_pairs={{0,3},{1,0},{2,1},{3,2},{4,7},{5,4},{6,5},{7,6},{8,11},{9,8},{10,9... | collective-permute-start | bytes 393224 | tf_op jit(solution)/shard_map/ppermute | solution.py:151
  92.4 18.4 %collective-permute-start.14 = (bf16[256,1024]{1,0:T(8,128)(2,1)S(1)}, bf16[256,1024]{1,0:T(8,128)(2,1)S(1)}, u32[]{:S(2)}, u32[]{:S(2)}) collective-permute-start(bf16[256,1024]{1,0:T(8,128)(2,1)S(1)} %fusion.51), channel_id=1, source_target_pairs={{0,4},{4,0},{8,12},{12,8},{1,5},{5,1},{9,13},{13,9},{2,6},{6,2},{1... | collective-permute-start | bytes 1572872 | tf_op jit(solution)/shard_map/ppermute | solution.py:155
  93.8 15.9 %collective-permute-start.15 = (bf16[256,1024]{1,0:T(8,128)(2,1)S(1)}, bf16[256,1024]{1,0:T(8,128)(2,1)S(1)}, u32[]{:S(2)}, u32[]{:S(2)}) collective-permute-start(bf16[256,1024]{1,0:T(8,128)(2,1)S(1)} %fusion.51), channel_id=1, source_target_pairs={{0,8},{4,12},{8,0},{12,4},{1,9},{5,13},{9,1},{13,5},{2,10},{6,14},... | collective-permute-start | bytes 1572872 | tf_op jit(solution)/shard_map/ppermute | solution.py:155
  95.0 4.7 %collective-permute-start.17 = (bf16[256,256]{1,0:T(8,128)(2,1)S(1)}, bf16[256,256]{1,0:T(8,128)(2,1)S(1)}, u32[]{:S(2)}, u32[]{:S(2)}) collective-permute-start(bf16[256,256]{1,0:T(8,128)(2,1)S(1)} %get-tuple-element.60), channel_id=1, source_target_pairs={{0,1},{1,2},{2,3},{3,0},{4,5},{5,6},{6,7},{7,4},{8,9},{9,10},{10,1... | collective-permute-start | bytes 393224 | tf_op jit(solution)/shard_map/ppermute | solution.py:151
  95.1 11.3 %collective-permute-start.18 = (bf16[256,256]{1,0:T(8,128)(2,1)S(1)}, bf16[256,256]{1,0:T(8,128)(2,1)S(1)}, u32[]{:S(2)}, u32[]{:S(2)}) collective-permute-start(bf16[256,256]{1,0:T(8,128)(2,1)S(1)} %get-tuple-element.61), channel_id=1, source_target_pairs={{0,2},{1,3},{2,0},{3,1},{4,6},{5,7},{6,4},{7,5},{8,10},{9,11},{10,... | collective-permute-start | bytes 393224 | tf_op jit(solution)/shard_map/ppermute | solution.py:151
  96.5 12.4 %collective-permute-start.19 = (bf16[256,256]{1,0:T(8,128)(2,1)S(1)}, bf16[256,256]{1,0:T(8,128)(2,1)S(1)}, u32[]{:S(2)}, u32[]{:S(2)}) collective-permute-start(bf16[256,256]{1,0:T(8,128)(2,1)S(1)} %get-tuple-element.62), channel_id=1, source_target_pairs={{0,3},{1,0},{2,1},{3,2},{4,7},{5,4},{6,5},{7,6},{8,11},{9,8},{10,9... | collective-permute-start | bytes 393224 | tf_op jit(solution)/shard_map/ppermute | solution.py:151
  108.9 15.7 %collective-permute-start.20 = (bf16[256,1024]{1,0:T(8,128)(2,1)S(1)}, bf16[256,1024]{1,0:T(8,128)(2,1)S(1)}, u32[]{:S(2)}, u32[]{:S(2)}) collective-permute-start(bf16[256,1024]{1,0:T(8,128)(2,1)S(1)} %fusion.55), channel_id=1, source_target_pairs={{0,4},{4,0},{8,12},{12,8},{1,5},{5,1},{9,13},{13,9},{2,6},{6,2},{1... | collective-permute-start | bytes 1572872 | tf_op jit(solution)/shard_map/ppermute | solution.py:155
  109.4 13.5 %collective-permute-start.21 = (bf16[256,1024]{1,0:T(8,128)(2,1)S(1)}, bf16[256,1024]{1,0:T(8,128)(2,1)S(1)}, u32[]{:S(2)}, u32[]{:S(2)}) collective-permute-start(bf16[256,1024]{1,0:T(8,128)(2,1)S(1)} %fusion.55), channel_id=1, source_target_pairs={{0,8},{4,12},{8,0},{12,4},{1,9},{5,13},{9,1},{13,5},{2,10},{6,14},... | collective-permute-start | bytes 1572872 | tf_op jit(solution)/shard_map/ppermute | solution.py:155
  109.7 16.4 %collective-permute-start.16 = (bf16[256,1024]{1,0:T(8,128)(2,1)S(1)}, bf16[256,1024]{1,0:T(8,128)(2,1)S(1)}, u32[]{:S(2)}, u32[]{:S(2)}) collective-permute-start(bf16[256,1024]{1,0:T(8,128)(2,1)S(1)} %collective-permute-done.15), channel_id=1, source_target_pairs={{0,4},{4,0},{8,12},{12,8},{1,5},{5,1},{9,13},{13,9},{2,6},{6,2},{1... | collective-permute-start | bytes 1572872 | tf_op jit(solution)/shard_map/ppermute | solution.py:155
  122.9 3.9 %collective-permute-start.22 = (bf16[256,1024]{1,0:T(8,128)(2,1)S(1)}, bf16[256,1024]{1,0:T(8,128)(2,1)S(1)}, u32[]{:S(2)}, u32[]{:S(2)}) collective-permute-start(bf16[256,1024]{1,0:T(8,128)(2,1)S(1)} %collective-permute-done.21), channel_id=1, source_target_pairs={{0,4},{4,0},{8,12},{12,8},{1,5},{5,1},{9,13},{13,9},{2,6},{6,2},{1... | collective-permute-start | bytes 1572872 | tf_op jit(solution)/shard_map/ppermute | solution.py:155

commit v4 on v3

--- a/solution.py
+++ b/solution.py
@@ -72,58 +72,68 @@
             out_refs[s * per + t][...] = (conv + skip_ref[...] * held).astype(jnp.bfloat16)
 
 
-def project_kernel(mats, ops, mode, *refs):
-    refs = refs[1:]
+def project_kernel(n, mats, ops, mode, where, *refs):
     pieces, weights = refs[:ops], refs[ops : ops + ops * mats]
-    outs = refs[ops + ops * mats :]
-    sums = []
+    refs = refs[ops + ops * mats :]
+    near, outs = (refs[:0], refs) if mode == "near" else (refs[:mats], refs[mats:])
+    sums = outs[:mats] if mode == "near" else outs[1:]
+    step = pl.program_id(0)
+
+    @pl.when(step == 0)
+    def _():
+        for m in range(mats):
+            sums[m][...] = jnp.zeros_like(sums[m]) if mode == "near" else near[m][...]
+
     for m in range(mats):
-        total = outs[m][0] if mode != "near" else None
+        total = sums[m][...]
         for p in range(ops):
-            term = jnp.dot(pieces[p][...], weights[m * ops + p][0], preferred_element_type=jnp.float32)
-            total = term if total is None else total + term
-        sums.append(total)
+            total = total + jnp.dot(
+                pieces[p][...], weights[m * ops + p][0], preferred_element_type=jnp.float32
+            )
+        sums[m][...] = total
+
     if mode == "near":
-        for m in range(mats):
-            outs[m][0] = sums[m]
-
-        @pl.when(pl.program_id(0) == 0)
+        outs[mats][...] = pieces[0][BLOCK:]
+    else:
+
+        @pl.when(step == pl.num_programs(0) - 1)
         def _():
-            outs[mats][...] = pieces[0][BLOCK:]
-    elif mode == "mix":
-        outs[mats][0] = (sums[0] * sums[1]).astype(jnp.bfloat16)
-    else:
-        outs[mats][0] = sums[0].astype(jnp.bfloat16)
+            cc = outs[0].shape[2]
+            for j in range(n):
+                ls = slice(j * cc, (j + 1) * cc)
+                value = sums[0][:, ls] * sums[1][:, ls] if mode == "mix" else sums[0][:, ls]
+                outs[0][lax.rem(j - where[0] + n, n)] = value.astype(jnp.bfloat16)
 
 
 def project(mode, where, pieces, distances, weight, mats, near, t, n):
     rows, width = pieces[0].shape
     channels = weight.shape[2]
-    cc = channels // n
+    depth = min(width, 256)
+    steps = width // depth
 
     def weight_spec(mat, far):
-        return pl.BlockSpec((1, width, cc), lambda s, at: (mat, at[1] ^ far, lax.rem(at[0] + s, n)))
-
-    specs = [pl.BlockSpec((rows, width), lambda s, at: (0, 0))] * len(pieces)
+        return pl.BlockSpec((1, depth, channels), lambda k, at: (mat, (at[1] ^ far) * steps + k, 0))
+
+    specs = [pl.BlockSpec((rows, depth), lambda k, at: (0, k))] * len(pieces)
     specs += [weight_spec(mat, far) for mat in mats for far in distances]
-    specs += [pl.BlockSpec((1, rows, cc), lambda s, at: (s, t, 0))] * len(near)
-    out_spec = pl.BlockSpec((1, rows, cc), lambda s, at: (s, 0, 0))
+    specs += [pl.BlockSpec((rows, channels), lambda k, at: (t, 0))] * len(near)
+    total = (rows, channels)
     if mode == "near":
-        shapes = [jax.ShapeDtypeStruct((n, rows, cc), jnp.float32)] * len(mats)
-        later = jax.ShapeDtypeStruct((rows - BLOCK, width), jnp.bfloat16)
+        shapes = [jax.ShapeDtypeStruct(total, jnp.float32)] * len(mats)
+        shapes.append(jax.ShapeDtypeStruct((rows - BLOCK, width), jnp.bfloat16))
+        out_specs = [pl.BlockSpec(total, lambda k, at: (0, 0))] * len(mats)
+        out_specs.append(pl.BlockSpec((rows - BLOCK, depth), lambda k, at: (0, k)))
+        scratch = []
     else:
-        shapes = [jax.ShapeDtypeStruct((n, rows, cc), jnp.bfloat16)]
-        later = None
-    out_specs = [out_spec] * len(shapes)
-    if later is not None:
-        shapes.append(later)
-        out_specs.append(pl.BlockSpec(later.shape, lambda s, at: (0, 0)))
+        shapes = [jax.ShapeDtypeStruct((n, rows, channels // n), jnp.bfloat16)]
+        out_specs = [pl.BlockSpec(shapes[0].shape, lambda k, at: (0, 0, 0))]
+        scratch = [pltpu.VMEM(total, jnp.float32)] * len(mats)
     flops = 2 * rows * width * channels * len(pieces) * len(mats)
     return pl.pallas_call(
-        functools.partial(project_kernel, len(mats), len(pieces), mode),
+        functools.partial(project_kernel, n, len(mats), len(pieces), mode),
         out_shape=shapes,
         grid_spec=pltpu.PrefetchScalarGridSpec(
-            num_scalar_prefetch=1, grid=(n,), in_specs=specs, out_specs=out_specs
+            num_scalar_prefetch=1, grid=(steps,), in_specs=specs, out_specs=out_specs, scratch_shapes=scratch
         ),
         compiler_params=pltpu.CompilerParams(vmem_limit_bytes=36 * 1024 * 1024),
         cost_estimate=pl.CostEstimate(flops=flops, bytes_accessed=flops // rows, transcendentals=0),

time: 129 us -> 130 us (level)
  transfers between devices with their start and end apart: 23 -> 23, of which waited for: 9 -> 9; matrix products, arithmetic and copies ran while one was open for 8% -> 8% of each run, Pallas kernels for 25% -> 26%
where the time goes in v4:
time: 130 us
  waiting for transfers between devices  45.2 us (35%)
  Pallas kernels  39 us (30%)
  starting transfers between devices  24 us (18%)
  local copies, waits for them, and re-layouts  13.6 us (10%)
  matrix products  6.05 us (5%)
  other arithmetic  1.4 us (1%)
    pallas_call x5, Pallas kernels, project(): pl.pallas_call(functools.partial(project_kernel, n, len(mats), len(pieces...  33.7 us
    ppermute x12, waiting for transfers between devices, shift(): return lax.ppermute(x, axis, [(i, (i + by) % n) for i in range(n)])  23 us
    ppermute x11, waiting for transfers between devices, flip(): return lax.ppermute(x, 'chan', [(i, i ^ bit) for i in range(n)])  22.2 us
    ppermute x12, starting transfers between devices, shift(): return lax.ppermute(x, axis, [(i, (i + by) % n) for i in range(n)])  14.3 us
    ppermute x11, starting transfers between devices, flip(): return lax.ppermute(x, 'chan', [(i, i ^ bit) for i in range(n)])  9.69 us
    unnamed x24, local copies, waits for them, and re-layouts  9.32 us
    dot_general x8, matrix products, shards(): term = jnp.dot(piece, weight, preferred_element_type=f32)  6.05 us
    pallas_call x1, Pallas kernels, convolve(): pl.pallas_call(functools.partial(conv_kernel, n, per), out_shape=[jax.Sha...  5.26 us
  transfers between devices with their start and end apart: 23, of which 9 were waited for; matrix products, arithmetic and copies ran while one was open for 8% of the time, Pallas kernels for 26%

profile of v4, /device:TPU:11, one launch (start us, length us, event | category | flops | bytes accessed | tf_op | source)
XLA Modules:
  0.0 129.6 jit_solution(18032749615114226992)
XLA Ops:
  0.0 0.7 collective-permute-start.2
  0.7 1.1 slice.51
  1.8 1.3 %collective-permute-start = (bf16[256,1024]{1,0:T(8,128)(2,1)S(1)}, bf16[256,1024]{1,0:T(8,128)(2,1)S(1)}, u32[]{:S(2)}, u32[]{:S(2)}) collective-permute-start(bf16[256,1024]{1,0:T(8,128)(2,1)S(1)} %slice.51), channel_id=1, source_target_pairs={{0,8},{4,12},{8,0},{12,4},{1,9},{5,13},{9,1},{13,5},{2,10},{6,14},... | collective-permute-start | bytes 1572872 | tf_op jit(solution)/shard_map/ppermute | solution.py:165
  3.2 1.0 copy-done.5
  4.1 1.2 copy-done.4
  5.4 1.2 copy-done.6
  6.6 11.3 %shard_map.73 = (f32[512,1024]{1,0:T(8,128)S(1)}, f32[512,1024]{1,0:T(8,128)S(1)}, f32[512,1024]{1,0:T(8,128)S(1)}, bf16[256,1024]{1,0:T(8,128)(2,1)}) custom-call(s32[2]{0:T(128)S(1)} %pad_add_fusion.where, bf16[512,1024]{1,0:T(8,128)(2,1)S(1)} %copy-done.4, bf16[512,1024]{1,0:T(8,128)(2,1)S(1)} %copy-done.6, bf16[3,4096,1024]{2,1,0:T(8,128)(2,1)} %bitcast.69, ...), custom_call_target="tpu_custom_call" | custom-call | flops 6442450944 | bytes 12582912 | tf_op jit(solution)/shard_map/pallas_call | solution.py:132
  17.9 1.4 %copy-done = f32[512,1024]{1,0:T(8,128)} copy-done((f32[512,1024]{1,0:T(8,128)}, f32[512,1024]{1,0:T(8,128)S(1)}, u32[]{:S(2)}) %copy-start) | copy-done | bytes 2097176
  19.2 1.3 %copy-done.2 = f32[512,1024]{1,0:T(8,128)} copy-done((f32[512,1024]{1,0:T(8,128)}, f32[512,1024]{1,0:T(8,128)S(1)}, u32[]{:S(2)}) %copy-start.2) | copy-done | bytes 2097176
  20.6 1.2 collective-permute-start.3
  22.5 11.6 %collective-permute-done.3.refs_0_ = bf16[256,1024]{1,0:T(8,128)(2,1)} collective-permute-done((bf16[256,1024]{1,0:T(8,128)(2,1)}, bf16[256,1024]{1,0:T(8,128)(2,1)}, u32[]{:S(2)}, u32[]{:S(2)}) %collective-permute-start.3) | collective-permute-done | bytes 524320 | tf_op jit(solution)/shard_map/ppermute | solution.py:165
  34.0 1.2 collective-permute-start.4
  35.2 2.3 %constant_dynamic-slice_fusion.refs_8_ = bf16[2048,256]{1,0:T(8,128)(2,1)} fusion(bf16[2048,1024]{1,0:T(8,128)(2,1)} %param.8, s32[]{:T(128)S(6)} %select_n.63), kind=kLoop, calls=%fused_computation.73 | loop fusion | bytes 2097156 | tf_op jit(solution)/shard_map/dynamic_slice | solution.py:184
  37.5 0.8 dynamic_slice.23
  38.3 1.6 %copy-done.1 = f32[512,1024]{1,0:T(8,128)S(1)} copy-done((f32[512,1024]{1,0:T(8,128)S(1)}, f32[512,1024]{1,0:T(8,128)}, u32[]{:S(2)}) %copy-start.1) | copy-done | bytes 2097176
  39.9 1.6 %copy-done.3 = f32[512,1024]{1,0:T(8,128)S(1)} copy-done((f32[512,1024]{1,0:T(8,128)S(1)}, f32[512,1024]{1,0:T(8,128)}, u32[]{:S(2)}) %copy-start.3) | copy-done | bytes 2097176
  41.4 6.4 %shard_map.76 = bf16[4,256,256]{2,1,0:T(8,128)(2,1)S(1)} custom-call(s32[2]{0:T(128)S(1)} %pad_add_fusion.where, bf16[256,1024]{1,0:T(8,128)(2,1)S(1)} %collective-permute-done.refs_0_, bf16[256,1024]{1,0:T(8,128)(2,1)S(1)} %collective-permute-done.1.refs_1_, bf16[3,4096,1024]{2,1,0:T(8,128)(2,1)} %bitcast.75, bf16[3,4096,1024]{2,1,0:T(8,128)(2,1)} %bitcast.76, ...), custom_call_target="tpu_custom_call" | custom-call | flops 2147483648 | bytes 8388608 | tf_op jit(solution)/shard_map/pallas_call | solution.py:132
  47.9 1.4 %collective-permute-start.5 = (bf16[256,256]{1,0:T(8,128)(2,1)S(1)}, bf16[256,256]{1,0:T(8,128)(2,1)S(1)}, u32[]{:S(2)}, u32[]{:S(2)}) collective-permute-start(bf16[256,256]{1,0:T(8,128)(2,1)S(1)} %get-tuple-element.69), channel_id=1, source_target_pairs={{0,1},{1,2},{2,3},{3,0},{4,5},{5,6},{6,7},{7,4},{8,9},{9,10},{10,1... | collective-permute-start | bytes 393224 | tf_op jit(solution)/shard_map/ppermute | solution.py:161
  49.3 1.1 collective-permute-start.7
  50.4 1.4 %collective-permute-start.9 = (bf16[256,256]{1,0:T(8,128)(2,1)S(1)}, bf16[256,256]{1,0:T(8,128)(2,1)S(1)}, u32[]{:S(2)}, u32[]{:S(2)}) collective-permute-start(bf16[256,256]{1,0:T(8,128)(2,1)S(1)} %get-tuple-element.67), channel_id=1, source_target_pairs={{0,3},{1,0},{2,1},{3,2},{4,7},{5,4},{6,5},{7,6},{8,11},{9,8},{10,9... | collective-permute-start | bytes 393224 | tf_op jit(solution)/shard_map/ppermute | solution.py:161
  51.8 6.5 %shard_map.74 = bf16[4,256,256]{2,1,0:T(8,128)(2,1)S(1)} custom-call(s32[2]{0:T(128)S(1)} %pad_add_fusion.where, bf16[256,1024]{1,0:T(8,128)(2,1)} %collective-permute-done.3.refs_0_, bf16[256,1024]{1,0:T(8,128)(2,1)} %collective-permute-done.4.refs_1_, bf16[3,4096,1024]{2,1,0:T(8,128)(2,1)} %bitcast.79, bf16[3,4096,1024]{2,1,0:T(8,128)(2,1)} %bitcast.80, ...), custom_call_target="tpu_custom_call" | custom-call | flops 2147483648 | bytes 8388608 | tf_op jit(solution)/shard_map/pallas_call | solution.py:132
  58.3 1.1 collective-permute-start.10
  59.8 1.9 %collective-permute-start.8 = (bf16[256,256]{1,0:T(8,128)(2,1)S(1)}, bf16[256,256]{1,0:T(8,128)(2,1)S(1)}, u32[]{:S(2)}, u32[]{:S(2)}) collective-permute-start(bf16[256,256]{1,0:T(8,128)(2,1)S(1)} %get-tuple-element.64), channel_id=1, source_target_pairs={{0,2},{1,3},{2,0},{3,1},{4,6},{5,7},{6,4},{7,5},{8,10},{9,11},{10,... | collective-permute-start | bytes 393224 | tf_op jit(solution)/shard_map/ppermute | solution.py:161
  61.7 4.8 %shard_map.77 = bf16[4,256,256]{2,1,0:T(8,128)(2,1)S(1)} custom-call(s32[2]{0:T(128)S(1)} %pad_add_fusion.where, bf16[256,1024]{1,0:T(8,128)(2,1)} %collective-permute-done.3.refs_0_, bf16[256,1024]{1,0:T(8,128)(2,1)} %collective-permute-done.4.refs_1_, bf16[3,4096,1024]{2,1,0:T(8,128)(2,1)} %bitcast.83, bf16[3,4096,1024]{2,1,0:T(8,128)(2,1)} %bitcast.84, ...), custom_call_target="tpu_custom_call" | custom-call | flops 1073741824 | bytes 4194304 | tf_op jit(solution)/shard_map/pallas_call | solution.py:132
  66.5 4.7 %shard_map.75 = bf16[4,256,256]{2,1,0:T(8,128)(2,1)S(1)} custom-call(s32[2]{0:T(128)S(1)} %pad_add_fusion.where, bf16[256,1024]{1,0:T(8,128)(2,1)S(1)} %collective-permute-done.refs_0_, bf16[256,1024]{1,0:T(8,128)(2,1)S(1)} %collective-permute-done.1.refs_1_, bf16[3,4096,1024]{2,1,0:T(8,128)(2,1)} %bitcast.85, bf16[3,4096,1024]{2,1,0:T(8,128)(2,1)} %bitcast.86, ...), custom_call_target="tpu_custom_call" | custom-call | flops 1073741824 | bytes 4194304 | tf_op jit(solution)/shard_map/pallas_call | solution.py:132
  71.9 5.3 %shard_map.78 = (bf16[256,256]{1,0:T(8,128)(2,1)S(1)}, bf16[256,256]{1,0:T(8,128)(2,1)S(1)}, bf16[256,256]{1,0:T(8,128)(2,1)S(1)}, bf16[256,256]{1,0:T(8,128)(2,...) custom-call(bf16[256,256]{1,0:T(8,128)(2,1)S(1)} %get-tuple-element., ...), custom_call_target="tpu_custom_call" | custom-call | flops 6000000000 | bytes 4000000 | tf_op jit(solution)/shard_map/pallas_call | solution.py:149
  77.2 1.3 %collective-permute-start.11 = (bf16[256,256]{1,0:T(8,128)(2,1)S(1)}, bf16[256,256]{1,0:T(8,128)(2,1)S(1)}, u32[]{:S(2)}, u32[]{:S(2)}) collective-permute-start(bf16[256,256]{1,0:T(8,128)(2,1)S(1)} %get-tuple-element.52), channel_id=1, source_target_pairs={{0,1},{1,2},{2,3},{3,0},{4,5},{5,6},{6,7},{7,4},{8,9},{9,10},{10,1... | collective-permute-start | bytes 393224 | tf_op jit(solution)/shard_map/ppermute | solution.py:161
  78.5 4.0 %collective-permute-start.12 = (bf16[256,256]{1,0:T(8,128)(2,1)S(1)}, bf16[256,256]{1,0:T(8,128)(2,1)S(1)}, u32[]{:S(2)}, u32[]{:S(2)}) collective-permute-start(bf16[256,256]{1,0:T(8,128)(2,1)S(1)} %get-tuple-element.53), channel_id=1, source_target_pairs={{0,2},{1,3},{2,0},{3,1},{4,6},{5,7},{6,4},{7,5},{8,10},{9,11},{10,... | collective-permute-start | bytes 393224 | tf_op jit(solution)/shard_map/ppermute | solution.py:161
  82.6 1.3 collective-permute-done.11
  83.9 6.8 %collective-permute-done.12 = bf16[256,256]{1,0:T(8,128)(2,1)S(1)} collective-permute-done((bf16[256,256]{1,0:T(8,128)(2,1)S(1)}, bf16[256,256]{1,0:T(8,128)(2,1)S(1)}, u32[]{:S(2)}, u32[]{:S(2)}) %collective-permute-start.12) | collective-permute-done | bytes 131104 | tf_op jit(solution)/shard_map/ppermute | solution.py:161
  90.8 2.5 %collective-permute-done.13 = bf16[256,256]{1,0:T(8,128)(2,1)S(1)} collective-permute-done((bf16[256,256]{1,0:T(8,128)(2,1)S(1)}, bf16[256,256]{1,0:T(8,128)(2,1)S(1)}, u32[]{:S(2)}, u32[]{:S(2)}) %collective-permute-start.13) | collective-permute-done | bytes 131104 | tf_op jit(solution)/shard_map/ppermute | solution.py:161
  93.4 1.4 %collective-permute-start.14 = (bf16[256,1024]{1,0:T(8,128)(2,1)S(1)}, bf16[256,1024]{1,0:T(8,128)(2,1)S(1)}, u32[]{:S(2)}, u32[]{:S(2)}) collective-permute-start(bf16[256,1024]{1,0:T(8,128)(2,1)S(1)} %fusion.51), channel_id=1, source_target_pairs={{0,4},{4,0},{8,12},{12,8},{1,5},{5,1},{9,13},{13,9},{2,6},{6,2},{1... | collective-permute-start | bytes 1572872 | tf_op jit(solution)/shard_map/ppermute | solution.py:165
  94.7 1.3 collective-permute-start.15
  96.0 1.4 %collective-permute-start.18 = (bf16[256,256]{1,0:T(8,128)(2,1)S(1)}, bf16[256,256]{1,0:T(8,128)(2,1)S(1)}, u32[]{:S(2)}, u32[]{:S(2)}) collective-permute-start(bf16[256,256]{1,0:T(8,128)(2,1)S(1)} %get-tuple-element.61), channel_id=1, source_target_pairs={{0,2},{1,3},{2,0},{3,1},{4,6},{5,7},{6,4},{7,5},{8,10},{9,11},{10,... | collective-permute-start | bytes 393224 | tf_op jit(solution)/shard_map/ppermute | solution.py:161
  97.9 2.8 %collective-permute-done.17 = bf16[256,256]{1,0:T(8,128)(2,1)S(1)} collective-permute-done((bf16[256,256]{1,0:T(8,128)(2,1)S(1)}, bf16[256,256]{1,0:T(8,128)(2,1)S(1)}, u32[]{:S(2)}, u32[]{:S(2)}) %collective-permute-start.17) | collective-permute-done | bytes 131104 | tf_op jit(solution)/shard_map/ppermute | solution.py:161
  100.7 6.5 %collective-permute-done.18 = bf16[256,256]{1,0:T(8,128)(2,1)S(1)} collective-permute-done((bf16[256,256]{1,0:T(8,128)(2,1)S(1)}, bf16[256,256]{1,0:T(8,128)(2,1)S(1)}, u32[]{:S(2)}, u32[]{:S(2)}) %collective-permute-start.18) | collective-permute-done | bytes 131104 | tf_op jit(solution)/shard_map/ppermute | solution.py:161
  107.3 2.5 %collective-permute-done.19 = bf16[256,256]{1,0:T(8,128)(2,1)S(1)} collective-permute-done((bf16[256,256]{1,0:T(8,128)(2,1)S(1)}, bf16[256,256]{1,0:T(8,128)(2,1)S(1)}, u32[]{:S(2)}, u32[]{:S(2)}) %collective-permute-start.19) | collective-permute-done | bytes 131104 | tf_op jit(solution)/shard_map/ppermute | solution.py:161
  111.0 0.7 fusion.6
  111.7 0.7 fusion.10
  112.5 0.8 fusion.19
  113.3 10.6 %collective-permute-done.21 = bf16[256,1024]{1,0:T(8,128)(2,1)S(1)} collective-permute-done((bf16[256,1024]{1,0:T(8,128)(2,1)S(1)}, bf16[256,1024]{1,0:T(8,128)(2,1)S(1)}, u32[]{:S(2)}, u32[]{:S(2)}) %collective-permute-start.21) | collective-permute-done | bytes 524320 | tf_op jit(solution)/shard_map/ppermute | solution.py:165
  123.9 0.8 collective-permute-start.22
  124.7 0.7 fusion.4
  125.5 0.7 fusion.8
  126.2 0.8 fusion.25
  127.0 0.8 fusion.37
  127.8 0.8 fusion.34
  128.6 1.0 pad_maximum_fusion
  (54 shorter events, 3.8 us)
Async XLA Ops:
  0.0 3.2 %collective-permute-start.2 = (bf16[512,1024]{1,0:T(8,128)(2,1)}, bf16[512,1024]{1,0:T(8,128)(2,1)S(1)}, u32[]{:S(2)}, u32[]{:S(2)}) collective-permute-start(bf16[512,1024]{1,0:T(8,128)(2,1)} %refs_0_.1), channel_id=1, source_target_pairs={{0,4},{4,0},{8,12},{12,8},{1,5},{5,1},{9,13},{13,9},{2,6},{6,2},{1... | collective-permute-start | bytes 3145736 | tf_op jit(solution)/shard_map/ppermute | solution.py:165
  1.8 18.8 %collective-permute-start = (bf16[256,1024]{1,0:T(8,128)(2,1)S(1)}, bf16[256,1024]{1,0:T(8,128)(2,1)S(1)}, u32[]{:S(2)}, u32[]{:S(2)}) collective-permute-start(bf16[256,1024]{1,0:T(8,128)(2,1)S(1)} %slice.51), channel_id=1, source_target_pairs={{0,8},{4,12},{8,0},{12,4},{1,9},{5,13},{9,1},{13,5},{2,10},{6,14},... | collective-permute-start | bytes 1572872 | tf_op jit(solution)/shard_map/ppermute | solution.py:165
  3.2 1.0 copy-start.5
  4.1 1.2 copy-start.4
  5.4 1.2 copy-start.6
  17.9 1.4 %copy-start = (f32[512,1024]{1,0:T(8,128)}, f32[512,1024]{1,0:T(8,128)S(1)}, u32[]{:S(2)}) copy-start(f32[512,1024]{1,0:T(8,128)S(1)} %get-tuple-element.36.refs_6_) | copy-start | bytes 6291460
  19.2 1.3 %copy-start.2 = (f32[512,1024]{1,0:T(8,128)}, f32[512,1024]{1,0:T(8,128)S(1)}, u32[]{:S(2)}) copy-start(f32[512,1024]{1,0:T(8,128)S(1)} %get-tuple-element.37.refs_7_) | copy-start | bytes 6291460
  20.6 13.5 %collective-permute-start.3 = (bf16[256,1024]{1,0:T(8,128)(2,1)}, bf16[256,1024]{1,0:T(8,128)(2,1)}, u32[]{:S(2)}, u32[]{:S(2)}) collective-permute-start(bf16[256,1024]{1,0:T(8,128)(2,1)} %get-tuple-element.35), channel_id=1, source_target_pairs={{0,8},{4,12},{8,0},{12,4},{1,9},{5,13},{9,1},{13,5},{2,10},{6,14},... | collective-permute-start | bytes 1572872 | tf_op jit(solution)/shard_map/ppermute | solution.py:165
  21.8 16.4 %collective-permute-start.1 = (bf16[256,1024]{1,0:T(8,128)(2,1)S(1)}, bf16[256,1024]{1,0:T(8,128)(2,1)S(1)}, u32[]{:S(2)}, u32[]{:S(2)}) collective-permute-start(bf16[256,1024]{1,0:T(8,128)(2,1)S(1)} %collective-permute-done.refs_0_), channel_id=1, source_target_pairs={{0,4},{4,0},{8,12},{12,8},{1,5},{5,1},{9,13},{13,9},{2,6},{6,2},{1... | collective-permute-start | bytes 1572872 | tf_op jit(solution)/shard_map/ppermute | solution.py:165
  34.0 17.7 %collective-permute-start.4 = (bf16[256,1024]{1,0:T(8,128)(2,1)}, bf16[256,1024]{1,0:T(8,128)(2,1)}, u32[]{:S(2)}, u32[]{:S(2)}) collective-permute-start(bf16[256,1024]{1,0:T(8,128)(2,1)} %collective-permute-done.3.refs_0_), channel_id=1, source_target_pairs={{0,4},{4,0},{8,12},{12,8},{1,5},{5,1},{9,13},{13,9},{2,6},{6,2},{1... | collective-permute-start | bytes 1572872 | tf_op jit(solution)/shard_map/ppermute | solution.py:165
  38.3 1.6 %copy-start.1 = (f32[512,1024]{1,0:T(8,128)S(1)}, f32[512,1024]{1,0:T(8,128)}, u32[]{:S(2)}) copy-start(f32[512,1024]{1,0:T(8,128)} %copy-done) | copy-start | bytes 6291460
  39.8 1.6 %copy-start.3 = (f32[512,1024]{1,0:T(8,128)S(1)}, f32[512,1024]{1,0:T(8,128)}, u32[]{:S(2)}) copy-start(f32[512,1024]{1,0:T(8,128)} %copy-done.2) | copy-start | bytes 6291460
  47.9 11.9 %collective-permute-start.5 = (bf16[256,256]{1,0:T(8,128)(2,1)S(1)}, bf16[256,256]{1,0:T(8,128)(2,1)S(1)}, u32[]{:S(2)}, u32[]{:S(2)}) collective-permute-start(bf16[256,256]{1,0:T(8,128)(2,1)S(1)} %get-tuple-element.69), channel_id=1, source_target_pairs={{0,1},{1,2},{2,3},{3,0},{4,5},{5,6},{6,7},{7,4},{8,9},{9,10},{10,1... | collective-permute-start | bytes 393224 | tf_op jit(solution)/shard_map/ppermute | solution.py:161
  49.3 22.0 %collective-permute-start.7 = (bf16[256,256]{1,0:T(8,128)(2,1)S(1)}, bf16[256,256]{1,0:T(8,128)(2,1)S(1)}, u32[]{:S(2)}, u32[]{:S(2)}) collective-permute-start(bf16[256,256]{1,0:T(8,128)(2,1)S(1)} %get-tuple-element.68), channel_id=1, source_target_pairs={{0,2},{1,3},{2,0},{3,1},{4,6},{5,7},{6,4},{7,5},{8,10},{9,11},{10,... | collective-permute-start | bytes 393224 | tf_op jit(solution)/shard_map/ppermute | solution.py:161
  50.4 20.9 %collective-permute-start.9 = (bf16[256,256]{1,0:T(8,128)(2,1)S(1)}, bf16[256,256]{1,0:T(8,128)(2,1)S(1)}, u32[]{:S(2)}, u32[]{:S(2)}) collective-permute-start(bf16[256,256]{1,0:T(8,128)(2,1)S(1)} %get-tuple-element.67), channel_id=1, source_target_pairs={{0,3},{1,0},{2,1},{3,2},{4,7},{5,4},{6,5},{7,6},{8,11},{9,8},{10,9... | collective-permute-start | bytes 393224 | tf_op jit(solution)/shard_map/ppermute | solution.py:161
  58.3 13.0 %collective-permute-start.10 = (bf16[256,256]{1,0:T(8,128)(2,1)S(1)}, bf16[256,256]{1,0:T(8,128)(2,1)S(1)}, u32[]{:S(2)}, u32[]{:S(2)}) collective-permute-start(bf16[256,256]{1,0:T(8,128)(2,1)S(1)} %get-tuple-element.63), channel_id=1, source_target_pairs={{0,3},{1,0},{2,1},{3,2},{4,7},{5,4},{6,5},{7,6},{8,11},{9,8},{10,9... | collective-permute-start | bytes 393224 | tf_op jit(solution)/shard_map/ppermute | solution.py:161
  59.4 11.9 %collective-permute-start.6 = (bf16[256,256]{1,0:T(8,128)(2,1)S(1)}, bf16[256,256]{1,0:T(8,128)(2,1)S(1)}, u32[]{:S(2)}, u32[]{:S(2)}) collective-permute-start(bf16[256,256]{1,0:T(8,128)(2,1)S(1)} %get-tuple-element.65), channel_id=1, source_target_pairs={{0,1},{1,2},{2,3},{3,0},{4,5},{5,6},{6,7},{7,4},{8,9},{9,10},{10,1... | collective-permute-start | bytes 393224 | tf_op jit(solution)/shard_map/ppermute | solution.py:161
  59.8 12.1 %collective-permute-start.8 = (bf16[256,256]{1,0:T(8,128)(2,1)S(1)}, bf16[256,256]{1,0:T(8,128)(2,1)S(1)}, u32[]{:S(2)}, u32[]{:S(2)}) collective-permute-start(bf16[256,256]{1,0:T(8,128)(2,1)S(1)} %get-tuple-element.64), channel_id=1, source_target_pairs={{0,2},{1,3},{2,0},{3,1},{4,6},{5,7},{6,4},{7,5},{8,10},{9,11},{10,... | collective-permute-start | bytes 393224 | tf_op jit(solution)/shard_map/ppermute | solution.py:161
  66.5 5.4 %copy-start.7 = (bf16[2048,256]{1,0:T(8,128)(2,1)S(1)}, bf16[2048,256]{1,0:T(8,128)(2,1)}, u32[]{:S(2)}) copy-start(bf16[2048,256]{1,0:T(8,128)(2,1)} %constant_dynamic-slice_fusion.refs_8_) | copy-start | bytes 3145732
  66.5 5.4 %copy-start.8 = (bf16[512,512]{1,0:T(8,128)(2,1)S(1)}, bf16[512,512]{1,0:T(8,128)(2,1)}, u32[]{:S(2)}) copy-start(bf16[512,512]{1,0:T(8,128)(2,1)} %constant.64.clone.refs_10_) | copy-start | bytes 1572868
  66.5 5.4 %copy-start.9 = (bf16[256,512]{1,0:T(8,128)(2,1)S(1)}, bf16[256,512]{1,0:T(8,128)(2,1)}, u32[]{:S(2)}) copy-start(bf16[256,512]{1,0:T(8,128)(2,1)} %constant.65.clone.refs_11_) | copy-start | bytes 786436
  71.9 39.1 %slice-start = ((s8[8388608]{0:T(1024)(128)(4,1)}), s8[4194304]{0:T(1024)(128)(4,1)S(1)}, s32[]{:S(2)}) async-start(s8[8388608]{0:T(1024)(128)(4,1)} %bitcast.87), calls=%async_computation | async-start | bytes 8388608
  71.9 39.0 %slice-start.1 = ((s8[8388608]{0:T(1024)(128)(4,1)}), s8[4194304]{0:T(1024)(128)(4,1)S(1)}, s32[]{:S(2)}) async-start(s8[8388608]{0:T(1024)(128)(4,1)} %bitcast.87), calls=%async_computation.1 | async-start | bytes 8388608
  77.2 6.7 %collective-permute-start.11 = (bf16[256,256]{1,0:T(8,128)(2,1)S(1)}, bf16[256,256]{1,0:T(8,128)(2,1)S(1)}, u32[]{:S(2)}, u32[]{:S(2)}) collective-permute-start(bf16[256,256]{1,0:T(8,128)(2,1)S(1)} %get-tuple-element.52), channel_id=1, source_target_pairs={{0,1},{1,2},{2,3},{3,0},{4,5},{5,6},{6,7},{7,4},{8,9},{9,10},{10,1... | collective-permute-start | bytes 393224 | tf_op jit(solution)/shard_map/ppermute | solution.py:161
  78.5 12.2 %collective-permute-start.12 = (bf16[256,256]{1,0:T(8,128)(2,1)S(1)}, bf16[256,256]{1,0:T(8,128)(2,1)S(1)}, u32[]{:S(2)}, u32[]{:S(2)}) collective-permute-start(bf16[256,256]{1,0:T(8,128)(2,1)S(1)} %get-tuple-element.53), channel_id=1, source_target_pairs={{0,2},{1,3},{2,0},{3,1},{4,6},{5,7},{6,4},{7,5},{8,10},{9,11},{10,... | collective-permute-start | bytes 393224 | tf_op jit(solution)/shard_map/ppermute | solution.py:161
  82.5 10.8 %collective-permute-start.13 = (bf16[256,256]{1,0:T(8,128)(2,1)S(1)}, bf16[256,256]{1,0:T(8,128)(2,1)S(1)}, u32[]{:S(2)}, u32[]{:S(2)}) collective-permute-start(bf16[256,256]{1,0:T(8,128)(2,1)S(1)} %get-tuple-element.54), channel_id=1, source_target_pairs={{0,3},{1,0},{2,1},{3,2},{4,7},{5,4},{6,5},{7,6},{8,11},{9,8},{10,9... | collective-permute-start | bytes 393224 | tf_op jit(solution)/shard_map/ppermute | solution.py:161
  93.4 18.4 %collective-permute-start.14 = (bf16[256,1024]{1,0:T(8,128)(2,1)S(1)}, bf16[256,1024]{1,0:T(8,128)(2,1)S(1)}, u32[]{:S(2)}, u32[]{:S(2)}) collective-permute-start(bf16[256,1024]{1,0:T(8,128)(2,1)S(1)} %fusion.51), channel_id=1, source_target_pairs={{0,4},{4,0},{8,12},{12,8},{1,5},{5,1},{9,13},{13,9},{2,6},{6,2},{1... | collective-permute-start | bytes 1572872 | tf_op jit(solution)/shard_map/ppermute | solution.py:165
  94.7 15.9 %collective-permute-start.15 = (bf16[256,1024]{1,0:T(8,128)(2,1)S(1)}, bf16[256,1024]{1,0:T(8,128)(2,1)S(1)}, u32[]{:S(2)}, u32[]{:S(2)}) collective-permute-start(bf16[256,1024]{1,0:T(8,128)(2,1)S(1)} %fusion.51), channel_id=1, source_target_pairs={{0,8},{4,12},{8,0},{12,4},{1,9},{5,13},{9,1},{13,5},{2,10},{6,14},... | collective-permute-start | bytes 1572872 | tf_op jit(solution)/shard_map/ppermute | solution.py:165
  96.0 4.7 %collective-permute-start.17 = (bf16[256,256]{1,0:T(8,128)(2,1)S(1)}, bf16[256,256]{1,0:T(8,128)(2,1)S(1)}, u32[]{:S(2)}, u32[]{:S(2)}) collective-permute-start(bf16[256,256]{1,0:T(8,128)(2,1)S(1)} %get-tuple-element.60), channel_id=1, source_target_pairs={{0,1},{1,2},{2,3},{3,0},{4,5},{5,6},{6,7},{7,4},{8,9},{9,10},{10,1... | collective-permute-start | bytes 393224 | tf_op jit(solution)/shard_map/ppermute | solution.py:161
  96.0 11.3 %collective-permute-start.18 = (bf16[256,256]{1,0:T(8,128)(2,1)S(1)}, bf16[256,256]{1,0:T(8,128)(2,1)S(1)}, u32[]{:S(2)}, u32[]{:S(2)}) collective-permute-start(bf16[256,256]{1,0:T(8,128)(2,1)S(1)} %get-tuple-element.61), channel_id=1, source_target_pairs={{0,2},{1,3},{2,0},{3,1},{4,6},{5,7},{6,4},{7,5},{8,10},{9,11},{10,... | collective-permute-start | bytes 393224 | tf_op jit(solution)/shard_map/ppermute | solution.py:161
  97.4 12.4 %collective-permute-start.19 = (bf16[256,256]{1,0:T(8,128)(2,1)S(1)}, bf16[256,256]{1,0:T(8,128)(2,1)S(1)}, u32[]{:S(2)}, u32[]{:S(2)}) collective-permute-start(bf16[256,256]{1,0:T(8,128)(2,1)S(1)} %get-tuple-element.62), channel_id=1, source_target_pairs={{0,3},{1,0},{2,1},{3,2},{4,7},{5,4},{6,5},{7,6},{8,11},{9,8},{10,9... | collective-permute-start | bytes 393224 | tf_op jit(solution)/shard_map/ppermute | solution.py:161
  109.8 15.7 %collective-permute-start.20 = (bf16[256,1024]{1,0:T(8,128)(2,1)S(1)}, bf16[256,1024]{1,0:T(8,128)(2,1)S(1)}, u32[]{:S(2)}, u32[]{:S(2)}) collective-permute-start(bf16[256,1024]{1,0:T(8,128)(2,1)S(1)} %fusion.55), channel_id=1, source_target_pairs={{0,4},{4,0},{8,12},{12,8},{1,5},{5,1},{9,13},{13,9},{2,6},{6,2},{1... | collective-permute-start | bytes 1572872 | tf_op jit(solution)/shard_map/ppermute | solution.py:165
  110.4 13.5 %collective-permute-start.21 = (bf16[256,1024]{1,0:T(8,128)(2,1)S(1)}, bf16[256,1024]{1,0:T(8,128)(2,1)S(1)}, u32[]{:S(2)}, u32[]{:S(2)}) collective-permute-start(bf16[256,1024]{1,0:T(8,128)(2,1)S(1)} %fusion.55), channel_id=1, source_target_pairs={{0,8},{4,12},{8,0},{12,4},{1,9},{5,13},{9,1},{13,5},{2,10},{6,14},... | collective-permute-start | bytes 1572872 | tf_op jit(solution)/shard_map/ppermute | solution.py:165
  110.6 16.4 %collective-permute-start.16 = (bf16[256,1024]{1,0:T(8,128)(2,1)S(1)}, bf16[256,1024]{1,0:T(8,128)(2,1)S(1)}, u32[]{:S(2)}, u32[]{:S(2)}) collective-permute-start(bf16[256,1024]{1,0:T(8,128)(2,1)S(1)} %collective-permute-done.15), channel_id=1, source_target_pairs={{0,4},{4,0},{8,12},{12,8},{1,5},{5,1},{9,13},{13,9},{2,6},{6,2},{1... | collective-permute-start | bytes 1572872 | tf_op jit(solution)/shard_map/ppermute | solution.py:165
  123.9 3.9 %collective-permute-start.22 = (bf16[256,1024]{1,0:T(8,128)(2,1)S(1)}, bf16[256,1024]{1,0:T(8,128)(2,1)S(1)}, u32[]{:S(2)}, u32[]{:S(2)}) collective-permute-start(bf16[256,1024]{1,0:T(8,128)(2,1)S(1)} %collective-permute-done.21), channel_id=1, source_target_pairs={{0,4},{4,0},{8,12},{12,8},{1,5},{5,1},{9,13},{13,9},{2,6},{6,2},{1... | collective-permute-start | bytes 1572872 | tf_op jit(solution)/shard_map/ppermute | solution.py:165

commit v5 on v3

--- a/solution.py
+++ b/solution.py
@@ -185,10 +185,11 @@
         first = flip(chunk(features, 0), n_chan, 2)
         beside = flip(features, n_chan, 1)
         *near, later = project("near", where, [features, beside], (0, 1), weight, (1, 2, 0), [], 0, n_ctx)
-        across = [first]
+        across, beyond = [first], [flip(first, n_chan, 1)]
         for t in parts[1:]:
-            across.append(flip(after(chunk(later, t - 1), across[-1]), n_chan, 2))
-        far = [[across[t], flip(across[t], n_chan, 1)] for t in parts]
+            across.append(flip(after(chunk(later, t - 1), beyond[-1]), n_chan, 2))
+            beyond.append(flip(across[-1], n_chan, 1))
+        far = [[across[t], beyond[t]] for t in parts]
         for t in parts:
             mixed = project("mix", where, far[t], (2, 3), weight, (1, 2), near[:2], t, n_ctx)[0]
             got.append(exchange([mixed[s] for s in range(n_ctx)], n_ctx))

time: 129 us -> 142 us (1.10)
  waiting for transfers between devices: 45.4 us -> 58.7 us
    ppermute x11, waiting for transfers between devices: 22.2 us -> 35.5 us  [flip(): return lax.ppermute(x, 'chan', [(i, i ^ bit) for i in range(n)])]
  transfers between devices with their start and end apart: 23 -> 23, of which waited for: 9 -> 10; matrix products, arithmetic and copies ran while one was open for 8% -> 7% of each run, Pallas kernels for 25% -> 23%
where the time goes in v5:
time: 142 us
  waiting for transfers between devices  58.7 us (41%)
  Pallas kernels  37.9 us (27%)
  starting transfers between devices  23.7 us (17%)
  local copies, waits for them, and re-layouts  13.6 us (10%)
  matrix products  6.05 us (4%)
    ppermute x11, waiting for transfers between devices, flip(): return lax.ppermute(x, 'chan', [(i, i ^ bit) for i in range(n)])  35.5 us
    pallas_call x5, Pallas kernels, project(): pl.pallas_call(functools.partial(project_kernel, len(mats), len(pieces),...  32.6 us
    ppermute x12, waiting for transfers between devices, shift(): return lax.ppermute(x, axis, [(i, (i + by) % n) for i in range(n)])  23.2 us
    ppermute x12, starting transfers between devices, shift(): return lax.ppermute(x, axis, [(i, (i + by) % n) for i in range(n)])  14.3 us
    ppermute x11, starting transfers between devices, flip(): return lax.ppermute(x, 'chan', [(i, i ^ bit) for i in range(n)])  9.4 us
    unnamed x24, local copies, waits for them, and re-layouts  9.32 us
    dot_general x8, matrix products, shards(): term = jnp.dot(piece, weight, preferred_element_type=f32)  6.05 us
    pallas_call x1, Pallas kernels, convolve(): pl.pallas_call(functools.partial(conv_kernel, n, per), out_shape=[jax.Sha...  5.26 us
  transfers between devices with their start and end apart: 23, of which 10 were waited for; matrix products, arithmetic and copies ran while one was open for 7% of the time, Pallas kernels for 23%

profile of v5, /device:TPU:11, one launch (start us, length us, event | category | flops | bytes accessed | tf_op | source)
XLA Modules:
  0.0 141.7 jit_solution(17196035867802113698)
XLA Ops:
  0.7 1.1 slice.51
  1.8 1.3 collective-permute-start
  3.1 12.2 %collective-permute-done.refs_1_ = bf16[256,1024]{1,0:T(8,128)(2,1)S(1)} collective-permute-done((bf16[256,1024]{1,0:T(8,128)(2,1)S(1)}, bf16[256,1024]{1,0:T(8,128)(2,1)S(1)}, u32[]{:S(2)}, u32[]{:S(2)}) %collective-permute-start) | collective-permute-done | bytes 524320 | tf_op jit(solution)/shard_map/ppermute | solution.py:155
  15.4 0.8 collective-permute-start.1
  16.2 1.0 copy-done.5
  17.1 1.2 copy-done.4
  18.4 1.2 copy-done.6
  19.6 10.7 %shard_map.73 = (f32[4,512,256]{2,1,0:T(8,128)S(1)}, f32[4,512,256]{2,1,0:T(8,128)S(1)}, f32[4,512,256]{2,1,0:T(8,128)S(1)}, bf16[256,1024]{1,0:T(8,128)(2,1)}) custom-call(s32[2]{0:T(128)S(1)} %pad_add_fusion.refs_0_, bf16[512,1024]{1,0:T(8,128)(2,1)S(1)} %copy-done.4, bf16[512,1024]{1,0:T(8,128)(2,1)S(1)} %copy-done.6, bf16[3,4096,1024]{2,1,0:T(8,128)(2,1)} %bitcast.69, ...), custom_call_target="tpu_custom_call" | custom-call | flops 6442450944 | bytes 12582912 | tf_op jit(solution)/shard_map/pallas_call | solution.py:122
  30.3 1.4 copy-done
  31.7 1.3 copy-done.2
  33.0 1.2 collective-permute-start.3
  34.3 12.6 %collective-permute-done.3.refs_1_ = bf16[256,1024]{1,0:T(8,128)(2,1)} collective-permute-done((bf16[256,1024]{1,0:T(8,128)(2,1)}, bf16[256,1024]{1,0:T(8,128)(2,1)}, u32[]{:S(2)}, u32[]{:S(2)}) %collective-permute-start.3) | collective-permute-done | bytes 524320 | tf_op jit(solution)/shard_map/ppermute | solution.py:155
  46.9 0.8 collective-permute-start.4
  47.7 2.3 %constant_dynamic-slice_fusion.refs_8_ = bf16[2048,256]{1,0:T(8,128)(2,1)} fusion(bf16[2048,1024]{1,0:T(8,128)(2,1)} %param.8, s32[]{:T(128)S(6)} %select_n.63), kind=kLoop, calls=%fused_computation.73 | loop fusion | bytes 2097156 | tf_op jit(solution)/shard_map/dynamic_slice | solution.py:174
  49.9 0.8 dynamic_slice.23
  50.7 1.6 %copy-done.1 = f32[4,512,256]{2,1,0:T(8,128)S(1)} copy-done((f32[4,512,256]{2,1,0:T(8,128)S(1)}, f32[4,512,256]{2,1,0:T(8,128)}, u32[]{:S(2)}) %copy-start.1) | copy-done | bytes 2097176
  52.3 1.6 %copy-done.3 = f32[4,512,256]{2,1,0:T(8,128)S(1)} copy-done((f32[4,512,256]{2,1,0:T(8,128)S(1)}, f32[4,512,256]{2,1,0:T(8,128)}, u32[]{:S(2)}) %copy-start.3) | copy-done | bytes 2097176
  53.9 6.1 %shard_map.76 = bf16[4,256,256]{2,1,0:T(8,128)(2,1)S(1)} custom-call(s32[2]{0:T(128)S(1)} %pad_add_fusion.refs_0_, bf16[256,1024]{1,0:T(8,128)(2,1)S(1)} %collective-permute-done.refs_1_, bf16[256,1024]{1,0:T(8,128)(2,1)S(1)} %collective-permute-done.1.refs_2_, bf16[3,4096,1024]{2,1,0:T(8,128)(2,1)} %bitcast.75, bf16[3,4096,1024]{2,1,0:T(8,128)(2,1)} %bitcast.76, ...), custom_call_target="tpu_custom_call" | custom-call | flops 2147483648 | bytes 8388608 | tf_op jit(solution)/shard_map/pallas_call | solution.py:122
  60.0 1.3 collective-permute-start.5
  61.3 1.1 collective-permute-start.7
  62.4 1.4 collective-permute-start.9
  63.8 6.6 %shard_map.74 = bf16[4,256,256]{2,1,0:T(8,128)(2,1)S(1)} custom-call(s32[2]{0:T(128)S(1)} %pad_add_fusion.refs_0_, bf16[256,1024]{1,0:T(8,128)(2,1)} %collective-permute-done.3.refs_1_, bf16[256,1024]{1,0:T(8,128)(2,1)} %collective-permute-done.4.refs_2_, bf16[3,4096,1024]{2,1,0:T(8,128)(2,1)} %bitcast.79, bf16[3,4096,1024]{2,1,0:T(8,128)(2,1)} %bitcast.80, ...), custom_call_target="tpu_custom_call" | custom-call | flops 2147483648 | bytes 8388608 | tf_op jit(solution)/shard_map/pallas_call | solution.py:122
  70.4 1.1 collective-permute-start.10
  71.9 1.9 %collective-permute-start.8 = (bf16[256,256]{1,0:T(8,128)(2,1)S(1)}, bf16[256,256]{1,0:T(8,128)(2,1)S(1)}, u32[]{:S(2)}, u32[]{:S(2)}) collective-permute-start(bf16[256,256]{1,0:T(8,128)(2,1)S(1)} %get-tuple-element.64), channel_id=1, source_target_pairs={{0,2},{1,3},{2,0},{3,1},{4,6},{5,7},{6,4},{7,5},{8,10},{9,11},{10,... | collective-permute-start | bytes 393224 | tf_op jit(solution)/shard_map/ppermute | solution.py:151
  73.8 4.8 %shard_map.77 = bf16[4,256,256]{2,1,0:T(8,128)(2,1)S(1)} custom-call(s32[2]{0:T(128)S(1)} %pad_add_fusion.refs_0_, bf16[256,1024]{1,0:T(8,128)(2,1)} %collective-permute-done.3.refs_1_, bf16[256,1024]{1,0:T(8,128)(2,1)} %collective-permute-done.4.refs_2_, bf16[3,4096,1024]{2,1,0:T(8,128)(2,1)} %bitcast.83, bf16[3,4096,1024]{2,1,0:T(8,128)(2,1)} %bitcast.84, ...), custom_call_target="tpu_custom_call" | custom-call | flops 1073741824 | bytes 4194304 | tf_op jit(solution)/shard_map/pallas_call | solution.py:122
  78.6 4.5 %shard_map.75 = bf16[4,256,256]{2,1,0:T(8,128)(2,1)S(1)} custom-call(s32[2]{0:T(128)S(1)} %pad_add_fusion.refs_0_, bf16[256,1024]{1,0:T(8,128)(2,1)S(1)} %collective-permute-done.refs_1_, bf16[256,1024]{1,0:T(8,128)(2,1)S(1)} %collective-permute-done.1.refs_2_, bf16[3,4096,1024]{2,1,0:T(8,128)(2,1)} %bitcast.85, bf16[3,4096,1024]{2,1,0:T(8,128)(2,1)} %bitcast.86, ...), custom_call_target="tpu_custom_call" | custom-call | flops 1073741824 | bytes 4194304 | tf_op jit(solution)/shard_map/pallas_call | solution.py:122
  83.2 0.8 collective-permute-done.8.refs_5_
  84.0 5.3 %shard_map.78 = (bf16[256,256]{1,0:T(8,128)(2,1)S(1)}, bf16[256,256]{1,0:T(8,128)(2,1)S(1)}, bf16[256,256]{1,0:T(8,128)(2,1)S(1)}, bf16[256,256]{1,0:T(8,128)(2,...) custom-call(bf16[256,256]{1,0:T(8,128)(2,1)S(1)} %get-tuple-element., ...), custom_call_target="tpu_custom_call" | custom-call | flops 6000000000 | bytes 4000000 | tf_op jit(solution)/shard_map/pallas_call | solution.py:139
  89.3 1.3 collective-permute-start.11
  90.6 4.0 %collective-permute-start.12 = (bf16[256,256]{1,0:T(8,128)(2,1)S(1)}, bf16[256,256]{1,0:T(8,128)(2,1)S(1)}, u32[]{:S(2)}, u32[]{:S(2)}) collective-permute-start(bf16[256,256]{1,0:T(8,128)(2,1)S(1)} %get-tuple-element.53), channel_id=1, source_target_pairs={{0,2},{1,3},{2,0},{3,1},{4,6},{5,7},{6,4},{7,5},{8,10},{9,11},{10,... | collective-permute-start | bytes 393224 | tf_op jit(solution)/shard_map/ppermute | solution.py:151
  94.7 1.3 collective-permute-done.11
  96.0 6.8 %collective-permute-done.12 = bf16[256,256]{1,0:T(8,128)(2,1)S(1)} collective-permute-done((bf16[256,256]{1,0:T(8,128)(2,1)S(1)}, bf16[256,256]{1,0:T(8,128)(2,1)S(1)}, u32[]{:S(2)}, u32[]{:S(2)}) %collective-permute-start.12) | collective-permute-done | bytes 131104 | tf_op jit(solution)/shard_map/ppermute | solution.py:151
  102.8 2.5 %collective-permute-done.13 = bf16[256,256]{1,0:T(8,128)(2,1)S(1)} collective-permute-done((bf16[256,256]{1,0:T(8,128)(2,1)S(1)}, bf16[256,256]{1,0:T(8,128)(2,1)S(1)}, u32[]{:S(2)}, u32[]{:S(2)}) %collective-permute-start.13) | collective-permute-done | bytes 131104 | tf_op jit(solution)/shard_map/ppermute | solution.py:151
  105.4 1.4 collective-permute-start.14
  106.8 1.3 collective-permute-start.15
  108.0 1.4 collective-permute-start.18
  109.9 2.8 %collective-permute-done.17 = bf16[256,256]{1,0:T(8,128)(2,1)S(1)} collective-permute-done((bf16[256,256]{1,0:T(8,128)(2,1)S(1)}, bf16[256,256]{1,0:T(8,128)(2,1)S(1)}, u32[]{:S(2)}, u32[]{:S(2)}) %collective-permute-start.17) | collective-permute-done | bytes 131104 | tf_op jit(solution)/shard_map/ppermute | solution.py:151
  112.8 6.5 %collective-permute-done.18 = bf16[256,256]{1,0:T(8,128)(2,1)S(1)} collective-permute-done((bf16[256,256]{1,0:T(8,128)(2,1)S(1)}, bf16[256,256]{1,0:T(8,128)(2,1)S(1)}, u32[]{:S(2)}, u32[]{:S(2)}) %collective-permute-start.18) | collective-permute-done | bytes 131104 | tf_op jit(solution)/shard_map/ppermute | solution.py:151
  119.4 2.5 %collective-permute-done.19 = bf16[256,256]{1,0:T(8,128)(2,1)S(1)} collective-permute-done((bf16[256,256]{1,0:T(8,128)(2,1)S(1)}, bf16[256,256]{1,0:T(8,128)(2,1)S(1)}, u32[]{:S(2)}, u32[]{:S(2)}) %collective-permute-start.19) | collective-permute-done | bytes 131104 | tf_op jit(solution)/shard_map/ppermute | solution.py:151
  123.8 0.7 fusion.10
  124.5 0.8 fusion.19
  125.3 10.6 %collective-permute-done.21 = bf16[256,1024]{1,0:T(8,128)(2,1)S(1)} collective-permute-done((bf16[256,1024]{1,0:T(8,128)(2,1)S(1)}, bf16[256,1024]{1,0:T(8,128)(2,1)S(1)}, u32[]{:S(2)}, u32[]{:S(2)}) %collective-permute-start.21) | collective-permute-done | bytes 524320 | tf_op jit(solution)/shard_map/ppermute | solution.py:155
  135.9 0.8 collective-permute-start.22
  137.5 0.7 fusion.8
  138.3 0.8 fusion.25
  139.1 0.8 fusion.37
  139.9 0.8 fusion.34
  140.6 1.0 pad_maximum_fusion
  (54 shorter events, 4.7 us)
Async XLA Ops:
  0.0 16.2 %collective-permute-start.2 = (bf16[512,1024]{1,0:T(8,128)(2,1)}, bf16[512,1024]{1,0:T(8,128)(2,1)S(1)}, u32[]{:S(2)}, u32[]{:S(2)}) collective-permute-start(bf16[512,1024]{1,0:T(8,128)(2,1)} %refs_1_.1), channel_id=1, source_target_pairs={{0,4},{4,0},{8,12},{12,8},{1,5},{5,1},{9,13},{13,9},{2,6},{6,2},{1... | collective-permute-start | bytes 3145736 | tf_op jit(solution)/shard_map/ppermute | solution.py:155
  1.8 13.6 %collective-permute-start = (bf16[256,1024]{1,0:T(8,128)(2,1)S(1)}, bf16[256,1024]{1,0:T(8,128)(2,1)S(1)}, u32[]{:S(2)}, u32[]{:S(2)}) collective-permute-start(bf16[256,1024]{1,0:T(8,128)(2,1)S(1)} %slice.51), channel_id=1, source_target_pairs={{0,8},{4,12},{8,0},{12,4},{1,9},{5,13},{9,1},{13,5},{2,10},{6,14},... | collective-permute-start | bytes 1572872 | tf_op jit(solution)/shard_map/ppermute | solution.py:155
  15.4 17.6 %collective-permute-start.1 = (bf16[256,1024]{1,0:T(8,128)(2,1)S(1)}, bf16[256,1024]{1,0:T(8,128)(2,1)S(1)}, u32[]{:S(2)}, u32[]{:S(2)}) collective-permute-start(bf16[256,1024]{1,0:T(8,128)(2,1)S(1)} %collective-permute-done.refs_1_), channel_id=1, source_target_pairs={{0,4},{4,0},{8,12},{12,8},{1,5},{5,1},{9,13},{13,9},{2,6},{6,2},{1... | collective-permute-start | bytes 1572872 | tf_op jit(solution)/shard_map/ppermute | solution.py:155
  16.2 1.0 copy-start.5
  17.1 1.2 copy-start.4
  18.4 1.2 copy-start.6
  30.3 1.4 copy-start
  31.7 1.3 copy-start.2
  33.0 13.9 %collective-permute-start.3 = (bf16[256,1024]{1,0:T(8,128)(2,1)}, bf16[256,1024]{1,0:T(8,128)(2,1)}, u32[]{:S(2)}, u32[]{:S(2)}) collective-permute-start(bf16[256,1024]{1,0:T(8,128)(2,1)} %get-tuple-element.35), channel_id=1, source_target_pairs={{0,8},{4,12},{8,0},{12,4},{1,9},{5,13},{9,1},{13,5},{2,10},{6,14},... | collective-permute-start | bytes 1572872 | tf_op jit(solution)/shard_map/ppermute | solution.py:155
  46.9 16.9 %collective-permute-start.4 = (bf16[256,1024]{1,0:T(8,128)(2,1)}, bf16[256,1024]{1,0:T(8,128)(2,1)}, u32[]{:S(2)}, u32[]{:S(2)}) collective-permute-start(bf16[256,1024]{1,0:T(8,128)(2,1)} %collective-permute-done.3.refs_1_), channel_id=1, source_target_pairs={{0,4},{4,0},{8,12},{12,8},{1,5},{5,1},{9,13},{13,9},{2,6},{6,2},{1... | collective-permute-start | bytes 1572872 | tf_op jit(solution)/shard_map/ppermute | solution.py:155
  50.7 1.6 %copy-start.1 = (f32[4,512,256]{2,1,0:T(8,128)S(1)}, f32[4,512,256]{2,1,0:T(8,128)}, u32[]{:S(2)}) copy-start(f32[4,512,256]{2,1,0:T(8,128)} %copy-done) | copy-start | bytes 6291460
  52.3 1.6 %copy-start.3 = (f32[4,512,256]{2,1,0:T(8,128)S(1)}, f32[4,512,256]{2,1,0:T(8,128)}, u32[]{:S(2)}) copy-start(f32[4,512,256]{2,1,0:T(8,128)} %copy-done.2) | copy-start | bytes 6291460
  60.0 12.0 %collective-permute-start.5 = (bf16[256,256]{1,0:T(8,128)(2,1)S(1)}, bf16[256,256]{1,0:T(8,128)(2,1)S(1)}, u32[]{:S(2)}, u32[]{:S(2)}) collective-permute-start(bf16[256,256]{1,0:T(8,128)(2,1)S(1)} %get-tuple-element.69), channel_id=1, source_target_pairs={{0,1},{1,2},{2,3},{3,0},{4,5},{5,6},{6,7},{7,4},{8,9},{9,10},{10,1... | collective-permute-start | bytes 393224 | tf_op jit(solution)/shard_map/ppermute | solution.py:151
  61.3 21.8 %collective-permute-start.7 = (bf16[256,256]{1,0:T(8,128)(2,1)S(1)}, bf16[256,256]{1,0:T(8,128)(2,1)S(1)}, u32[]{:S(2)}, u32[]{:S(2)}) collective-permute-start(bf16[256,256]{1,0:T(8,128)(2,1)S(1)} %get-tuple-element.68), channel_id=1, source_target_pairs={{0,2},{1,3},{2,0},{3,1},{4,6},{5,7},{6,4},{7,5},{8,10},{9,11},{10,... | collective-permute-start | bytes 393224 | tf_op jit(solution)/shard_map/ppermute | solution.py:151
  62.4 20.7 %collective-permute-start.9 = (bf16[256,256]{1,0:T(8,128)(2,1)S(1)}, bf16[256,256]{1,0:T(8,128)(2,1)S(1)}, u32[]{:S(2)}, u32[]{:S(2)}) collective-permute-start(bf16[256,256]{1,0:T(8,128)(2,1)S(1)} %get-tuple-element.67), channel_id=1, source_target_pairs={{0,3},{1,0},{2,1},{3,2},{4,7},{5,4},{6,5},{7,6},{8,11},{9,8},{10,9... | collective-permute-start | bytes 393224 | tf_op jit(solution)/shard_map/ppermute | solution.py:151
  70.4 12.8 %collective-permute-start.10 = (bf16[256,256]{1,0:T(8,128)(2,1)S(1)}, bf16[256,256]{1,0:T(8,128)(2,1)S(1)}, u32[]{:S(2)}, u32[]{:S(2)}) collective-permute-start(bf16[256,256]{1,0:T(8,128)(2,1)S(1)} %get-tuple-element.63), channel_id=1, source_target_pairs={{0,3},{1,0},{2,1},{3,2},{4,7},{5,4},{6,5},{7,6},{8,11},{9,8},{10,9... | collective-permute-start | bytes 393224 | tf_op jit(solution)/shard_map/ppermute | solution.py:151
  71.5 11.6 %collective-permute-start.6 = (bf16[256,256]{1,0:T(8,128)(2,1)S(1)}, bf16[256,256]{1,0:T(8,128)(2,1)S(1)}, u32[]{:S(2)}, u32[]{:S(2)}) collective-permute-start(bf16[256,256]{1,0:T(8,128)(2,1)S(1)} %get-tuple-element.65), channel_id=1, source_target_pairs={{0,1},{1,2},{2,3},{3,0},{4,5},{5,6},{6,7},{7,4},{8,9},{9,10},{10,1... | collective-permute-start | bytes 393224 | tf_op jit(solution)/shard_map/ppermute | solution.py:151
  71.9 12.0 %collective-permute-start.8 = (bf16[256,256]{1,0:T(8,128)(2,1)S(1)}, bf16[256,256]{1,0:T(8,128)(2,1)S(1)}, u32[]{:S(2)}, u32[]{:S(2)}) collective-permute-start(bf16[256,256]{1,0:T(8,128)(2,1)S(1)} %get-tuple-element.64), channel_id=1, source_target_pairs={{0,2},{1,3},{2,0},{3,1},{4,6},{5,7},{6,4},{7,5},{8,10},{9,11},{10,... | collective-permute-start | bytes 393224 | tf_op jit(solution)/shard_map/ppermute | solution.py:151
  78.6 5.4 %copy-start.7 = (bf16[2048,256]{1,0:T(8,128)(2,1)S(1)}, bf16[2048,256]{1,0:T(8,128)(2,1)}, u32[]{:S(2)}) copy-start(bf16[2048,256]{1,0:T(8,128)(2,1)} %constant_dynamic-slice_fusion.refs_8_) | copy-start | bytes 3145732
  78.6 5.3 %copy-start.8 = (bf16[512,512]{1,0:T(8,128)(2,1)S(1)}, bf16[512,512]{1,0:T(8,128)(2,1)}, u32[]{:S(2)}) copy-start(bf16[512,512]{1,0:T(8,128)(2,1)} %constant.64.clone.refs_10_) | copy-start | bytes 1572868
  78.6 5.3 %copy-start.9 = (bf16[256,512]{1,0:T(8,128)(2,1)S(1)}, bf16[256,512]{1,0:T(8,128)(2,1)}, u32[]{:S(2)}) copy-start(bf16[256,512]{1,0:T(8,128)(2,1)} %constant.65.clone.refs_11_) | copy-start | bytes 786436
  84.0 39.0 %slice-start = ((s8[8388608]{0:T(1024)(128)(4,1)}), s8[4194304]{0:T(1024)(128)(4,1)S(1)}, s32[]{:S(2)}) async-start(s8[8388608]{0:T(1024)(128)(4,1)} %bitcast.87), calls=%async_computation | async-start | bytes 8388608
  84.0 39.0 %slice-start.1 = ((s8[8388608]{0:T(1024)(128)(4,1)}), s8[4194304]{0:T(1024)(128)(4,1)S(1)}, s32[]{:S(2)}) async-start(s8[8388608]{0:T(1024)(128)(4,1)} %bitcast.87), calls=%async_computation.1 | async-start | bytes 8388608
  89.3 6.7 %collective-permute-start.11 = (bf16[256,256]{1,0:T(8,128)(2,1)S(1)}, bf16[256,256]{1,0:T(8,128)(2,1)S(1)}, u32[]{:S(2)}, u32[]{:S(2)}) collective-permute-start(bf16[256,256]{1,0:T(8,128)(2,1)S(1)} %get-tuple-element.52), channel_id=1, source_target_pairs={{0,1},{1,2},{2,3},{3,0},{4,5},{5,6},{6,7},{7,4},{8,9},{9,10},{10,1... | collective-permute-start | bytes 393224 | tf_op jit(solution)/shard_map/ppermute | solution.py:151
  90.6 12.2 %collective-permute-start.12 = (bf16[256,256]{1,0:T(8,128)(2,1)S(1)}, bf16[256,256]{1,0:T(8,128)(2,1)S(1)}, u32[]{:S(2)}, u32[]{:S(2)}) collective-permute-start(bf16[256,256]{1,0:T(8,128)(2,1)S(1)} %get-tuple-element.53), channel_id=1, source_target_pairs={{0,2},{1,3},{2,0},{3,1},{4,6},{5,7},{6,4},{7,5},{8,10},{9,11},{10,... | collective-permute-start | bytes 393224 | tf_op jit(solution)/shard_map/ppermute | solution.py:151
  94.6 10.8 %collective-permute-start.13 = (bf16[256,256]{1,0:T(8,128)(2,1)S(1)}, bf16[256,256]{1,0:T(8,128)(2,1)S(1)}, u32[]{:S(2)}, u32[]{:S(2)}) collective-permute-start(bf16[256,256]{1,0:T(8,128)(2,1)S(1)} %get-tuple-element.54), channel_id=1, source_target_pairs={{0,3},{1,0},{2,1},{3,2},{4,7},{5,4},{6,5},{7,6},{8,11},{9,8},{10,9... | collective-permute-start | bytes 393224 | tf_op jit(solution)/shard_map/ppermute | solution.py:151
  105.4 18.4 %collective-permute-start.14 = (bf16[256,1024]{1,0:T(8,128)(2,1)S(1)}, bf16[256,1024]{1,0:T(8,128)(2,1)S(1)}, u32[]{:S(2)}, u32[]{:S(2)}) collective-permute-start(bf16[256,1024]{1,0:T(8,128)(2,1)S(1)} %fusion.51), channel_id=1, source_target_pairs={{0,4},{4,0},{8,12},{12,8},{1,5},{5,1},{9,13},{13,9},{2,6},{6,2},{1... | collective-permute-start | bytes 1572872 | tf_op jit(solution)/shard_map/ppermute | solution.py:155
  106.8 15.9 %collective-permute-start.15 = (bf16[256,1024]{1,0:T(8,128)(2,1)S(1)}, bf16[256,1024]{1,0:T(8,128)(2,1)S(1)}, u32[]{:S(2)}, u32[]{:S(2)}) collective-permute-start(bf16[256,1024]{1,0:T(8,128)(2,1)S(1)} %fusion.51), channel_id=1, source_target_pairs={{0,8},{4,12},{8,0},{12,4},{1,9},{5,13},{9,1},{13,5},{2,10},{6,14},... | collective-permute-start | bytes 1572872 | tf_op jit(solution)/shard_map/ppermute | solution.py:155
  108.0 4.7 %collective-permute-start.17 = (bf16[256,256]{1,0:T(8,128)(2,1)S(1)}, bf16[256,256]{1,0:T(8,128)(2,1)S(1)}, u32[]{:S(2)}, u32[]{:S(2)}) collective-permute-start(bf16[256,256]{1,0:T(8,128)(2,1)S(1)} %get-tuple-element.60), channel_id=1, source_target_pairs={{0,1},{1,2},{2,3},{3,0},{4,5},{5,6},{6,7},{7,4},{8,9},{9,10},{10,1... | collective-permute-start | bytes 393224 | tf_op jit(solution)/shard_map/ppermute | solution.py:151
  108.0 11.3 %collective-permute-start.18 = (bf16[256,256]{1,0:T(8,128)(2,1)S(1)}, bf16[256,256]{1,0:T(8,128)(2,1)S(1)}, u32[]{:S(2)}, u32[]{:S(2)}) collective-permute-start(bf16[256,256]{1,0:T(8,128)(2,1)S(1)} %get-tuple-element.61), channel_id=1, source_target_pairs={{0,2},{1,3},{2,0},{3,1},{4,6},{5,7},{6,4},{7,5},{8,10},{9,11},{10,... | collective-permute-start | bytes 393224 | tf_op jit(solution)/shard_map/ppermute | solution.py:151
  109.4 12.4 %collective-permute-start.19 = (bf16[256,256]{1,0:T(8,128)(2,1)S(1)}, bf16[256,256]{1,0:T(8,128)(2,1)S(1)}, u32[]{:S(2)}, u32[]{:S(2)}) collective-permute-start(bf16[256,256]{1,0:T(8,128)(2,1)S(1)} %get-tuple-element.62), channel_id=1, source_target_pairs={{0,3},{1,0},{2,1},{3,2},{4,7},{5,4},{6,5},{7,6},{8,11},{9,8},{10,9... | collective-permute-start | bytes 393224 | tf_op jit(solution)/shard_map/ppermute | solution.py:151
  121.9 15.7 %collective-permute-start.20 = (bf16[256,1024]{1,0:T(8,128)(2,1)S(1)}, bf16[256,1024]{1,0:T(8,128)(2,1)S(1)}, u32[]{:S(2)}, u32[]{:S(2)}) collective-permute-start(bf16[256,1024]{1,0:T(8,128)(2,1)S(1)} %fusion.55), channel_id=1, source_target_pairs={{0,4},{4,0},{8,12},{12,8},{1,5},{5,1},{9,13},{13,9},{2,6},{6,2},{1... | collective-permute-start | bytes 1572872 | tf_op jit(solution)/shard_map/ppermute | solution.py:155
  122.4 13.5 %collective-permute-start.21 = (bf16[256,1024]{1,0:T(8,128)(2,1)S(1)}, bf16[256,1024]{1,0:T(8,128)(2,1)S(1)}, u32[]{:S(2)}, u32[]{:S(2)}) collective-permute-start(bf16[256,1024]{1,0:T(8,128)(2,1)S(1)} %fusion.55), channel_id=1, source_target_pairs={{0,8},{4,12},{8,0},{12,4},{1,9},{5,13},{9,1},{13,5},{2,10},{6,14},... | collective-permute-start | bytes 1572872 | tf_op jit(solution)/shard_map/ppermute | solution.py:155
  122.7 16.4 %collective-permute-start.16 = (bf16[256,1024]{1,0:T(8,128)(2,1)S(1)}, bf16[256,1024]{1,0:T(8,128)(2,1)S(1)}, u32[]{:S(2)}, u32[]{:S(2)}) collective-permute-start(bf16[256,1024]{1,0:T(8,128)(2,1)S(1)} %collective-permute-done.15), channel_id=1, source_target_pairs={{0,4},{4,0},{8,12},{12,8},{1,5},{5,1},{9,13},{13,9},{2,6},{6,2},{1... | collective-permute-start | bytes 1572872 | tf_op jit(solution)/shard_map/ppermute | solution.py:155
  135.9 3.9 %collective-permute-start.22 = (bf16[256,1024]{1,0:T(8,128)(2,1)S(1)}, bf16[256,1024]{1,0:T(8,128)(2,1)S(1)}, u32[]{:S(2)}, u32[]{:S(2)}) collective-permute-start(bf16[256,1024]{1,0:T(8,128)(2,1)S(1)} %collective-permute-done.21), channel_id=1, source_target_pairs={{0,4},{4,0},{8,12},{12,8},{1,5},{5,1},{9,13},{13,9},{2,6},{6,2},{1... | collective-permute-start | bytes 1572872 | tf_op jit(solution)/shard_map/ppermute | solution.py:155
